TPU v7x, 32 devices: a whole 2x2x4 slice. The times are simulated.
32 devices in a mesh: mode: 4 (over y, x), dp: 8 (over z, core).
Axes of the slice: x: 2, y: 2, z: 4, core: 2. Of those that a mesh axis runs over, the one named last changes fastest.
Arguments:
- rows: bfloat16 [32, 1024, 768], P(('mode', 'dp')), may hold values from -6 to 6
- memory: bfloat16 [32, 512, 768], P(('mode', 'dp')), may hold values from -6 to 6
- cotangent: bfloat16 [32, 1024, 768], P(('mode', 'dp')), may hold values from -6 to 6
- mode_ids: int32 [32], replicated, may hold values from 0 to 3, as said below
- target_lengths: int32 [32], replicated, may hold values from 128 to 1024
- encoder_lengths: int32 [32], replicated, may hold values from 32 to 512
- self_q: bfloat16 [768, 768], P(('mode', 'dp')), may hold values from -0.21875 to 0.21875
- self_k: bfloat16 [768, 768], P(('mode', 'dp')), may hold values from -0.21875 to 0.21875
- self_v: bfloat16 [768, 768], P(('mode', 'dp')), may hold values from -0.21875 to 0.21875
- self_o: bfloat16 [768, 768], P(('mode', 'dp')), may hold values from -1.75 to 1.75
- self_gain: bfloat16 [768], P(('mode', 'dp')), may hold values from 0.5 to 1.5
- cross_q: bfloat16 [768, 768], P(('mode', 'dp')), may hold values from -0.21875 to 0.21875
- cross_k: bfloat16 [768, 768], P(('mode', 'dp')), may hold values from -0.21875 to 0.21875
- cross_v: bfloat16 [768, 768], P(('mode', 'dp')), may hold values from -0.21875 to 0.21875
- cross_o: bfloat16 [768, 768], P(('mode', 'dp')), may hold values from -1.75 to 1.75
- cross_gain: bfloat16 [768], P(('mode', 'dp')), may hold values from 0.5 to 1.5
- ffn_gain: bfloat16 [768], P(('mode', 'dp')), may hold values from 0.5 to 1.5
- ffn_gate: bfloat16 [4, 768, 2048], P('mode', 'dp'), may hold values from -0.21875 to 0.21875
- ffn_up: bfloat16 [4, 768, 2048], P('mode', 'dp'), may hold values from -0.21875 to 0.21875
- ffn_down: bfloat16 [4, 2048, 768], P('mode', 'dp'), may hold values from -0.125 to 0.125
Outputs:
- output: bfloat16 [32, 1024, 768], P(('mode', 'dp'))
- rows_grad: bfloat16 [32, 1024, 768], P(('mode', 'dp'))
- memory_grad: bfloat16 [32, 512, 768], P(('mode', 'dp'))
- self_q_grad: float32 [768, 768], P(('mode', 'dp'))
- self_k_grad: float32 [768, 768], P(('mode', 'dp'))
- self_v_grad: float32 [768, 768], P(('mode', 'dp'))
- self_o_grad: float32 [768, 768], P(('mode', 'dp'))
- self_gain_grad: float32 [768], P(('mode', 'dp'))
- cross_q_grad: float32 [768, 768], P(('mode', 'dp'))
- cross_k_grad: float32 [768, 768], P(('mode', 'dp'))
- cross_v_grad: float32 [768, 768], P(('mode', 'dp'))
- cross_o_grad: float32 [768, 768], P(('mode', 'dp'))
- cross_gain_grad: float32 [768], P(('mode', 'dp'))
- ffn_gain_grad: float32 [768], P(('mode', 'dp'))
- ffn_gate_grad: float32 [4, 768, 2048], P('mode', 'dp')
- ffn_up_grad: float32 [4, 768, 2048], P('mode', 'dp')
- ffn_down_grad: float32 [4, 2048, 768], P('mode', 'dp')
Inputs may be any that keep to these rules, and one draw needn't show every extreme that they name: `mode_ids`: each mode names exactly one in 4 of the rows.
All inputs are finite; a program needn't handle non-finite values.
Results may differ from a plain program's by a relative error of at most 0.022.
Values may be sent and summed in bfloat16 or wider, within the bound.
No kernel may reach another device: no remote copies, remote signals or barrier semaphores. Data moves between devices by JAX's collectives and lax.ppermute only.
A program may use at most 320 MiB of HBM per device.

v0:
```python
import jax
import jax.numpy as jnp
from jax import lax
from jax.sharding import PartitionSpec as P

HEADS = 12
HEAD_DIM = 64


EPS = 1e-06
NEG = -1e30


def norm_piece(value, gain):
    return value * lax.rsqrt(jnp.mean(value * value, axis=-1, keepdims=True) + EPS) * gain


def product(left, right):
    return jnp.dot(left, right, preferred_element_type=jnp.float32)


def product_left(left, right):
    return lax.dot_general(
        left, right, (((0,), (0,)), ((), ())), preferred_element_type=jnp.float32
    )


def product_right(left, right):
    return lax.dot_general(
        left, right, (((1,), (1,)), ((), ())), preferred_element_type=jnp.float32
    )


def allowed_keys(start, block, key_count, limit, causal):
    query_pos = start + jnp.arange(block, dtype=jnp.int32)
    key_pos = jnp.arange(key_count, dtype=jnp.int32)
    if causal:
        return key_pos[None, :] <= query_pos[:, None]
    return jnp.broadcast_to(key_pos[None, :] < limit, (block, key_count))


def attend_forward(query, keys, values, limit, causal):
    length = query.shape[0]
    key_count = keys.shape[0]
    block = min(512, length)
    scale = float(HEAD_DIM) ** (-0.5)
    query_heads = query.reshape(length // block, block, HEADS, HEAD_DIM)
    key_heads = keys.reshape(key_count, HEADS, HEAD_DIM)
    value_heads = values.reshape(key_count, HEADS, HEAD_DIM)
    starts = jnp.arange(length // block, dtype=jnp.int32) * block

    def one_block(item):
        query_block, start = item
        allowed = allowed_keys(start, block, key_count, limit, causal)
        raw = (
            jnp.einsum("qhd,khd->hqk", query_block, key_heads, preferred_element_type=jnp.float32)
            * scale
        )
        raw = jnp.where(allowed[None], raw, NEG)
        top = jnp.max(raw, axis=-1, keepdims=True)
        expo = jnp.exp(raw - top)
        total = jnp.sum(expo, axis=-1, keepdims=True)
        weights = (expo / total).astype(jnp.bfloat16)
        mixed = jnp.einsum("hqk,khd->qhd", weights, value_heads, preferred_element_type=jnp.float32)
        return (mixed.reshape(block, HEADS * HEAD_DIM), top[..., 0] + jnp.log(total[..., 0]))

    mixed, log_total = lax.map(one_block, (query_heads, starts))
    return (mixed.reshape(length, HEADS * HEAD_DIM), log_total)


def attend_backward(query, keys, values, log_total, grad_mixed, limit, causal):
    length = query.shape[0]
    key_count = keys.shape[0]
    block = min(512, length)
    scale = float(HEAD_DIM) ** (-0.5)
    query_heads = query.reshape(length // block, block, HEADS, HEAD_DIM)
    grad_heads = grad_mixed.reshape(length // block, block, HEADS, HEAD_DIM)
    key_heads = keys.reshape(key_count, HEADS, HEAD_DIM)
    value_heads = values.reshape(key_count, HEADS, HEAD_DIM)
    starts = jnp.arange(length // block, dtype=jnp.int32) * block

    def one_block(carry, item):
        grad_keys, grad_values = carry
        query_block, grad_block, log_block, start = item
        allowed = allowed_keys(start, block, key_count, limit, causal)
        raw = (
            jnp.einsum("qhd,khd->hqk", query_block, key_heads, preferred_element_type=jnp.float32)
            * scale
        )
        probs = jnp.where(allowed[None], jnp.exp(raw - log_block[..., None]), 0.0)
        grad_probs = jnp.einsum(
            "qhd,khd->hqk", grad_block, value_heads, preferred_element_type=jnp.float32
        )
        inner = jnp.sum(probs * grad_probs, axis=-1, keepdims=True)
        grad_scores = (probs * (grad_probs - inner)).astype(jnp.bfloat16)
        grad_query = (
            jnp.einsum("hqk,khd->qhd", grad_scores, key_heads, preferred_element_type=jnp.float32)
            * scale
        )
        grad_keys = (
            grad_keys
            + jnp.einsum(
                "hqk,qhd->khd", grad_scores, query_block, preferred_element_type=jnp.float32
            )
            * scale
        )
        grad_values = grad_values + jnp.einsum(
            "hqk,qhd->khd",
            probs.astype(jnp.bfloat16),
            grad_block,
            preferred_element_type=jnp.float32,
        )
        return ((grad_keys, grad_values), grad_query.reshape(block, HEADS * HEAD_DIM))

    empty = jnp.zeros((key_count, HEADS, HEAD_DIM), jnp.float32)
    sums, grad_query = lax.scan(
        one_block, (empty, empty), (query_heads, grad_heads, log_total, starts)
    )
    return (
        grad_query.reshape(length, HEADS * HEAD_DIM),
        sums[0].reshape(key_count, HEADS * HEAD_DIM),
        sums[1].reshape(key_count, HEADS * HEAD_DIM),
    )


def split_rows(value, count):
    return value.reshape(count, value.shape[0] // count, value.shape[1])


def move_rows(first, second, third, order):
    count = lax.axis_size(("mode", "dp"))
    spread = (
        lax.all_to_all(
            split_rows(first, count), ("mode", "dp"), split_axis=0, concat_axis=0, tiled=True
        ),
        lax.all_to_all(
            split_rows(second, count), ("mode", "dp"), split_axis=0, concat_axis=0, tiled=True
        ),
        lax.all_to_all(
            split_rows(third, count), ("mode", "dp"), split_axis=0, concat_axis=0, tiled=True
        ),
    )
    picked_a = jnp.take(spread[0], order, axis=0)
    picked_b = jnp.take(spread[1], order, axis=0)
    picked_c = jnp.take(spread[2], order, axis=0)
    settled = (
        lax.all_to_all(picked_a, ("mode", "dp"), split_axis=0, concat_axis=0, tiled=True),
        lax.all_to_all(picked_b, ("mode", "dp"), split_axis=0, concat_axis=0, tiled=True),
        lax.all_to_all(picked_c, ("mode", "dp"), split_axis=0, concat_axis=0, tiled=True),
    )
    return tuple((piece.reshape(-1, piece.shape[2]) for piece in settled))


def gelu_piece(gate, up):
    return jax.nn.gelu(gate, approximate=True) * up


def on_device(
    rows,
    memory,
    cotangent,
    mode_ids,
    target_lengths,
    encoder_lengths,
    self_q,
    self_k,
    self_v,
    self_o,
    self_gain,
    cross_q,
    cross_k,
    cross_v,
    cross_o,
    cross_gain,
    ffn_gain,
    ffn_gate,
    ffn_up,
    ffn_down,
):
    devices = lax.axis_size(("mode", "dp"))
    per_mode = lax.axis_size("dp")
    here = lax.axis_index(("mode", "dp"))
    index = jnp.arange(devices, dtype=jnp.int32)
    same = mode_ids[:, None] == mode_ids[None, :]
    earlier = index[None, :] < index[:, None]
    rank = jnp.sum(jnp.where(same & earlier, 1, 0), axis=1).astype(jnp.int32)
    target = mode_ids * per_mode + rank
    source = jnp.sum(jnp.where(target[:, None] == index[None, :], index[:, None], 0), axis=0)
    held = jnp.sum(jnp.where(index == here, source, 0))
    live_len = jnp.sum(jnp.where(index == held, target_lengths, 0))
    memory_len = jnp.sum(jnp.where(index == held, encoder_lengths, 0))
    tokens, memory_row, incoming = move_rows(rows[0], memory[0], cotangent[0], source)
    wq, wk, wv, wo, gain_self = (
        lax.all_gather(self_q, ("mode", "dp"), axis=0, tiled=True),
        lax.all_gather(self_k, ("mode", "dp"), axis=0, tiled=True),
        lax.all_gather(self_v, ("mode", "dp"), axis=0, tiled=True),
        lax.all_gather(self_o, ("mode", "dp"), axis=0, tiled=True),
        lax.all_gather(self_gain, ("mode", "dp"), axis=0, tiled=True),
    )
    tokens_wide = tokens.astype(jnp.float32)
    h1 = norm_piece(tokens_wide, gain_self.astype(jnp.float32)).astype(jnp.bfloat16)
    query = product(h1, wq).astype(jnp.bfloat16)
    keys = product(h1, wk).astype(jnp.bfloat16)
    values = product(h1, wv).astype(jnp.bfloat16)
    mixed, log_self = attend_forward(query, keys, values, 0, True)
    mixed = mixed.astype(jnp.bfloat16)
    x1 = tokens_wide + product(mixed, wo)
    cq, ck, cv, co, gain_cross, gain_ffn = (
        lax.all_gather(cross_q, ("mode", "dp"), axis=0, tiled=True),
        lax.all_gather(cross_k, ("mode", "dp"), axis=0, tiled=True),
        lax.all_gather(cross_v, ("mode", "dp"), axis=0, tiled=True),
        lax.all_gather(cross_o, ("mode", "dp"), axis=0, tiled=True),
        lax.all_gather(cross_gain, ("mode", "dp"), axis=0, tiled=True),
        lax.all_gather(ffn_gain, ("mode", "dp"), axis=0, tiled=True),
    )
    h2 = norm_piece(x1, gain_cross.astype(jnp.float32)).astype(jnp.bfloat16)
    cross_query = product(h2, cq).astype(jnp.bfloat16)
    cross_keys = product(memory_row, ck).astype(jnp.bfloat16)
    cross_values = product(memory_row, cv).astype(jnp.bfloat16)
    cross_mixed, log_cross = attend_forward(
        cross_query, cross_keys, cross_values, memory_len, False
    )
    cross_mixed = cross_mixed.astype(jnp.bfloat16)
    x2 = x1 + product(cross_mixed, co)
    gathered = (
        lax.all_gather(ffn_gate, "dp", axis=1, tiled=True),
        lax.all_gather(ffn_up, "dp", axis=1, tiled=True),
        lax.all_gather(ffn_down, "dp", axis=1, tiled=True),
    )
    wg, wu, wd = (gathered[0][0], gathered[1][0], gathered[2][0])
    h3 = norm_piece(x2, gain_ffn.astype(jnp.float32)).astype(jnp.bfloat16)
    gate = product(h3, wg)
    up = product(h3, wu)
    hidden = gelu_piece(gate, up).astype(jnp.bfloat16)
    valid = (jnp.arange(x2.shape[0], dtype=jnp.int32) < live_len)[:, None]
    result = jnp.where(valid, x2 + product(hidden, wd), 0.0).astype(jnp.bfloat16)
    grad = jnp.where(valid, incoming.astype(jnp.float32), 0.0)
    grad_low = grad.astype(jnp.bfloat16)
    grad_down = product_left(hidden, grad_low)
    grad_hidden = product_right(grad_low, wd)
    unused, pull_gelu = jax.vjp(gelu_piece, gate, up)
    grad_gate, grad_up = pull_gelu(grad_hidden)
    grad_gate = grad_gate.astype(jnp.bfloat16)
    grad_up = grad_up.astype(jnp.bfloat16)
    grad_wg = product_left(h3, grad_gate)
    grad_wu = product_left(h3, grad_up)
    grad_h3 = product_right(grad_gate, wg) + product_right(grad_up, wu)
    unused, pull_norm = jax.vjp(norm_piece, x2, gain_ffn.astype(jnp.float32))
    grad_x2_norm, grad_gain_ffn = pull_norm(grad_h3)
    grad_x2 = grad + grad_x2_norm
    ffn_sums = (
        lax.psum_scatter(
            grad_wg[None].astype(jnp.bfloat16), "dp", scatter_dimension=1, tiled=True
        ).astype(jnp.float32),
        lax.psum_scatter(
            grad_wu[None].astype(jnp.bfloat16), "dp", scatter_dimension=1, tiled=True
        ).astype(jnp.float32),
        lax.psum_scatter(
            grad_down[None].astype(jnp.bfloat16), "dp", scatter_dimension=1, tiled=True
        ).astype(jnp.float32),
    )
    grad_two = grad_x2.astype(jnp.bfloat16)
    grad_co = product_left(cross_mixed, grad_two)
    grad_cross_mixed = product_right(grad_two, co).astype(jnp.bfloat16)
    grad_cq_act, grad_ck_act, grad_cv_act = attend_backward(
        cross_query, cross_keys, cross_values, log_cross, grad_cross_mixed, memory_len, False
    )
    grad_cq_act = grad_cq_act.astype(jnp.bfloat16)
    grad_ck_act = grad_ck_act.astype(jnp.bfloat16)
    grad_cv_act = grad_cv_act.astype(jnp.bfloat16)
    grad_cq = product_left(h2, grad_cq_act)
    grad_ck = product_left(memory_row, grad_ck_act)
    grad_cv = product_left(memory_row, grad_cv_act)
    grad_memory = product_right(grad_ck_act, ck) + product_right(grad_cv_act, cv)
    grad_h2 = product_right(grad_cq_act, cq)
    unused, pull_norm = jax.vjp(norm_piece, x1, gain_cross.astype(jnp.float32))
    grad_x1_norm, grad_gain_cross = pull_norm(grad_h2)
    grad_x1 = grad_x2 + grad_x1_norm
    cross_sums = (
        lax.psum_scatter(grad_cq, ("mode", "dp"), scatter_dimension=0, tiled=True),
        lax.psum_scatter(grad_ck, ("mode", "dp"), scatter_dimension=0, tiled=True),
        lax.psum_scatter(grad_cv, ("mode", "dp"), scatter_dimension=0, tiled=True),
        lax.psum_scatter(grad_co, ("mode", "dp"), scatter_dimension=0, tiled=True),
        lax.psum_scatter(grad_gain_cross, ("mode", "dp"), scatter_dimension=0, tiled=True),
        lax.psum_scatter(grad_gain_ffn, ("mode", "dp"), scatter_dimension=0, tiled=True),
    )
    grad_one = grad_x1.astype(jnp.bfloat16)
    grad_wo = product_left(mixed, grad_one)
    grad_mixed = product_right(grad_one, wo).astype(jnp.bfloat16)
    grad_q_act, grad_k_act, grad_v_act = attend_backward(
        query, keys, values, log_self, grad_mixed, 0, True
    )
    grad_q_act = grad_q_act.astype(jnp.bfloat16)
    grad_k_act = grad_k_act.astype(jnp.bfloat16)
    grad_v_act = grad_v_act.astype(jnp.bfloat16)
    grad_wq = product_left(h1, grad_q_act)
    grad_wk = product_left(h1, grad_k_act)
    grad_wv = product_left(h1, grad_v_act)
    grad_h1 = (
        product_right(grad_q_act, wq)
        + product_right(grad_k_act, wk)
        + product_right(grad_v_act, wv)
    )
    unused, pull_norm = jax.vjp(norm_piece, tokens_wide, gain_self.astype(jnp.float32))
    grad_x_norm, grad_gain_self = pull_norm(grad_h1)
    grad_tokens = grad_x1 + grad_x_norm
    self_sums = (
        lax.psum_scatter(grad_wq, ("mode", "dp"), scatter_dimension=0, tiled=True),
        lax.psum_scatter(grad_wk, ("mode", "dp"), scatter_dimension=0, tiled=True),
        lax.psum_scatter(grad_wv, ("mode", "dp"), scatter_dimension=0, tiled=True),
        lax.psum_scatter(grad_wo, ("mode", "dp"), scatter_dimension=0, tiled=True),
        lax.psum_scatter(grad_gain_self, ("mode", "dp"), scatter_dimension=0, tiled=True),
    )
    output, rows_grad, memory_grad = move_rows(
        result, grad_tokens.astype(jnp.bfloat16), grad_memory.astype(jnp.bfloat16), target
    )
    return (
        output[None],
        rows_grad[None],
        memory_grad[None],
        self_sums[0],
        self_sums[1],
        self_sums[2],
        self_sums[3],
        self_sums[4],
        cross_sums[0],
        cross_sums[1],
        cross_sums[2],
        cross_sums[3],
        cross_sums[4],
        cross_sums[5],
        ffn_sums[0],
        ffn_sums[1],
        ffn_sums[2],
    )


def solution(mesh):
    placed = (
        P(("mode", "dp"), None, None),
        P(("mode", "dp"), None, None),
        P(("mode", "dp"), None, None),
        P(),
        P(),
        P(),
        P(("mode", "dp"), None),
        P(("mode", "dp"), None),
        P(("mode", "dp"), None),
        P(("mode", "dp"), None),
        P(("mode", "dp")),
        P(("mode", "dp"), None),
        P(("mode", "dp"), None),
        P(("mode", "dp"), None),
        P(("mode", "dp"), None),
        P(("mode", "dp")),
        P(("mode", "dp")),
        P("mode", "dp", None),
        P("mode", "dp", None),
        P("mode", "dp", None),
    )
    return jax.shard_map(
        on_device,
        mesh=mesh,
        in_specs=placed,
        out_specs=(
            P(("mode", "dp"), None, None),
            P(("mode", "dp"), None, None),
            P(("mode", "dp"), None, None),
            P(("mode", "dp"), None),
            P(("mode", "dp"), None),
            P(("mode", "dp"), None),
            P(("mode", "dp"), None),
            P(("mode", "dp")),
            P(("mode", "dp"), None),
            P(("mode", "dp"), None),
            P(("mode", "dp"), None),
            P(("mode", "dp"), None),
            P(("mode", "dp")),
            P(("mode", "dp")),
            P("mode", "dp", None),
            P("mode", "dp", None),
            P("mode", "dp", None),
        ),
        check_vma=False,
    )
```

profile of v0, /device:TPU:0, one launch (start us, length us, event | category | flops | bytes accessed | tf_op | source)
XLA Modules:
  0.0 1603.1 jit_solution(676722133729145396)
XLA Ops:
  20.7 22.0 %all-to-all-done.2 = bf16[32,16,768]{2,1,0:T(8,128)(2,1)S(1)} async-done(((bf16[32,16,768]{2,1,0:T(8,128)(2,1)}), bf16[32,16,768]{2,1,0:T(8,128)(2,1)S(1)}, u32[]{:S(2)}, u32[]{:S(2)}) %all-to-all-start.2) | async-done | bytes 786464 | tf_op jit(solution)/shard_map/all_to_all | solution.py:136
  42.7 45.0 %all_to_all.60 = bf16[32,32,768]{2,1,0:T(8,128)(2,1)} all-to-all(bf16[32,32,768]{2,1,0:T(8,128)(2,1)S(1)} %bitcast.311), channel_id=1, replica_groups=mesh['mode'=4,'dp'=8] {'mode','dp'}, dimensions={0} | all-to-all | bytes 3145728 | tf_op jit(solution)/shard_map/all_to_all | solution.py:133
  94.1 40.0 %all-to-all-done.6 = bf16[32,32,768]{2,1,0:T(8,128)(2,1)S(1)} async-done(((bf16[32,32,768]{2,1,0:T(8,128)(2,1)}), bf16[32,32,768]{2,1,0:T(8,128)(2,1)S(1)}, u32[]{:S(2)}, u32[]{:S(2)}) %all-to-all-start.6) | async-done | bytes 1572896 | tf_op jit(solution)/shard_map/all_to_all | solution.py:139
  163.7 60.8 %all-reduce.7 = (bf16[768]{0:T(1024)(128)(2,1)S(1)}, bf16[768]{0:T(1024)(128)(2,1)S(1)}, bf16[768]{0:T(1024)(128)(2,1)S(1)}) all-reduce(bf16[768]{0:T(1024)(128)(2,1)S(1)} %dynamic-update-slice, bf16[768]{0:T(1024)(128)(2,1)S(1)} %dynamic-update-slice.1, ...), channel_id=1, replica_groups=mesh['mode'=4,'dp'=8] {'mode','dp'}, use_global_device_ids=true, to_apply=%add | all-reduce | flops 2304 | bytes 9216
  261.0 55.5 %all-gather.14.cloned.1.call-done = bf16[768,768]{1,0:T(8,128)(2,1)} async-done(((bf16[24,768]{1,0:T(8,128)(2,1)}), bf16[768,768]{1,0:T(8,128)(2,1)}) %all-gather.14.cloned.1.call-update) | async-done | bytes 1179664 | tf_op jit(solution)/shard_map/all_gather | solution.py:195
  320.9 81.4 %while.54 = (s32[]{:T(128)}, bf16[2,512,768]{2,1,0:T(8,128)(2,1)}, f32[2,12,512]{2,1,0:T(8,128)S(1)}, s32[2]{0:T(128)S(1)}, bf16[2,512,12,64]{1,3,2,0:T(8,128)(2...) while((s32[]{:T(128)}, bf16[2,512,768]{2,1,0:T(8,128)(2,1)}, ...), condition=%wide.region_8.10_spmd, body=%wide.region_5.9_spmd.sunk | while | flops 1686628864 | bytes 192639152 | solution.py:67
  409.4 19.3 %all-gather.20.cloned.1.call-done = bf16[768,768]{1,0:T(8,128)(2,1)} async-done(((bf16[24,768]{1,0:T(8,128)(2,1)}), bf16[768,768]{1,0:T(8,128)(2,1)}) %all-gather.20.cloned.1.call-update) | async-done | bytes 1179664 | tf_op jit(solution)/shard_map/all_gather | solution.py:209
  439.0 28.0 %while.55 = (s32[]{:T(128)}, bf16[2,512,768]{2,1,0:T(8,128)(2,1)}, f32[2,12,512]{2,1,0:T(8,128)S(1)}, s32[]{:T(128)}, bf16[2,512,12,64]{1,3,2,0:T(8,128)(2,1)S(1...) while((s32[]{:T(128)}, bf16[2,512,768]{2,1,0:T(8,128)(2,1)}, ...), condition=%wide.region_14.17_spmd, body=%wide.region_11.16_spmd.sunk | while | flops 843049472 | bytes 44263532 | solution.py:67
  495.3 28.5 %all-gather.32.cloned.1.call-done = bf16[1,2048,768]{2,1,0:T(8,128)(2,1)} async-done(((bf16[1,256,768]{2,1,0:T(8,128)(2,1)}), bf16[1,2048,768]{2,1,0:T(8,128)(2,1)}) %all-gather.32.cloned.1.call-update) | async-done | bytes 3145744 | tf_op jit(solution)/shard_map/all_gather | solution.py:228
  533.0 29.5 %all-gather.30.cloned.1.call-done = bf16[1,768,2048]{2,1,0:T(8,128)(2,1)} async-done(((bf16[1,96,2048]{2,1,0:T(8,128)(2,1)}), bf16[1,768,2048]{2,1,0:T(8,128)(2,1)}) %all-gather.30.cloned.1.call-update) | async-done | bytes 3145744 | tf_op jit(solution)/shard_map/all_gather | solution.py:227
  571.6 29.7 %all-gather.28.cloned.1.call-done = bf16[1,768,2048]{2,1,0:T(8,128)(2,1)} async-done(((bf16[1,96,2048]{2,1,0:T(8,128)(2,1)}), bf16[1,768,2048]{2,1,0:T(8,128)(2,1)}) %all-gather.28.cloned.1.call-update) | async-done | bytes 3145744 | tf_op jit(solution)/shard_map/all_gather | solution.py:226
  674.3 58.0 %while.56 = (s32[]{:T(128)}, f32[512,12,64]{0,2,1:T(8,128)}, f32[512,12,64]{0,2,1:T(8,128)}, bf16[2,512,768]{2,1,0:T(8,128)(2,1)}, bf16[2,512,12,64]{1,3,2,0:T(8...) while((s32[]{:T(128)}, f32[512,12,64]{0,2,1:T(8,128)}, ...), condition=%wide.region_19.22_spmd.clone, body=%wide.region_17.21_spmd.clone.sunk | while | flops 2063198720 | bytes 141748528 | solution.py:116
  782.1 176.2 %while.57 = (s32[]{:T(128)}, f32[1024,12,64]{0,2,1:T(8,128)}, f32[1024,12,64]{0,2,1:T(8,128)}, bf16[2,512,768]{2,1,0:T(8,128)(2,1)}, bf16[2,512,12,64]{1,3,2,0:T...) while((s32[]{:T(128)}, f32[1024,12,64]{0,2,1:T(8,128)}, ...), condition=%wide.region_23.26_spmd.clone, body=%wide.region_21.25_spmd.clone.sunk | while | flops 4126140928 | bytes 227987696 | solution.py:116
  808.8 18.3 %multiply_reduce_fusion.11 = (f32[12,512]{1,0:T(8,128)S(1)}, f32[12,512,1024]{2,1,0:T(8,128)}) fusion(f32[12,512,1024]{2,1,0:T(8,128)} %fusion.251, f32[12,512]{1,0:T(8,128)S(1)} %dynamic-slice_bitcast_fusion.5, pred[512,1024]{1,0:T(8,128)(4,1)S(1)} %iota_compare_fusion.14, bf16[1024,12,64]{0,2,1:T(8,128)(2,1)} %get-tuple-element.866, ...), kind=kOutput, calls=%fused_computation.66.clone.1 | convolution fusion | flops 836757504 | bytes 53264388 | tf_op jit(solution)/shard_map/while/body/eval_jaxpr/qhd,khd->hqk/dot_general | solution.py:91
  827.0 21.5 %multiply_convert_fusion.11 = bf16[12,512,1024]{2,1,0:T(8,128)(2,1)} fusion(f32[12,512,1024]{2,1,0:T(8,128)} %get-tuple-element.747, f32[12,512,1024]{2,1,0:T(8,128)} %fusion.251, f32[12,512]{1,0:T(8,128)S(1)} %get-tuple-element.748, f32[12,512]{1,0:T(8,128)S(1)} %dynamic-slice_bitcast_fusion.5, pred[512,1024]{1,0:T(8,128)(4,1)S(1)} %iota_compare_fusion.14), kind=kLoop, calls=%fused_computation.65.clone.1 | loop fusion | flops 37748736 | bytes 63488000 | tf_op jit(solution)/shard_map/while/body/eval_jaxpr/convert_element_type | solution.py:95
  896.5 18.3 %multiply_reduce_fusion.11 = (f32[12,512]{1,0:T(8,128)S(1)}, f32[12,512,1024]{2,1,0:T(8,128)}) fusion(f32[12,512,1024]{2,1,0:T(8,128)} %fusion.251, f32[12,512]{1,0:T(8,128)S(1)} %dynamic-slice_bitcast_fusion.5, pred[512,1024]{1,0:T(8,128)(4,1)S(1)} %iota_compare_fusion.14, bf16[1024,12,64]{0,2,1:T(8,128)(2,1)} %get-tuple-element.866, ...), kind=kOutput, calls=%fused_computation.66.clone.1 | convolution fusion | flops 836757504 | bytes 53264388 | tf_op jit(solution)/shard_map/while/body/eval_jaxpr/qhd,khd->hqk/dot_general | solution.py:91
  914.8 21.8 %multiply_convert_fusion.11 = bf16[12,512,1024]{2,1,0:T(8,128)(2,1)} fusion(f32[12,512,1024]{2,1,0:T(8,128)} %get-tuple-element.747, f32[12,512,1024]{2,1,0:T(8,128)} %fusion.251, f32[12,512]{1,0:T(8,128)S(1)} %get-tuple-element.748, f32[12,512]{1,0:T(8,128)S(1)} %dynamic-slice_bitcast_fusion.5, pred[512,1024]{1,0:T(8,128)(4,1)S(1)} %iota_compare_fusion.14), kind=kLoop, calls=%fused_computation.65.clone.1 | loop fusion | flops 37748736 | bytes 63488000 | tf_op jit(solution)/shard_map/while/body/eval_jaxpr/convert_element_type | solution.py:95
  989.9 34.9 %all-to-all-done.8 = bf16[32,32,768]{2,1,0:T(8,128)(2,1)S(1)} async-done(((bf16[32,32,768]{2,1,0:T(8,128)(2,1)}), bf16[32,32,768]{2,1,0:T(8,128)(2,1)S(1)}, u32[]{:S(2)}, u32[]{:S(2)}) %all-to-all-start.8) | async-done | bytes 1572896 | tf_op jit(solution)/shard_map/all_to_all | solution.py:136
  1060.4 35.6 %all-to-all-done.9 = bf16[32,32,768]{2,1,0:T(8,128)(2,1)S(1)} async-done(((bf16[32,32,768]{2,1,0:T(8,128)(2,1)}), bf16[32,32,768]{2,1,0:T(8,128)(2,1)S(1)}, u32[]{:S(2)}, u32[]{:S(2)}) %all-to-all-start.9) | async-done | bytes 1572896 | tf_op jit(solution)/shard_map/all_to_all | solution.py:148
  1098.7 64.4 %all-reduce.6 = (f32[768]{0:T(1024)S(1)}, f32[768]{0:T(1024)S(1)}, f32[768]{0:T(1024)S(1)}) all-reduce(f32[768]{0:T(1024)S(1)} %get-tuple-element.419, f32[768]{0:T(1024)S(1)} %copy-done.60, f32[768]{0:T(1024)S(1)} %copy-done.59), channel_id=6, replica_groups=mesh['mode'=4,'dp'=8] {'mode','dp'}, use_global_device_ids=true, to_apply=%region_30.33.clone | all-reduce | flops 2304 | bytes 18432
  1174.3 103.8 %reduce-scatter.18.cloned.1.call-done = f32[24,768]{1,0:T(8,128)} async-done(((f32[768,768]{1,0:T(8,128)}), f32[24,768]{1,0:T(8,128)}) %reduce-scatter.18.cloned.1.call-update) | async-done | bytes 73744 | tf_op jit(solution)/shard_map/reduce_scatter | solution.py:311
  1278.1 104.6 %reduce-scatter.14.cloned.1.call-done = f32[24,768]{1,0:T(8,128)} async-done(((f32[768,768]{1,0:T(8,128)}), f32[24,768]{1,0:T(8,128)}) %reduce-scatter.14.cloned.1.call-update) | async-done | bytes 73744 | tf_op jit(solution)/shard_map/reduce_scatter | solution.py:309
  1382.7 104.0 %reduce-scatter.12.cloned.1.call-done = f32[24,768]{1,0:T(8,128)} async-done(((f32[768,768]{1,0:T(8,128)}), f32[24,768]{1,0:T(8,128)}) %reduce-scatter.12.cloned.1.call-update) | async-done | bytes 73744 | tf_op jit(solution)/shard_map/reduce_scatter | solution.py:308
  1486.7 104.8 %reduce-scatter.16.cloned.1.call-done = f32[24,768]{1,0:T(8,128)} async-done(((f32[768,768]{1,0:T(8,128)}), f32[24,768]{1,0:T(8,128)}) %reduce-scatter.16.cloned.1.call-update) | async-done | bytes 73744 | tf_op jit(solution)/shard_map/reduce_scatter | solution.py:310
  (443 shorter events, 623.9 us)
Async XLA Ops:
  7.2 222.3 %all-gather.24.cloned.1.call-start = ((), (), s32[]{:S(2)}) async-start(), calls=%async_computation.29 | async-start | bytes 1216512 | tf_op jit(solution)/shard_map/all_gather | solution.py:211
  7.9 224.8 %all-gather.22.cloned.1.call-start = ((), (), s32[]{:S(2)}) async-start(), calls=%async_computation.28 | async-start | bytes 1216512 | tf_op jit(solution)/shard_map/all_gather | solution.py:210
  8.7 234.6 %all-gather.12.cloned.1.call-start = ((), (), s32[]{:S(2)}) async-start(), calls=%async_computation.23 | async-start | bytes 1216512 | tf_op jit(solution)/shard_map/all_gather | solution.py:194
  9.4 247.7 %all-gather.16.cloned.1.call-start = ((), (), s32[]{:S(2)}) async-start(), calls=%async_computation.25 | async-start | bytes 1216512 | tf_op jit(solution)/shard_map/all_gather | solution.py:196
  10.0 306.5 %all-gather.14.cloned.1.call-start = ((), (), s32[]{:S(2)}) async-start(), calls=%async_computation.24 | async-start | bytes 1216512 | tf_op jit(solution)/shard_map/all_gather | solution.py:195
  10.6 391.8 %all-gather.18.cloned.1.call-start = ((), (), s32[]{:S(2)}) async-start(), calls=%async_computation.26 | async-start | bytes 1216512 | tf_op jit(solution)/shard_map/all_gather | solution.py:197
  11.2 417.6 %all-gather.20.cloned.1.call-start = ((), (), s32[]{:S(2)}) async-start(), calls=%async_computation.27 | async-start | bytes 1216512 | tf_op jit(solution)/shard_map/all_gather | solution.py:209
  11.9 473.0 %all-gather.26.cloned.1.call-start = ((), (), s32[]{:S(2)}) async-start(), calls=%async_computation.30 | async-start | bytes 1216512 | tf_op jit(solution)/shard_map/all_gather | solution.py:212
  20.0 503.8 %all-gather.32.cloned.1.call-start = ((), (), s32[]{:S(2)}) async-start(), calls=%async_computation.33 | async-start | bytes 3538944 | tf_op jit(solution)/shard_map/all_gather | solution.py:228
  90.5 472.0 %all-gather.30.cloned.1.call-start = ((), (), s32[]{:S(2)}) async-start(), calls=%async_computation.32 | async-start | bytes 3538944 | tf_op jit(solution)/shard_map/all_gather | solution.py:227
  162.2 439.0 %all-gather.28.cloned.1.call-start = ((), (), s32[]{:S(2)}) async-start(), calls=%async_computation.31 | async-start | bytes 3538944 | tf_op jit(solution)/shard_map/all_gather | solution.py:226
  236.0 254.7 %all-to-all-start.7 = ((bf16[32,32,768]{2,1,0:T(8,128)(2,1)}), bf16[32,32,768]{2,1,0:T(8,128)(2,1)}, u32[]{:S(2)}, u32[]{:S(2)}) async-start(bf16[32,32,768]{2,1,0:T(8,128)(2,1)} %get-tuple-element.514), calls=%async_computation.7 | async-start | bytes 3145728 | tf_op jit(solution)/shard_map/all_to_all | solution.py:149
  240.5 924.4 %reduce-scatter.28.cloned.1.call-start = ((), (), s32[]{:S(2)}) async-start(), calls=%async_computation.42 | async-start | bytes 3538944 | tf_op jit(solution)/shard_map/reduce_scatter | solution.py:252
  625.8 541.0 %reduce-scatter.30.cloned.1.call-start = ((), (), s32[]{:S(2)}) async-start(), calls=%async_computation.43 | async-start | bytes 3538944 | tf_op jit(solution)/shard_map/reduce_scatter | solution.py:255
  633.7 535.1 %reduce-scatter.32.cloned.1.call-start = ((), (), s32[]{:S(2)}) async-start(), calls=%async_computation.44 | async-start | bytes 3538944 | tf_op jit(solution)/shard_map/reduce_scatter | solution.py:258
  654.1 516.6 %reduce-scatter.26.cloned.1.call-start = ((), (), s32[]{:S(2)}) async-start(), calls=%async_computation.41 | async-start | bytes 2433024 | tf_op jit(solution)/shard_map/reduce_scatter | solution.py:283
  673.0 497.7 %reduce-scatter.24.cloned.1.call-start = ((), (), s32[]{:S(2)}) async-start(), calls=%async_computation.40 | async-start | bytes 2433024 | tf_op jit(solution)/shard_map/reduce_scatter | solution.py:282
  738.3 432.4 %reduce-scatter.22.cloned.1.call-start = ((), (), s32[]{:S(2)}) async-start(), calls=%async_computation.39 | async-start | bytes 2433024 | tf_op jit(solution)/shard_map/reduce_scatter | solution.py:281
  749.6 424.6 %reduce-scatter.20.cloned.1.call-start = ((), (), s32[]{:S(2)}) async-start(), calls=%async_computation.38 | async-start | bytes 2433024 | tf_op jit(solution)/shard_map/reduce_scatter | solution.py:280
  774.9 201.5 %all-to-all-start.4 = ((bf16[32,32,768]{2,1,0:T(8,128)(2,1)}), bf16[32,32,768]{2,1,0:T(8,128)(2,1)}, u32[]{:S(2)}, u32[]{:S(2)}) async-start(bf16[32,32,768]{2,1,0:T(8,128)(2,1)} %bitcast.313), calls=%async_computation.4 | async-start | bytes 3145728 | tf_op jit(solution)/shard_map/all_to_all | solution.py:133
  780.8 497.3 %reduce-scatter.18.cloned.1.call-start = ((), (), s32[]{:S(2)}) async-start(), calls=%async_computation.37 | async-start | bytes 2433024 | tf_op jit(solution)/shard_map/reduce_scatter | solution.py:311
  982.5 400.2 %reduce-scatter.14.cloned.1.call-start = ((), (), s32[]{:S(2)}) async-start(), calls=%async_computation.35 | async-start | bytes 2433024 | tf_op jit(solution)/shard_map/reduce_scatter | solution.py:309
  1028.2 458.5 %reduce-scatter.12.cloned.1.call-start = ((), (), s32[]{:S(2)}) async-start(), calls=%async_computation.34 | async-start | bytes 2433024 | tf_op jit(solution)/shard_map/reduce_scatter | solution.py:308
  1056.0 535.5 %reduce-scatter.16.cloned.1.call-start = ((), (), s32[]{:S(2)}) async-start(), calls=%async_computation.36 | async-start | bytes 2433024 | tf_op jit(solution)/shard_map/reduce_scatter | solution.py:310
  (98 other events, 1317.7 us)
Sparse Core Ops, SparseCore 0:
  11.1 63.4 all-gather.23
  77.6 57.1 all-gather.21
  137.8 60.8 all-gather.11
  201.6 55.4 all-gather.15
  259.9 56.4 all-gather.13
  319.3 53.1 all-gather.17
  375.5 53.1 all-gather.19
  431.7 53.1 all-gather.25
  486.5 37.2 all-gather.31
  525.3 37.1 all-gather.29
  564.1 37.1 all-gather.27
  625.9 39.2 reduce-scatter.27
  667.5 39.4 reduce-scatter.29
  709.1 39.4 reduce-scatter.31
  754.2 101.2 reduce-scatter.25
  862.1 97.9 reduce-scatter.23
  965.7 102.1 reduce-scatter.21
  1074.5 99.7 reduce-scatter.19
  1180.1 97.9 reduce-scatter.17
  1284.7 98.0 reduce-scatter.13
  1388.6 98.0 reduce-scatter.11
  1493.4 98.0 reduce-scatter.15
where the time goes:
time: 1610 us; the launch traced here: 1600 us
  waiting for transfers between devices  771 us (48%)
  matrix products  367 us (23%)
  blocking collectives  170 us (11%)
  other arithmetic  136 us (8%)
  local copies, waits for them, and re-layouts  97.1 us (6%)
  starting transfers between devices  45.9 us (3%)
    unnamed x2, blocking collectives  125 us
    reduce_scatter x1, waiting for transfers between devices, on_device(): lax.psum_scatter(grad_wv, ('mode', 'dp'), scatter_dimension=0, tiled=True)  105 us
    reduce_scatter x1, waiting for transfers between devices, on_device(): lax.psum_scatter(grad_wk, ('mode', 'dp'), scatter_dimension=0, tiled=True)  105 us
    reduce_scatter x1, waiting for transfers between devices, on_device(): lax.psum_scatter(grad_wq, ('mode', 'dp'), scatter_dimension=0, tiled=True)  104 us
    reduce_scatter x1, waiting for transfers between devices, on_device(): lax.psum_scatter(grad_wo, ('mode', 'dp'), scatter_dimension=0, tiled=True)  104 us
    dot_general x11, matrix products, product(): return jnp.dot(left, right, preferred_element_type=jnp.float32)  65 us
    convert_element_type x4, other arithmetic, one_block(): grad_scores = (probs * (grad_probs - inner)).astype(jnp.bfloat16)  57.6 us
    all_to_all x2, waiting for transfers between devices, move_rows(): lax.all_to_all(split_rows(second, count), ('mode', 'dp'), split_axis=0, c...  57 us
  transfers between devices with their start and end apart: 33, of which 18 were waited for; matrix products, arithmetic and copies ran while one was open for 34% of the time, Pallas kernels for 0%

commit v1 on v0

v1 whole, which is shorter than its diff:
```python
import functools

import jax
import jax.numpy as jnp
from jax import lax
from jax.experimental import pallas as pl
from jax.experimental.pallas import tpu as pltpu
from jax.sharding import PartitionSpec as P

HEADS = 12
HEAD_DIM = 64
PAIR = 2 * HEAD_DIM
EPS = 1e-06
NEG = -1e30
SCALE = HEAD_DIM ** -0.5
QB = 256
ALL = ("mode", "dp")
BF = jnp.bfloat16
F32 = jnp.float32
VMEM = 56 * 2**20


def nt(left, right):
    return lax.dot_general(left, right, (((1,), (1,)), ((), ())), preferred_element_type=F32)


def nn(left, right):
    return jnp.dot(left, right, preferred_element_type=F32)


def tn(left, right):
    return lax.dot_general(left, right, (((0,), (0,)), ((), ())), preferred_element_type=F32)


def head_lanes(value, h):
    lane = lax.broadcasted_iota(jnp.int32, value.shape, 1)
    return jnp.where((lane >= HEAD_DIM) == (h == 1), value, jnp.zeros_like(value))


def masks(causal, key_count, qb, limit):
    if causal:
        parts = []
        if qb:
            parts.append((0, qb * QB, None))
        row = lax.broadcasted_iota(jnp.int32, (QB, QB), 0)
        col = lax.broadcasted_iota(jnp.int32, (QB, QB), 1)
        parts.append((qb * QB, QB, row <= col))
        return parts
    row = lax.broadcasted_iota(jnp.int32, (key_count, QB), 0)
    return [(0, key_count, row < limit)]


def attend_fwd_kernel(causal, lens, q_ref, k_ref, v_ref, o_ref, lse_ref, vt):
    live, limit = lens[0], lens[1]
    length, key_count = q_ref.shape[0], k_ref.shape[0]
    vt[...] = jnp.swapaxes(v_ref[...].astype(F32), 0, 1).astype(BF)
    for qb in range(length // QB):
        at = pl.ds(qb * QB, QB)

        @pl.when(qb * QB < live)
        def _(qb=qb, at=at):
            query = q_ref[at, :] * jnp.asarray(SCALE, BF)
            parts = masks(causal, key_count, qb, limit)
            outs = []
            for h in range(2):
                mine = head_lanes(query, h)
                scores = []
                for first, count, mask in parts:
                    s = nt(k_ref[pl.ds(first, count), :], mine)
                    scores.append(s if mask is None else jnp.where(mask, s, NEG))
                top = functools.reduce(
                    jnp.maximum, [jnp.max(s, axis=0, keepdims=True) for s in scores]
                )
                total, mixed = 0.0, 0.0
                for (first, count, _), s in zip(parts, scores):
                    p = jnp.exp(s - top)
                    total = total + jnp.sum(p, axis=0, keepdims=True)
                    mixed = mixed + nn(
                        vt[pl.ds(h * HEAD_DIM, HEAD_DIM), pl.ds(first, count)], p.astype(BF)
                    )
                outs.append(mixed / total)
                lse_ref[0, pl.ds(h, 1), at] = top + jnp.log(total)
            o_ref[at, :] = jnp.swapaxes(jnp.concatenate(outs, axis=0), 0, 1).astype(BF)

        @pl.when(qb * QB >= live)
        def _(at=at):
            o_ref[at, :] = jnp.zeros((QB, PAIR), BF)
            lse_ref[0, pl.ds(0, 2), at] = jnp.zeros((2, QB), F32)


def attend_bwd_kernel(
    causal, lens, q_ref, k_ref, v_ref, o_ref, do_ref, lse_ref, dq_ref, dk_ref, dv_ref, kt, dk, dv
):
    live, limit = lens[0], lens[1]
    length, key_count = q_ref.shape[0], k_ref.shape[0]
    kt[...] = jnp.swapaxes(k_ref[...].astype(F32), 0, 1).astype(BF)
    dk[...] = jnp.zeros_like(dk)
    dv[...] = jnp.zeros_like(dv)
    for qb in range(length // QB):
        at = pl.ds(qb * QB, QB)

        @pl.when(qb * QB < live)
        def _(qb=qb, at=at):
            query = q_ref[at, :] * jnp.asarray(SCALE, BF)
            grad = do_ref[at, :]
            inner = jnp.swapaxes(o_ref[at, :].astype(F32) * grad.astype(F32), 0, 1)
            parts = masks(causal, key_count, qb, limit)
            sums = [[0.0, 0.0] for _ in parts]
            outs = []
            for h in range(2):
                mine = head_lanes(query, h)
                grad_mine = head_lanes(grad, h)
                lse = lse_ref[0, pl.ds(h, 1), at]
                delta = jnp.sum(inner[h * HEAD_DIM : (h + 1) * HEAD_DIM], axis=0, keepdims=True)
                grad_query = 0.0
                for i, (first, count, mask) in enumerate(parts):
                    keys = pl.ds(first, count)
                    p = jnp.exp(nt(k_ref[keys, :], mine) - lse)
                    if mask is not None:
                        p = jnp.where(mask, p, 0.0)
                    dp = nt(v_ref[keys, :], grad_mine)
                    ds = (p * (dp - delta)).astype(BF)
                    sums[i][0] = sums[i][0] + nn(ds, mine)
                    sums[i][1] = sums[i][1] + nn(p.astype(BF), grad_mine)
                    grad_query = grad_query + nn(kt[pl.ds(h * HEAD_DIM, HEAD_DIM), keys], ds)
                outs.append(grad_query * SCALE)
            for (first, count, _), (sum_k, sum_v) in zip(parts, sums):
                dk[pl.ds(first, count), :] += sum_k
                dv[pl.ds(first, count), :] += sum_v
            dq_ref[at, :] = jnp.swapaxes(jnp.concatenate(outs, axis=0), 0, 1).astype(BF)

        @pl.when(qb * QB >= live)
        def _(at=at):
            dq_ref[at, :] = jnp.zeros((QB, PAIR), BF)

    dk_ref[...] = dk[...].astype(BF)
    dv_ref[...] = dv[...].astype(BF)


def columns(rows, first):
    return pl.BlockSpec((rows, PAIR), lambda g, lens: (0, first + g))


def attend_forward(query, keys, values, lens, causal):
    (qa, q0), (ka, k0), (va, v0) = query, keys, values
    length, key_count = qa.shape[0], ka.shape[0]
    pairs = HEADS // 2
    pixels = length * key_count * HEADS // (2 if causal else 1)
    return pl.pallas_call(
        functools.partial(attend_fwd_kernel, causal),
        grid_spec=pltpu.PrefetchScalarGridSpec(
            num_scalar_prefetch=1,
            grid=(pairs,),
            in_specs=[columns(length, q0), columns(key_count, k0), columns(key_count, v0)],
            out_specs=[
                columns(length, 0),
                pl.BlockSpec((1, 2, length), lambda g, lens: (g, 0, 0)),
            ],
            scratch_shapes=[pltpu.VMEM((PAIR, key_count), BF)],
        ),
        out_shape=[
            jax.ShapeDtypeStruct((length, HEADS * HEAD_DIM), BF),
            jax.ShapeDtypeStruct((pairs, 2, length), F32),
        ],
        compiler_params=pltpu.CompilerParams(vmem_limit_bytes=VMEM),
        cost_estimate=pl.CostEstimate(
            flops=pixels * 4 * HEAD_DIM * 4, bytes_accessed=8 * length * 768, transcendentals=pixels
        ),
        name="attend_causal" if causal else "attend_memory",
    )(lens, qa, ka, va)


def attend_backward(query, keys, values, mixed, grad, lse, lens, causal):
    (qa, q0), (ka, k0), (va, v0) = query, keys, values
    length, key_count = qa.shape[0], ka.shape[0]
    pairs = HEADS // 2
    pixels = length * key_count * HEADS // (2 if causal else 1)
    return pl.pallas_call(
        functools.partial(attend_bwd_kernel, causal),
        grid_spec=pltpu.PrefetchScalarGridSpec(
            num_scalar_prefetch=1,
            grid=(pairs,),
            in_specs=[
                columns(length, q0),
                columns(key_count, k0),
                columns(key_count, v0),
                columns(length, 0),
                columns(length, 0),
                pl.BlockSpec((1, 2, length), lambda g, lens: (g, 0, 0)),
            ],
            out_specs=[columns(length, 0), columns(key_count, 0), columns(key_count, 0)],
            scratch_shapes=[
                pltpu.VMEM((PAIR, key_count), BF),
                pltpu.VMEM((key_count, PAIR), F32),
                pltpu.VMEM((key_count, PAIR), F32),
            ],
        ),
        out_shape=[
            jax.ShapeDtypeStruct((length, HEADS * HEAD_DIM), BF),
            jax.ShapeDtypeStruct((key_count, HEADS * HEAD_DIM), BF),
            jax.ShapeDtypeStruct((key_count, HEADS * HEAD_DIM), BF),
        ],
        compiler_params=pltpu.CompilerParams(vmem_limit_bytes=VMEM),
        cost_estimate=pl.CostEstimate(
            flops=pixels * 10 * HEAD_DIM * 3, bytes_accessed=16 * length * 768, transcendentals=pixels
        ),
        name="attend_causal_back" if causal else "attend_memory_back",
    )(lens, qa, ka, va, mixed, grad, lse)


GELU_A = 0.7978845608028654
GELU_B = 0.044715


def feed_kernel(
    h_ref, g_ref, gu_ref, down_ref, y_ref, dh_ref, hid_ref, dgu_ref, *, ff, step
):
    h, g = h_ref[...], g_ref[...]
    y, dh = 0.0, 0.0
    for c in range(0, ff, step):
        wg = gu_ref[:, pl.ds(c, step)]
        wu = gu_ref[:, pl.ds(ff + c, step)]
        wd = down_ref[pl.ds(c, step), :]
        gate, up, dhid = nn(h, wg), nn(h, wu), nt(g, wd)
        square = gate * gate
        th = jnp.tanh(gate * (GELU_A + (GELU_A * GELU_B) * square))
        half = 0.5 + 0.5 * th
        act = gate * half
        slope = half + (0.5 * gate) * (1.0 - th * th) * (
            GELU_A + (3.0 * GELU_A * GELU_B) * square
        )
        hidden = (act * up).astype(BF)
        dgate = (dhid * up * slope).astype(BF)
        dup = (dhid * act).astype(BF)
        hid_ref[:, pl.ds(c, step)] = hidden
        dgu_ref[:, pl.ds(c, step)] = dgate
        dgu_ref[:, pl.ds(ff + c, step)] = dup
        y = y + nn(hidden, wd)
        dh = dh + nt(dgate, wg) + nt(dup, wu)
    y_ref[...] = y.astype(BF)
    dh_ref[...] = dh.astype(BF)


def feed(h3, grad, wgu, wd):
    tokens, width = h3.shape
    ff = wd.shape[0]
    block = min(256, tokens)

    def by_token(n):
        return pl.BlockSpec((block, n), lambda i: (i, 0))

    def whole(a):
        return pl.BlockSpec(a.shape, lambda i: (0, 0))

    return pl.pallas_call(
        functools.partial(feed_kernel, ff=ff, step=512),
        grid=(tokens // block,),
        in_specs=[by_token(width), by_token(width), whole(wgu), whole(wd)],
        out_specs=[by_token(width), by_token(width), by_token(ff), by_token(2 * ff)],
        out_shape=[
            jax.ShapeDtypeStruct((tokens, width), BF),
            jax.ShapeDtypeStruct((tokens, width), BF),
            jax.ShapeDtypeStruct((tokens, ff), BF),
            jax.ShapeDtypeStruct((tokens, 2 * ff), BF),
        ],
        compiler_params=pltpu.CompilerParams(vmem_limit_bytes=VMEM),
        cost_estimate=pl.CostEstimate(
            flops=12 * tokens * width * ff, bytes_accessed=40 * 2**20, transcendentals=tokens * ff
        ),
        name="feed",
    )(h3, grad, wgu, wd)


def reorder_kernel(order, x_ref, o_ref):
    def move(i, carry):
        o_ref[i] = x_ref[order[i]]
        return carry

    lax.fori_loop(0, o_ref.shape[0], move, 0)


def reorder(value, order):
    return pl.pallas_call(
        reorder_kernel,
        grid_spec=pltpu.PrefetchScalarGridSpec(
            num_scalar_prefetch=1,
            grid=(1,),
            in_specs=[pl.BlockSpec(value.shape, lambda i, order: (0, 0, 0))],
            out_specs=pl.BlockSpec(value.shape, lambda i, order: (0, 0, 0)),
        ),
        out_shape=jax.ShapeDtypeStruct(value.shape, value.dtype),
        compiler_params=pltpu.CompilerParams(vmem_limit_bytes=16 * 2**20),
        cost_estimate=pl.CostEstimate(
            flops=0, bytes_accessed=2 * value.size * 2, transcendentals=0
        ),
        name="reorder",
    )(order, value)


def to_modes(value, source):
    count = lax.axis_size(ALL)
    tokens, width = value.shape
    piece = tokens // count
    dealt = value.reshape(piece // 8, count, 8, width).swapaxes(0, 1).reshape(count, piece, width)
    spread = lax.all_to_all(dealt, ALL, 0, 0, tiled=True)
    return lax.all_to_all(reorder(spread, source), "mode", 0, 0, tiled=True).reshape(tokens, width)


def from_modes(value, target):
    count = lax.axis_size(ALL)
    tokens, width = value.shape
    piece = tokens // count
    spread = lax.all_to_all(value.reshape(count, piece, width), "mode", 0, 0, tiled=True)
    dealt = lax.all_to_all(reorder(spread, target), ALL, 0, 0, tiled=True)
    return dealt.reshape(count, piece // 8, 8, width).swapaxes(0, 1).reshape(tokens, width)


def norm_piece(value, gain):
    return value * lax.rsqrt(jnp.mean(value * value, axis=-1, keepdims=True) + EPS) * gain


def gather_all(*pieces):
    return lax.all_gather(jnp.concatenate(pieces, axis=1), ALL, axis=0, tiled=True)


def lanes_of(*vectors):
    columns_ = jnp.stack(vectors, axis=1)
    return jnp.pad(columns_, ((0, 0), (0, 256 - len(vectors))))


def on_device(
    rows,
    memory,
    cotangent,
    mode_ids,
    target_lengths,
    encoder_lengths,
    self_q,
    self_k,
    self_v,
    self_o,
    self_gain,
    cross_q,
    cross_k,
    cross_v,
    cross_o,
    cross_gain,
    ffn_gain,
    ffn_gate,
    ffn_up,
    ffn_down,
):
    devices = lax.axis_size(ALL)
    per_mode = lax.axis_size("dp")
    here = lax.axis_index(ALL)
    width = rows.shape[2]
    ff = ffn_gate.shape[2]
    index = jnp.arange(devices, dtype=jnp.int32)
    same = mode_ids[:, None] == mode_ids[None, :]
    earlier = index[None, :] < index[:, None]
    rank = jnp.sum(jnp.where(same & earlier, 1, 0), axis=1).astype(jnp.int32)
    target = mode_ids * per_mode + rank
    source = jnp.sum(
        jnp.where(target[:, None] == index[None, :], index[:, None], 0), axis=0
    ).astype(jnp.int32)
    live_len = jnp.sum(jnp.where(index == here, target_lengths, 0))
    memory_len = jnp.sum(jnp.where(index == here, encoder_lengths, 0))
    lens = jnp.stack([live_len, memory_len]).astype(jnp.int32)
    tokens, memory_row, incoming = rows[0], memory[0], cotangent[0]
    valid = (jnp.arange(tokens.shape[0], dtype=jnp.int32) < live_len)[:, None]
    grad_low = jnp.where(valid, incoming, jnp.zeros_like(incoming))

    own = gather_all(self_q, self_k, self_v, self_o, lanes_of(self_gain, cross_gain, ffn_gain))
    crossing = gather_all(cross_q, cross_k, cross_v, cross_o)
    wgu = lax.all_gather(
        jnp.concatenate([ffn_gate[0], ffn_up[0]], axis=1), "dp", axis=0, tiled=True
    )
    wd = lax.all_gather(ffn_down[0], "dp", axis=0, tiled=True)
    routed_grad = to_modes(grad_low, source)

    wqkv, wo = own[:, : 3 * width], own[:, 3 * width : 4 * width]
    gains = own[:, 4 * width : 4 * width + 8].astype(F32)
    gain_self, gain_cross, gain_ffn = gains[:, 0], gains[:, 1], gains[:, 2]
    tokens_wide = tokens.astype(F32)
    h1 = norm_piece(tokens_wide, gain_self).astype(BF)
    qkv = nn(h1, wqkv).astype(BF)
    pairs = HEADS // 2
    self_in = ((qkv, 0), (qkv, pairs), (qkv, 2 * pairs))
    mixed, log_self = attend_forward(*self_in, lens, True)
    x1 = tokens_wide + nn(mixed, wo)

    cq, ckv, co = crossing[:, :width], crossing[:, width : 3 * width], crossing[:, 3 * width :]
    h2 = norm_piece(x1, gain_cross).astype(BF)
    cross_query = nn(h2, cq).astype(BF)
    cross_kv = nn(memory_row, ckv).astype(BF)
    cross_in = ((cross_query, 0), (cross_kv, 0), (cross_kv, pairs))
    cross_mixed, log_cross = attend_forward(*cross_in, lens, False)
    x2 = x1 + nn(cross_mixed, co)
    h3 = norm_piece(x2, gain_ffn).astype(BF)

    routed_h = to_modes(h3, source)
    routed_y, routed_dh, hidden, dgu = feed(routed_h, routed_grad, wgu, wd)
    grad_h3 = from_modes(routed_dh, target)
    y = from_modes(routed_y, target)
    grad_wgu = tn(routed_h, dgu).astype(BF)
    grad_wd = tn(hidden, routed_grad).astype(BF)
    sum_wgu = lax.psum_scatter(grad_wgu, "dp", scatter_dimension=0, tiled=True)
    sum_wd = lax.psum_scatter(grad_wd, "dp", scatter_dimension=0, tiled=True)
    result = jnp.where(valid, x2 + y.astype(F32), 0.0).astype(BF)

    unused, pull_norm = jax.vjp(norm_piece, x2, gain_ffn)
    grad_x2_norm, grad_gain_ffn = pull_norm(grad_h3.astype(F32))
    grad_x2 = grad_low.astype(F32) + grad_x2_norm
    grad_two = grad_x2.astype(BF)
    grad_co = tn(cross_mixed, grad_two)
    grad_cross_mixed = nt(grad_two, co).astype(BF)
    dcq, dck, dcv = attend_backward(
        *cross_in, cross_mixed, grad_cross_mixed, log_cross, lens, False
    )
    grad_cq = tn(h2, dcq)
    grad_ck = tn(memory_row, dck)
    grad_cv = tn(memory_row, dcv)
    grad_memory = (nt(dck, ckv[:, :width]) + nt(dcv, ckv[:, width:])).astype(BF)
    unused, pull_norm = jax.vjp(norm_piece, x1, gain_cross)
    grad_x1_norm, grad_gain_cross = pull_norm(nt(dcq, cq))
    grad_x1 = grad_x2 + grad_x1_norm
    cross_grads = jnp.concatenate(
        [grad_cq.astype(BF), grad_ck.astype(BF), grad_cv.astype(BF), grad_co.astype(BF)], axis=1
    )
    cross_sum = lax.psum_scatter(cross_grads, ALL, scatter_dimension=0, tiled=True)

    grad_one = grad_x1.astype(BF)
    grad_wo = tn(mixed, grad_one)
    grad_mixed = nt(grad_one, wo).astype(BF)
    dq, dk, dv = attend_backward(*self_in, mixed, grad_mixed, log_self, lens, True)
    grad_h1 = (
        nt(dq, wqkv[:, :width]) + nt(dk, wqkv[:, width : 2 * width]) + nt(dv, wqkv[:, 2 * width :])
    )
    unused, pull_norm = jax.vjp(norm_piece, tokens_wide, gain_self)
    grad_x_norm, grad_gain_self = pull_norm(grad_h1)
    grad_tokens = (grad_x1 + grad_x_norm).astype(BF)
    own_grads = jnp.concatenate(
        [
            tn(h1, dq).astype(BF),
            tn(h1, dk).astype(BF),
            tn(h1, dv).astype(BF),
            grad_wo.astype(BF),
            lanes_of(grad_gain_self, grad_gain_cross, grad_gain_ffn).astype(BF),
        ],
        axis=1,
    )
    own_sum = lax.psum_scatter(own_grads, ALL, scatter_dimension=0, tiled=True).astype(F32)
    cross_sum = cross_sum.astype(F32)
    sum_wgu = sum_wgu.astype(F32)

    def block(value, i):
        return value[:, i * width : (i + 1) * width]

    gain_sums = own_sum[:, 4 * width : 4 * width + 8]
    return (
        result[None],
        grad_tokens[None],
        grad_memory[None],
        block(own_sum, 0),
        block(own_sum, 1),
        block(own_sum, 2),
        block(own_sum, 3),
        gain_sums[:, 0],
        block(cross_sum, 0),
        block(cross_sum, 1),
        block(cross_sum, 2),
        block(cross_sum, 3),
        gain_sums[:, 1],
        gain_sums[:, 2],
        sum_wgu[None, :, :ff],
        sum_wgu[None, :, ff:],
        sum_wd.astype(F32)[None],
    )


def solution(mesh):
    rows = P(ALL, None, None)
    weight = P(ALL, None)
    gain = P(ALL)
    feeding = P("mode", "dp", None)
    return jax.shard_map(
        on_device,
        mesh=mesh,
        in_specs=(
            (rows,) * 3
            + (P(),) * 3
            + (weight,) * 4
            + (gain,)
            + (weight,) * 4
            + (gain,) * 2
            + (feeding,) * 3
        ),
        out_specs=(
            (rows,) * 3
            + (weight,) * 4
            + (gain,)
            + (weight,) * 4
            + (gain,) * 2
            + (feeding,) * 3
        ),
        check_vma=False,
    )
```

time: 1610 us -> 882 us (0.55)
  matrix products: 367 us -> 90.4 us
  waiting for transfers between devices: 771 us -> 523 us
  blocking collectives: 170 us -> 23.6 us
  other arithmetic: 136 us -> 28.6 us
  Pallas kernels: 0 us -> 76.1 us
  local copies, waits for them, and re-layouts: 97.1 us -> 48.8 us
  starting transfers between devices: 45.9 us -> 65.9 us
    reduce_scatter x11 -> x2, waiting for transfers between devices: 421 us -> 63.1 us  [the longest x1 63.1 us: on_device(): sum_wgu = lax.psum_scatter(grad_wgu, 'dp', scatter_dimension=0, tiled=True)]
    dot_general x61 -> x23, matrix products: 367 us -> 90.4 us  [the longest x10 36.1 us: tn(): lax.dot_general(left, right, (((0,), (0,)), ((), ())), preferred_element_...]
    unnamed x22 -> x10, waiting for transfers between devices: 7.1 us -> 161 us
    unnamed x2 -> x0, blocking collectives: 125 us -> none
    convert_element_type x20 -> x6, other arithmetic: 82.4 us -> 4.81 us  [the longest x1 1.78 us: on_device(): grad_x2_norm, grad_gain_ffn = pull_norm(grad_h3.astype(F32))]
    pallas_call x0 -> x9, Pallas kernels: none -> 76.1 us  [the longest x1 28.9 us: feed(): pl.pallas_call(functools.partial(feed_kernel, ff=ff, step=512), grid=(tok...]
    all_gather x11 -> x4, waiting for transfers between devices: 184 us -> 120 us  [the longest x2 120 us: gather_all(): lax.all_gather(jnp.concatenate(pieces, axis=1), ALL, axis=0, tiled=True)]
    reduce_sum x7 -> x3, other arithmetic: 33.1 us -> 2.04 us  [the longest x1 0.78 us: norm_piece(): value * lax.rsqrt(jnp.mean(value * value, axis=-1, keepdims=True) + EPS)]
  transfers between devices with their start and end apart: 33 -> 15, of which waited for: 18 -> 11; matrix products, arithmetic and copies ran while one was open for 34% -> 17% of each run, Pallas kernels for 0% -> 5%
where the time goes in v1:
time: 882 us; the launch traced here: 872 us
  waiting for transfers between devices  523 us (59%)
  matrix products  90.4 us (10%)
  Pallas kernels  76.1 us (9%)
  starting transfers between devices  65.9 us (7%)
  local copies, waits for them, and re-layouts  48.8 us (6%)
  other arithmetic  28.6 us (3%)
  blocking collectives  23.6 us (3%)
  between operations  15 us (2%)
    unnamed x10, waiting for transfers between devices  161 us
    all_gather x2, waiting for transfers between devices, gather_all(): lax.all_gather(jnp.concatenate(pieces, axis=1), ALL, axis=0, tiled=True)  120 us
    all_to_all x2, waiting for transfers between devices, from_modes(): dealt = lax.all_to_all(reorder(spread, target), ALL, 0, 0, tiled=True)  80.2 us
    reduce_scatter x1, waiting for transfers between devices, on_device(): sum_wgu = lax.psum_scatter(grad_wgu, 'dp', scatter_dimension=0, tiled=True)  63.1 us
    all_to_all x2, waiting for transfers between devices, to_modes(): spread = lax.all_to_all(dealt, ALL, 0, 0, tiled=True)  51.3 us
    all_to_all x2, starting transfers between devices, to_modes(): spread = lax.all_to_all(dealt, ALL, 0, 0, tiled=True)  48.4 us
    unnamed x89, local copies, waits for them, and re-layouts  41.7 us
    dot_general x10, matrix products, tn(): lax.dot_general(left, right, (((0,), (0,)), ((), ())), preferred_element_...  36.1 us
  transfers between devices with their start and end apart: 15, of which 11 were waited for; matrix products, arithmetic and copies ran while one was open for 17% of the time, Pallas kernels for 5%

profile of v1, /device:TPU:0, one launch (start us, length us, event | category | flops | bytes accessed | tf_op | source)
XLA Modules:
  0.0 871.8 jit_solution(9637402320073958274)
XLA Ops:
  19.1 7.3 all-to-all-start.2
  30.8 56.2 %all-gather.8.cloned.1.call-done = bf16[768,3072]{1,0:T(8,128)(2,1)} async-done(((bf16[24,3072]{1,0:T(8,128)(2,1)}), bf16[768,3072]{1,0:T(8,128)(2,1)}) %all-gather.8.cloned.1.call-update) | async-done | bytes 4718608 | tf_op jit(solution)/shard_map/all_gather | solution.py:323
  91.2 63.4 %all-gather.6.cloned.1.call-done = bf16[768,3328]{1,0:T(8,128)(2,1)} async-done(((bf16[24,3328]{1,0:T(8,128)(2,1)}), bf16[768,3328]{1,0:T(8,128)(2,1)}) %all-gather.6.cloned.1.call-update) | async-done | bytes 5111824 | tf_op jit(solution)/shard_map/all_gather | solution.py:323
  156.2 8.6 convolution_convert_fusion.1.q_ref.k_ref.v_ref
  164.8 9.0 %attend_causal.1 = (bf16[1024,768]{1,0:T(8,128)(2,1)}, f32[6,2,1024]{2,1,0:T(2,128)}) custom-call(s32[2]{0:T(128)} %pad_add_fusion.lens, bf16[1024,2304]{1,0:T(8,128)(2,1)} %convolution_convert_fusion.1.q_ref.k_ref.v_ref, bf16[1024,2304]{1,0:T(8,128)(2,1)} %convolution_convert_fusion.1.q_ref.k_ref.v_ref, ...), custom_call_target="tpu_custom_call" | custom-call | flops 6442450944 | bytes 6291456 | tf_op jit(solution)/shard_map/attend_causal/pallas_call | solution.py:149
  181.9 10.2 %attend_memory.1 = (bf16[1024,768]{1,0:T(8,128)(2,1)}, f32[6,2,1024]{2,1,0:T(2,128)}) custom-call(s32[2]{0:T(128)} %pad_add_fusion.lens, bf16[1024,768]{1,0:T(8,128)(2,1)} %convolution_convert_fusion.6.q_ref, bf16[512,1536]{1,0:T(8,128)(2,1)} %fusion.14.k_ref.v_ref, bf16[512,1536]{1,0:T(8,128)(2,1)} %fusion.14.k_ref.v_ref), custom_call_target="tpu_custom_call" | custom-call | flops 6442450944 | bytes 6291456 | tf_op jit(solution)/shard_map/attend_memory/pallas_call | solution.py:149
  198.4 41.1 %all-to-all-start = ((bf16[32,32,768]{2,1,0:T(8,128)(2,1)}), bf16[32,32,768]{2,1,0:T(8,128)(2,1)}, u32[]{:S(2)}, u32[]{:S(2)}) async-start(bf16[32,32,768]{2,1,0:T(8,128)(2,1)} %bitcast.118), calls=%async_computation | async-start | bytes 3145728 | tf_op jit(solution)/shard_map/all_to_all | solution.py:305
  241.8 51.3 %all-to-all-done.x_ref = bf16[32,32,768]{2,1,0:T(8,128)(2,1)} async-done(((bf16[32,32,768]{2,1,0:T(8,128)(2,1)}), bf16[32,32,768]{2,1,0:T(8,128)(2,1)}, u32[]{:S(2)}, u32[]{:S(2)}) %all-to-all-start) | async-done | bytes 1572896 | tf_op jit(solution)/shard_map/all_to_all | solution.py:305
  300.0 15.6 %all-to-all-done.3 = bf16[32,32,768]{2,1,0:T(8,128)(2,1)S(1)} async-done(((bf16[32,32,768]{2,1,0:T(8,128)(2,1)}), bf16[32,32,768]{2,1,0:T(8,128)(2,1)S(1)}, u32[]{:S(2)}, u32[]{:S(2)}) %all-to-all-start.3) | async-done | bytes 1572896 | tf_op jit(solution)/shard_map/all_to_all | solution.py:306
  320.4 18.6 %all-to-all-done.1 = bf16[32,32,768]{2,1,0:T(8,128)(2,1)S(1)} async-done(((bf16[32,32,768]{2,1,0:T(8,128)(2,1)}), bf16[32,32,768]{2,1,0:T(8,128)(2,1)S(1)}, u32[]{:S(2)}, u32[]{:S(2)}) %all-to-all-start.1) | async-done | bytes 1572896 | tf_op jit(solution)/shard_map/all_to_all | solution.py:306
  340.2 28.9 %feed.1 = (bf16[1024,768]{1,0:T(8,128)(2,1)}, bf16[1024,768]{1,0:T(8,128)(2,1)}, bf16[1024,2048]{1,0:T(8,128)(2,1)}, bf16[1024,4096]{1,0:T(8,128)(2,1)}) custom-call(bf16[1024,768]{1,0:T(8,128)(2,1)} %bitcast.121, bf16[1024,768]{1,0:T(8,128)(2,1)} %bitcast.123, bf16[768,4096]{1,0:T(8,128)(2,1)} %all-gather.10.cloned.1.call-done.gu_ref, ...), custom_call_target="tpu_custom_call" | custom-call | flops 19327352832 | bytes 41943040 | tf_op jit(solution)/shard_map/feed/pallas_call | solution.py:255
  369.0 23.6 %all_to_all.40.x_ref = bf16[32,32,768]{2,1,0:T(8,128)(2,1)} all-to-all(bf16[32,32,768]{2,1,0:T(8,128)(2,1)} %bitcast.126), channel_id=1, replica_groups=mesh['mode'=4,'dp'=8] {'mode'}, dimensions={0} | all-to-all | bytes 3145728 | tf_op jit(solution)/shard_map/all_to_all | solution.py:313
  399.6 13.9 %all-to-all-done.4.x_ref = bf16[32,32,768]{2,1,0:T(8,128)(2,1)S(1)} async-done(((bf16[32,32,768]{2,1,0:T(8,128)(2,1)}), bf16[32,32,768]{2,1,0:T(8,128)(2,1)S(1)}, u32[]{:S(2)}, u32[]{:S(2)}) %all-to-all-start.4) | async-done | bytes 1572896 | tf_op jit(solution)/shard_map/all_to_all | solution.py:313
  418.9 36.9 %all-to-all-done.7 = bf16[32,32,768]{2,1,0:T(8,128)(2,1)} async-done(((bf16[32,32,768]{2,1,0:T(8,128)(2,1)}), bf16[32,32,768]{2,1,0:T(8,128)(2,1)}, u32[]{:S(2)}, u32[]{:S(2)}) %all-to-all-start.7) | async-done | bytes 1572896 | tf_op jit(solution)/shard_map/all_to_all | solution.py:314
  458.7 7.9 convolution_convert_fusion.2
  471.1 43.3 %all-to-all-done.5 = bf16[32,32,768]{2,1,0:T(8,128)(2,1)S(1)} async-done(((bf16[32,32,768]{2,1,0:T(8,128)(2,1)}), bf16[32,32,768]{2,1,0:T(8,128)(2,1)S(1)}, u32[]{:S(2)}, u32[]{:S(2)}) %all-to-all-start.5) | async-done | bytes 1572896 | tf_op jit(solution)/shard_map/all_to_all | solution.py:314
  526.6 10.4 %attend_memory_back.1 = (bf16[1024,768]{1,0:T(8,128)(2,1)}, bf16[512,768]{1,0:T(8,128)(2,1)}, bf16[512,768]{1,0:T(8,128)(2,1)}) custom-call(s32[2]{0:T(128)} %pad_add_fusion.lens, bf16[1024,768]{1,0:T(8,128)(2,1)} %convolution_convert_fusion.6.q_ref, bf16[512,1536]{1,0:T(8,128)(2,1)} %fusion.14.k_ref.v_ref, bf16[512,1536]{1,0:T(8,128)(2,1)} %fusion.14.k_ref.v_ref, ...), custom_call_target="tpu_custom_call" | custom-call | flops 12079595520 | bytes 12582912 | tf_op jit(solution)/shard_map/attend_memory_back/pallas_call | solution.py:178
  546.5 6.7 copy.96
  563.2 10.7 %attend_causal_back.1 = (bf16[1024,768]{1,0:T(8,128)(2,1)}, bf16[1024,768]{1,0:T(8,128)(2,1)}, bf16[1024,768]{1,0:T(8,128)(2,1)}) custom-call(s32[2]{0:T(128)} %pad_add_fusion.lens, bf16[1024,2304]{1,0:T(8,128)(2,1)} %convolution_convert_fusion.1.q_ref.k_ref.v_ref, bf16[1024,2304]{1,0:T(8,128)(2,1)} %convolution_convert_fusion.1.q_ref.k_ref.v_ref, ...), custom_call_target="tpu_custom_call" | custom-call | flops 12079595520 | bytes 12582912 | tf_op jit(solution)/shard_map/attend_causal_back/pallas_call | solution.py:178
  596.3 7.7 copy.94
  604.1 11.6 %convolution_convert_fusion = bf16[768,4096]{1,0:T(8,128)(2,1)} fusion(bf16[1024,768]{1,0:T(8,128)(2,1)} %bitcast.122, bf16[1024,4096]{1,0:T(8,128)(2,1)} %get-tuple-element.43), kind=kOutput, calls=%fused_computation | convolution fusion | flops 6445596672 | bytes 16252928 | tf_op jit(solution)/shard_map/dot_general | solution.py:32
  626.2 50.2 %reduce-scatter.15.cloned.1.call-done = bf16[24,3072]{1,0:T(8,128)(2,1)} async-done(((bf16[768,3072]{1,0:T(8,128)(2,1)}), bf16[24,3072]{1,0:T(8,128)(2,1)}) %reduce-scatter.15.cloned.1.call-update) | async-done | bytes 147472
  680.9 110.0 %reduce-scatter.13.cloned.1.call-done = bf16[24,3328]{1,0:T(8,128)(2,1)} async-done(((bf16[768,3328]{1,0:T(8,128)(2,1)}), bf16[24,3328]{1,0:T(8,128)(2,1)}) %reduce-scatter.13.cloned.1.call-update) | async-done | bytes 159760
  799.1 63.1 %reduce-scatter.9.cloned.1.call-done = bf16[96,4096]{1,0:T(8,128)(2,1)} async-done(((bf16[768,4096]{1,0:T(8,128)(2,1)}), bf16[96,4096]{1,0:T(8,128)(2,1)}) %reduce-scatter.9.cloned.1.call-update) | async-done | bytes 786448 | tf_op jit(solution)/shard_map/reduce_scatter | solution.py:407
  (180 shorter events, 150.5 us)
Async XLA Ops:
  7.2 79.8 %copy-start = (bf16[1,512,768]{2,1,0:T(8,128)(2,1)S(1)}, bf16[1,512,768]{2,1,0:T(8,128)(2,1)}, u32[]{:S(2)}) copy-start(bf16[1,512,768]{2,1,0:T(8,128)(2,1)} %param.21) | copy-start | bytes 2359300
  7.2 9.2 %copy-start.27 = (s32[32]{0:T(128)S(1)}, s32[32]{0:T(128)}, u32[]{:S(2)}) copy-start(s32[32]{0:T(128)} %param.24) | copy-start | bytes 388
  7.2 10.5 %copy-start.18 = (bf16[1,1024,768]{2,1,0:T(8,128)(2,1)S(1)}, bf16[1,1024,768]{2,1,0:T(8,128)(2,1)}, u32[]{:S(2)}) copy-start(bf16[1,1024,768]{2,1,0:T(8,128)(2,1)} %param.22) | copy-start | bytes 4718596
  7.2 79.8 %all-gather.8.cloned.1.call-start = ((), (), s32[]{:S(2)}) async-start(), calls=%async_computation.13 | async-start | bytes 4866048 | tf_op jit(solution)/shard_map/all_gather | solution.py:323
  8.9 145.6 %all-gather.6.cloned.1.call-start = ((), (), s32[]{:S(2)}) async-start(), calls=%async_computation.12 | async-start | bytes 5271552 | tf_op jit(solution)/shard_map/all_gather | solution.py:323
  13.6 306.8 %all-gather.12.cloned.1.call-start = ((), (), s32[]{:S(2)}) async-start(), calls=%async_computation.17 | async-start | bytes 3538944 | tf_op jit(solution)/shard_map/all_gather | solution.py:378
  14.3 306.1 %all-gather.10.cloned.1.call-start = ((), (), s32[]{:S(2)}) async-start(), calls=%async_computation.14 | async-start | bytes 7077888 | tf_op jit(solution)/shard_map/all_gather | solution.py:375
  19.1 179.2 %all-to-all-start.2 = ((bf16[32,32,768]{2,1,0:T(8,128)(2,1)}), bf16[32,32,768]{2,1,0:T(8,128)(2,1)S(1)}, u32[]{:S(2)}, u32[]{:S(2)}) async-start(bf16[32,32,768]{2,1,0:T(8,128)(2,1)} %fusion.17), calls=%async_computation.2 | async-start | bytes 3145728 | tf_op jit(solution)/shard_map/all_to_all | solution.py:305
  30.7 60.5 %copy-start.25 = (f32[1024]{0:T(1024)}, f32[1024]{0:T(1024)S(1)}, u32[]{:S(2)}) copy-start(f32[1024]{0:T(1024)S(1)} %fusion.9) | copy-start | bytes 12292
  177.1 15.1 %copy-start.13 = (f32[1024,768]{1,0:T(8,128)}, f32[1024,768]{1,0:T(8,128)S(1)}, u32[]{:S(2)}) copy-start(f32[1024,768]{1,0:T(8,128)S(1)} %get-tuple-element.138) | copy-start | bytes 9437188
  197.0 42.4 %copy-start.29 = (s32[32]{0:T(128)S(1)}, s32[32]{0:T(128)}, u32[]{:S(2)}) copy-start(s32[32]{0:T(128)} %param.23) | copy-start | bytes 388
  198.4 94.7 %all-to-all-start = ((bf16[32,32,768]{2,1,0:T(8,128)(2,1)}), bf16[32,32,768]{2,1,0:T(8,128)(2,1)}, u32[]{:S(2)}, u32[]{:S(2)}) async-start(bf16[32,32,768]{2,1,0:T(8,128)(2,1)} %bitcast.118), calls=%async_computation | async-start | bytes 3145728 | tf_op jit(solution)/shard_map/all_to_all | solution.py:305
  293.1 22.5 %all-to-all-start.3 = ((bf16[32,32,768]{2,1,0:T(8,128)(2,1)}), bf16[32,32,768]{2,1,0:T(8,128)(2,1)S(1)}, u32[]{:S(2)}, u32[]{:S(2)}) async-start(bf16[32,32,768]{2,1,0:T(8,128)(2,1)} %copy-done.2), calls=%async_computation.3 | async-start | bytes 3145728 | tf_op jit(solution)/shard_map/all_to_all | solution.py:306
  316.8 22.2 %all-to-all-start.1 = ((bf16[32,32,768]{2,1,0:T(8,128)(2,1)}), bf16[32,32,768]{2,1,0:T(8,128)(2,1)S(1)}, u32[]{:S(2)}, u32[]{:S(2)}) async-start(bf16[32,32,768]{2,1,0:T(8,128)(2,1)} %reorder.4), calls=%async_computation.1 | async-start | bytes 3145728 | tf_op jit(solution)/shard_map/all_to_all | solution.py:306
  392.7 20.8 %all-to-all-start.4 = ((bf16[32,32,768]{2,1,0:T(8,128)(2,1)}), bf16[32,32,768]{2,1,0:T(8,128)(2,1)S(1)}, u32[]{:S(2)}, u32[]{:S(2)}) async-start(bf16[32,32,768]{2,1,0:T(8,128)(2,1)} %bitcast.125), calls=%async_computation.4 | async-start | bytes 3145728 | tf_op jit(solution)/shard_map/all_to_all | solution.py:313
  413.5 42.3 %all-to-all-start.7 = ((bf16[32,32,768]{2,1,0:T(8,128)(2,1)}), bf16[32,32,768]{2,1,0:T(8,128)(2,1)}, u32[]{:S(2)}, u32[]{:S(2)}) async-start(bf16[32,32,768]{2,1,0:T(8,128)(2,1)} %copy-done.3), calls=%async_computation.7 | async-start | bytes 3145728 | tf_op jit(solution)/shard_map/all_to_all | solution.py:314
  455.8 58.6 %all-to-all-start.5 = ((bf16[32,32,768]{2,1,0:T(8,128)(2,1)}), bf16[32,32,768]{2,1,0:T(8,128)(2,1)S(1)}, u32[]{:S(2)}, u32[]{:S(2)}) async-start(bf16[32,32,768]{2,1,0:T(8,128)(2,1)} %reorder.6), calls=%async_computation.5 | async-start | bytes 3145728 | tf_op jit(solution)/shard_map/all_to_all | solution.py:314
  458.5 165.8 %reduce-scatter.11.cloned.1.call-start = ((), (), s32[]{:S(2)}) async-start(), calls=%async_computation.16 | async-start | bytes 3538944 | tf_op jit(solution)/shard_map/reduce_scatter | solution.py:408
  466.6 209.9 %reduce-scatter.15.cloned.1.call-start = ((), (), s32[]{:S(2)}) async-start(), calls=%async_computation.19 | async-start | bytes 4866048
  521.8 18.2 %copy-start.16 = (f32[1024,768]{1,0:T(8,128)}, f32[1024,768]{1,0:T(8,128)S(1)}, u32[]{:S(2)}) copy-start(f32[1024,768]{1,0:T(8,128)S(1)} %get-tuple-element.122) | copy-start | bytes 9437188
  553.2 237.8 %reduce-scatter.13.cloned.1.call-start = ((), (), s32[]{:S(2)}) async-start(), calls=%async_computation.18 | async-start | bytes 5271552
  558.4 34.7 %copy-start.10 = (f32[1024,768]{1,0:T(8,128)}, f32[1024,768]{1,0:T(8,128)S(1)}, u32[]{:S(2)}) copy-start(f32[1024,768]{1,0:T(8,128)S(1)} %fusion.6) | copy-start | bytes 9437188
  604.1 258.2 %reduce-scatter.9.cloned.1.call-start = ((), (), s32[]{:S(2)}) async-start(), calls=%async_computation.15 | async-start | bytes 7077888 | tf_op jit(solution)/shard_map/reduce_scatter | solution.py:407
  795.0 69.8 %copy-start.1 = (bf16[1,512,768]{2,1,0:T(8,128)(2,1)S(1)}, bf16[1,512,768]{2,1,0:T(8,128)(2,1)}, u32[]{:S(2)}) copy-start(bf16[1,512,768]{2,1,0:T(8,128)(2,1)} %param.21) | copy-start | bytes 2359300
  (27 other events, 74.7 us)
Sparse Core Ops, SparseCore 0:
  11.7 75.3 all-gather.7
  90.6 63.9 all-gather.5
  156.2 37.1 all-gather.11
  195.5 85.3 all-gather.9
  466.7 57.6 reduce-scatter.10
  553.3 123.0 reduce-scatter.14
  682.9 108.0 reduce-scatter.12
  793.3 68.9 reduce-scatter.8

commit v2 on v1

--- a/solution.py
+++ b/solution.py
@@ -164,7 +164,7 @@
         ],
         compiler_params=pltpu.CompilerParams(vmem_limit_bytes=VMEM),
         cost_estimate=pl.CostEstimate(
-            flops=pixels * 4 * HEAD_DIM * 4, bytes_accessed=8 * length * 768, transcendentals=pixels
+            flops=32 * 10**9, bytes_accessed=8 * length * 768, transcendentals=pixels
         ),
         name="attend_causal" if causal else "attend_memory",
     )(lens, qa, ka, va)
@@ -202,7 +202,7 @@
         ],
         compiler_params=pltpu.CompilerParams(vmem_limit_bytes=VMEM),
         cost_estimate=pl.CostEstimate(
-            flops=pixels * 10 * HEAD_DIM * 3, bytes_accessed=16 * length * 768, transcendentals=pixels
+            flops=40 * 10**9, bytes_accessed=16 * length * 768, transcendentals=pixels
         ),
         name="attend_causal_back" if causal else "attend_memory_back",
     )(lens, qa, ka, va, mixed, grad, lse)
@@ -306,12 +306,16 @@
     return lax.all_to_all(reorder(spread, source), "mode", 0, 0, tiled=True).reshape(tokens, width)
 
 
-def from_modes(value, target):
+def from_modes(value, target, late=None, later=None):
     count = lax.axis_size(ALL)
     tokens, width = value.shape
     piece = tokens // count
     spread = lax.all_to_all(value.reshape(count, piece, width), "mode", 0, 0, tiled=True)
+    if late is not None:
+        spread = tied(spread, late)
     dealt = lax.all_to_all(reorder(spread, target), ALL, 0, 0, tiled=True)
+    if later is not None:
+        dealt = tied(dealt, later)
     return dealt.reshape(count, piece // 8, 8, width).swapaxes(0, 1).reshape(tokens, width)
 
 
@@ -319,13 +323,116 @@
     return value * lax.rsqrt(jnp.mean(value * value, axis=-1, keepdims=True) + EPS) * gain
 
 
-def gather_all(*pieces):
-    return lax.all_gather(jnp.concatenate(pieces, axis=1), ALL, axis=0, tiled=True)
+def swap(value, j):
+    count = lax.axis_size(ALL)
+    return lax.ppermute(value, ALL, [(i, i ^ j) for i in range(count)])
+
+
+def device_number():
+    return lax.axis_index(ALL).astype(jnp.int32)[None]
+
+
+def place_kernel(me, even_ref, odd_ref, o_ref):
+    for t in range(even_ref.shape[0]):
+        o_ref[jnp.bitwise_xor(2 * t, me[0])] = even_ref[t]
+        o_ref[jnp.bitwise_xor(2 * t + 1, me[0])] = odd_ref[t]
+
+
+def place(even, odd):
+    count, rows, width = even.shape
+    step = width
+
+    def block(n):
+        return pl.BlockSpec((n, rows, step), lambda i, me: (0, 0, i))
+
+    return pl.pallas_call(
+        place_kernel,
+        grid_spec=pltpu.PrefetchScalarGridSpec(
+            num_scalar_prefetch=1,
+            grid=(width // step,),
+            in_specs=[block(count)] * 2,
+            out_specs=block(2 * count),
+        ),
+        out_shape=jax.ShapeDtypeStruct((2 * count, rows, width), even.dtype),
+        compiler_params=pltpu.CompilerParams(vmem_limit_bytes=24 * 2**20),
+        cost_estimate=pl.CostEstimate(
+            flops=0, bytes_accessed=8 * even.size, transcendentals=0
+        ),
+        name="place",
+    )(device_number(), even, odd)
+
+
+def gather_all(piece):
+    per_mode, modes = lax.axis_size("dp"), lax.axis_size("mode")
+    column = jnp.stack([piece] + [swap(piece, 2 * j) for j in range(1, per_mode // 2)])
+    plane = jnp.stack([column] + [swap(column, per_mode * j) for j in range(1, modes)])
+    plane = plane.reshape((-1,) + piece.shape)
+    return place(plane, swap(plane, 1)).reshape(-1, piece.shape[1])
+
+
+def take_kernel(parts, me, *refs):
+    ins, (keep_ref, send_ref) = refs[:parts], refs[parts:]
+    first = 0
+    for in_ref in ins:
+        at = pl.ds(first, in_ref.shape[2])
+        first += in_ref.shape[2]
+        for t in range(keep_ref.shape[0]):
+            keep_ref[t, :, at] = in_ref[jnp.bitwise_xor(2 * t, me[0])]
+            send_ref[t, :, at] = in_ref[jnp.bitwise_xor(2 * t + 1, me[0])]
+
+
+def take(parts):
+    count, rows = parts[0].shape[:2]
+    width = sum(part.shape[2] for part in parts)
+    half = jax.ShapeDtypeStruct((count // 2, rows, width), parts[0].dtype)
+
+    def whole(shape):
+        return pl.BlockSpec(shape, lambda i, me: (0, 0, 0))
+
+    return pl.pallas_call(
+        functools.partial(take_kernel, len(parts)),
+        grid_spec=pltpu.PrefetchScalarGridSpec(
+            num_scalar_prefetch=1,
+            grid=(1,),
+            in_specs=[whole(part.shape) for part in parts],
+            out_specs=[whole(half.shape)] * 2,
+        ),
+        out_shape=[half, half],
+        compiler_params=pltpu.CompilerParams(vmem_limit_bytes=48 * 2**20),
+        cost_estimate=pl.CostEstimate(
+            flops=0, bytes_accessed=8 * half.size, transcendentals=0
+        ),
+        name="take",
+    )(device_number(), *parts)
+
+
+def add_up(parts):
+    return functools.reduce(jnp.add, [part.astype(F32) for part in parts])
+
+
+def scatter_pairs(parts):
+    count = lax.axis_size(ALL)
+    parts = [part.reshape(count, part.shape[0] // count, part.shape[1]) for part in parts]
+    keep, send = take(parts)
+    return add_up([keep, swap(send, 1)]).astype(BF)
+
+
+def scatter_chips(plane):
+    per_mode, modes = lax.axis_size("dp"), lax.axis_size("mode")
+    plane = plane.reshape((modes, per_mode // 2) + plane.shape[1:])
+    column = add_up(
+        [plane[0]] + [swap(plane[j], per_mode * j) for j in range(1, modes)]
+    ).astype(BF)
+    return add_up([column[0]] + [swap(column[j], 2 * j) for j in range(1, per_mode // 2)])
+
+
+def tied(first, second):
+    return lax.optimization_barrier((first, second))[0]
 
 
 def lanes_of(*vectors):
     columns_ = jnp.stack(vectors, axis=1)
-    return jnp.pad(columns_, ((0, 0), (0, 256 - len(vectors))))
+    return jnp.pad(columns_, ((0, 0), (0, 128 - len(vectors))))
 
 
 def on_device(
@@ -370,16 +477,24 @@
     valid = (jnp.arange(tokens.shape[0], dtype=jnp.int32) < live_len)[:, None]
     grad_low = jnp.where(valid, incoming, jnp.zeros_like(incoming))
 
-    own = gather_all(self_q, self_k, self_v, self_o, lanes_of(self_gain, cross_gain, ffn_gain))
-    crossing = gather_all(cross_q, cross_k, cross_v, cross_o)
+    crossing = lax.all_gather(
+        jnp.concatenate([cross_q, cross_k, cross_v, cross_o], axis=1), ALL, axis=0, tiled=True
+    )
+    own = gather_all(
+        jnp.concatenate(
+            [self_q, self_k, self_v, lanes_of(self_gain, cross_gain, ffn_gain)], axis=1
+        )
+    )
+    wo = gather_all(tied(self_o, own))
+    feeding = (ffn_gate, ffn_up, ffn_down)
     wgu = lax.all_gather(
-        jnp.concatenate([ffn_gate[0], ffn_up[0]], axis=1), "dp", axis=0, tiled=True
-    )
-    wd = lax.all_gather(ffn_down[0], "dp", axis=0, tiled=True)
-    routed_grad = to_modes(grad_low, source)
-
-    wqkv, wo = own[:, : 3 * width], own[:, 3 * width : 4 * width]
-    gains = own[:, 4 * width : 4 * width + 8].astype(F32)
+        jnp.concatenate([feeding[0][0], feeding[1][0]], axis=1), "dp", axis=0, tiled=True
+    )
+    wd = lax.all_gather(feeding[2][0], "dp", axis=0, tiled=True)
+    routed_grad = to_modes(tied(grad_low, own), source)
+
+    wqkv = own[:, : 3 * width]
+    gains = own[:, 3 * width : 3 * width + 8].astype(F32)
     gain_self, gain_cross, gain_ffn = gains[:, 0], gains[:, 1], gains[:, 2]
     tokens_wide = tokens.astype(F32)
     h1 = norm_piece(tokens_wide, gain_self).astype(BF)
@@ -395,18 +510,18 @@
     cross_kv = nn(memory_row, ckv).astype(BF)
     cross_in = ((cross_query, 0), (cross_kv, 0), (cross_kv, pairs))
     cross_mixed, log_cross = attend_forward(*cross_in, lens, False)
+    cross_mixed, routed_grad = lax.optimization_barrier((cross_mixed, routed_grad))
     x2 = x1 + nn(cross_mixed, co)
     h3 = norm_piece(x2, gain_ffn).astype(BF)
 
     routed_h = to_modes(h3, source)
     routed_y, routed_dh, hidden, dgu = feed(routed_h, routed_grad, wgu, wd)
-    grad_h3 = from_modes(routed_dh, target)
-    y = from_modes(routed_y, target)
     grad_wgu = tn(routed_h, dgu).astype(BF)
     grad_wd = tn(hidden, routed_grad).astype(BF)
     sum_wgu = lax.psum_scatter(grad_wgu, "dp", scatter_dimension=0, tiled=True)
     sum_wd = lax.psum_scatter(grad_wd, "dp", scatter_dimension=0, tiled=True)
-    result = jnp.where(valid, x2 + y.astype(F32), 0.0).astype(BF)
+    grad_h3 = from_modes(routed_dh, target)
+    grad_h3 = tied(grad_h3, (grad_wgu, grad_wd))
 
     unused, pull_norm = jax.vjp(norm_piece, x2, gain_ffn)
     grad_x2_norm, grad_gain_ffn = pull_norm(grad_h3.astype(F32))
@@ -424,39 +539,37 @@
     unused, pull_norm = jax.vjp(norm_piece, x1, gain_cross)
     grad_x1_norm, grad_gain_cross = pull_norm(nt(dcq, cq))
     grad_x1 = grad_x2 + grad_x1_norm
-    cross_grads = jnp.concatenate(
-        [grad_cq.astype(BF), grad_ck.astype(BF), grad_cv.astype(BF), grad_co.astype(BF)], axis=1
-    )
-    cross_sum = lax.psum_scatter(cross_grads, ALL, scatter_dimension=0, tiled=True)
-
     grad_one = grad_x1.astype(BF)
     grad_wo = tn(mixed, grad_one)
     grad_mixed = nt(grad_one, wo).astype(BF)
+    cross_pair = scatter_pairs(
+        [part.astype(BF) for part in (grad_cq, grad_ck, grad_cv, grad_co, grad_wo)]
+    )
+    grad_mixed, cross_pair = lax.optimization_barrier((grad_mixed, cross_pair))
+    cross_sum = scatter_chips(cross_pair)
     dq, dk, dv = attend_backward(*self_in, mixed, grad_mixed, log_self, lens, True)
+    y = from_modes(tied(routed_y, grad_h3), target, dcq, dq)
+    result = jnp.where(valid, x2 + y.astype(F32), 0.0).astype(BF)
     grad_h1 = (
         nt(dq, wqkv[:, :width]) + nt(dk, wqkv[:, width : 2 * width]) + nt(dv, wqkv[:, 2 * width :])
     )
     unused, pull_norm = jax.vjp(norm_piece, tokens_wide, gain_self)
     grad_x_norm, grad_gain_self = pull_norm(grad_h1)
     grad_tokens = (grad_x1 + grad_x_norm).astype(BF)
-    own_grads = jnp.concatenate(
+    own_sum = scatter_chips(scatter_pairs(
         [
             tn(h1, dq).astype(BF),
             tn(h1, dk).astype(BF),
             tn(h1, dv).astype(BF),
-            grad_wo.astype(BF),
             lanes_of(grad_gain_self, grad_gain_cross, grad_gain_ffn).astype(BF),
-        ],
-        axis=1,
-    )
-    own_sum = lax.psum_scatter(own_grads, ALL, scatter_dimension=0, tiled=True).astype(F32)
-    cross_sum = cross_sum.astype(F32)
+        ]
+    ))
     sum_wgu = sum_wgu.astype(F32)
 
     def block(value, i):
         return value[:, i * width : (i + 1) * width]
 
-    gain_sums = own_sum[:, 4 * width : 4 * width + 8]
+    gain_sums = own_sum[:, 3 * width : 3 * width + 8]
     return (
         result[None],
         grad_tokens[None],
@@ -464,7 +577,7 @@
         block(own_sum, 0),
         block(own_sum, 1),
         block(own_sum, 2),
-        block(own_sum, 3),
+        block(cross_sum, 4),
         gain_sums[:, 0],
         block(cross_sum, 0),
         block(cross_sum, 1),

time: 882 us -> 638 us (0.72)
  waiting for transfers between devices: 523 us -> 177 us
  Pallas kernels: 76.1 us -> 165 us
  blocking collectives: 23.6 us -> 75.5 us
  local copies, waits for them, and re-layouts: 48.8 us -> 19.9 us
    unnamed x10 -> x5, waiting for transfers between devices: 161 us -> 1.28 us
    all_gather x4 -> x3, waiting for transfers between devices: 120 us -> 0.06 us  [the longest x1 0.02 us: on_device(): lax.all_gather(jnp.concatenate([cross_q, cross_k, cross_v, cross_o], axis...]
    ppermute x0 -> x28, waiting for transfers between devices: none -> 102 us  [swap(): return lax.ppermute(value, ALL, [(i, i ^ j) for i in range(count)])]
    reduce_scatter x1, waiting for transfers between devices: 63.1 us -> 0.01 us  [on_device(): sum_wgu = lax.psum_scatter(grad_wgu, 'dp', scatter_dimension=0, tiled=True)]
    all_to_all x0 -> x1, blocking collectives: none -> 52.7 us  [to_modes(): spread = lax.all_to_all(dealt, ALL, 0, 0, tiled=True)]
    pallas_call x2, Pallas kernels: 21.1 us -> 66.6 us  [attend_backward(): pl.pallas_call(functools.partial(attend_bwd_kernel, causal), grid_spec=pl...]
    all_to_all x2 -> x1, waiting for transfers between devices: 51.3 us -> 7.1 us  [to_modes(): spread = lax.all_to_all(dealt, ALL, 0, 0, tiled=True)]
    all_to_all x2, waiting for transfers between devices: 80.2 us -> 36.5 us  [from_modes(): dealt = lax.all_to_all(reorder(spread, target), ALL, 0, 0, tiled=True)]
  transfers between devices with their start and end apart: 15 -> 39, of which waited for: 11 -> 23; matrix products, arithmetic and copies ran while one was open for 17% -> 19% of each run, Pallas kernels for 5% -> 21%
where the time goes in v2:
time: 638 us; the launch traced here: 632 us
  waiting for transfers between devices  177 us (28%)
  Pallas kernels  165 us (26%)
  matrix products  83 us (13%)
  blocking collectives  75.5 us (12%)
  starting transfers between devices  66.3 us (10%)
  other arithmetic  31 us (5%)
  local copies, waits for them, and re-layouts  19.9 us (3%)
  between operations  14.9 us (2%)
    ppermute x28, waiting for transfers between devices, swap(): return lax.ppermute(value, ALL, [(i, i ^ j) for i in range(count)])  102 us
    pallas_call x2, Pallas kernels, attend_backward(): pl.pallas_call(functools.partial(attend_bwd_kernel, causal), grid_spec=pl...  66.6 us
    pallas_call x2, Pallas kernels, attend_forward(): pl.pallas_call(functools.partial(attend_fwd_kernel, causal), grid_spec=pl...  56.1 us
    all_to_all x1, blocking collectives, to_modes(): spread = lax.all_to_all(dealt, ALL, 0, 0, tiled=True)  52.7 us
    all_to_all x2, waiting for transfers between devices, from_modes(): dealt = lax.all_to_all(reorder(spread, target), ALL, 0, 0, tiled=True)  36.5 us
    ppermute x28, starting transfers between devices, swap(): return lax.ppermute(value, ALL, [(i, i ^ j) for i in range(count)])  34.2 us
    dot_general x10, matrix products, tn(): lax.dot_general(left, right, (((0,), (0,)), ((), ())), preferred_element_...  32.2 us
    pallas_call x1, Pallas kernels, feed(): pl.pallas_call(functools.partial(feed_kernel, ff=ff, step=512), grid=(tok...  28.8 us
  transfers between devices with their start and end apart: 39, of which 23 were waited for; matrix products, arithmetic and copies ran while one was open for 19% of the time, Pallas kernels for 21%

profile of v2, /device:TPU:0, one launch (start us, length us, event | category | flops | bytes accessed | tf_op | source)
XLA Modules:
  0.0 632.3 jit_solution(6902445787736977891)
XLA Ops:
  28.4 9.8 %collective-permute-done.4 = bf16[4,24,2432]{2,1,0:T(8,128)(2,1)S(1)} collective-permute-done((bf16[4,24,2432]{2,1,0:T(8,128)(2,1)S(1)}, bf16[4,24,2432]{2,1,0:T(8,128)(2,1)S(1)}, u32[]{:S(2)}, u32[]{:S(2)}) %collective-permute-start.4) | collective-permute-done | bytes 466976 | tf_op jit(solution)/shard_map/ppermute | solution.py:328
  40.1 11.9 %collective-permute-done.5 = bf16[4,24,2432]{2,1,0:T(8,128)(2,1)S(1)} collective-permute-done((bf16[4,24,2432]{2,1,0:T(8,128)(2,1)S(1)}, bf16[4,24,2432]{2,1,0:T(8,128)(2,1)S(1)}, u32[]{:S(2)}, u32[]{:S(2)}) %collective-permute-start.5) | collective-permute-done | bytes 466976 | tf_op jit(solution)/shard_map/ppermute | solution.py:328
  70.3 5.2 all-to-all-start
  79.5 8.6 %convolution_convert_fusion.1.q_ref.k_ref.v_ref = bf16[1024,2304]{1,0:T(8,128)(2,1)} fusion(bf16[768,2432]{1,0:T(8,128)(2,1)} %bitcast.160, bf16[1,1024,768]{2,1,0:T(8,128)(2,1)} %param.20, f32[768]{0:T(1024)S(1)} %get-tuple-element.84, f32[1024]{0:T(1024)S(1)} %fusion.51), kind=kOutput, calls=%fused_computation.7 | convolution fusion | flops 3629383680 | bytes 9837568 | tf_op jit(solution)/shard_map/dot_general | solution.py:28
  88.1 5.0 collective-permute-done.11
  97.3 28.0 %attend_causal.1 = (bf16[1024,768]{1,0:T(8,128)(2,1)}, f32[6,2,1024]{2,1,0:T(2,128)}) custom-call(s32[2]{0:T(128)} %pad_add_fusion.lens, bf16[1024,2304]{1,0:T(8,128)(2,1)} %convolution_convert_fusion.1.q_ref.k_ref.v_ref, bf16[1024,2304]{1,0:T(8,128)(2,1)} %convolution_convert_fusion.1.q_ref.k_ref.v_ref, ...), custom_call_target="tpu_custom_call" | custom-call | flops 32000000000 | bytes 6291456 | tf_op jit(solution)/shard_map/attend_causal/pallas_call | solution.py:149
  131.7 7.1 %all-to-all-done.x_ref = bf16[32,32,768]{2,1,0:T(8,128)(2,1)S(1)} async-done(((bf16[32,32,768]{2,1,0:T(8,128)(2,1)}), bf16[32,32,768]{2,1,0:T(8,128)(2,1)S(1)}, u32[]{:S(2)}, u32[]{:S(2)}) %all-to-all-start) | async-done | bytes 1572896 | tf_op jit(solution)/shard_map/all_to_all | solution.py:305
  153.0 28.1 %attend_memory.1 = (bf16[1024,768]{1,0:T(8,128)(2,1)}, f32[6,2,1024]{2,1,0:T(2,128)}) custom-call(s32[2]{0:T(128)} %pad_add_fusion.lens, bf16[1024,768]{1,0:T(8,128)(2,1)} %convolution_convert_fusion.6.q_ref, bf16[512,1536]{1,0:T(8,128)(2,1)} %fusion.17.k_ref.v_ref, bf16[512,1536]{1,0:T(8,128)(2,1)} %fusion.17.k_ref.v_ref), custom_call_target="tpu_custom_call" | custom-call | flops 32000000000 | bytes 6291456 | tf_op jit(solution)/shard_map/attend_memory/pallas_call | solution.py:149
  187.8 52.7 %all_to_all.40.x_ref = bf16[32,32,768]{2,1,0:T(8,128)(2,1)S(1)} all-to-all(bf16[32,32,768]{2,1,0:T(8,128)(2,1)S(1)} %bitcast.182), channel_id=1, replica_groups=mesh['mode'=4,'dp'=8] {'mode','dp'}, dimensions={0} | all-to-all | bytes 3145728 | tf_op jit(solution)/shard_map/all_to_all | solution.py:305
  246.1 18.5 %all-to-all-done.3 = bf16[32,32,768]{2,1,0:T(8,128)(2,1)S(1)} async-done(((bf16[32,32,768]{2,1,0:T(8,128)(2,1)}), bf16[32,32,768]{2,1,0:T(8,128)(2,1)S(1)}, u32[]{:S(2)}, u32[]{:S(2)}) %all-to-all-start.3) | async-done | bytes 1572896 | tf_op jit(solution)/shard_map/all_to_all | solution.py:306
  265.8 28.8 %feed.1 = (bf16[1024,768]{1,0:T(8,128)(2,1)}, bf16[1024,768]{1,0:T(8,128)(2,1)}, bf16[1024,2048]{1,0:T(8,128)(2,1)}, bf16[1024,4096]{1,0:T(8,128)(2,1)}) custom-call(bf16[1024,768]{1,0:T(8,128)(2,1)} %bitcast.187, bf16[1024,768]{1,0:T(8,128)(2,1)} %bitcast.185, bf16[768,4096]{1,0:T(8,128)(2,1)} %all-gather.7.cloned.1.call-done.gu_ref, ...), custom_call_target="tpu_custom_call" | custom-call | flops 19327352832 | bytes 41943040 | tf_op jit(solution)/shard_map/feed/pallas_call | solution.py:255
  294.6 22.8 %all_to_all.41.x_ref = bf16[32,32,768]{2,1,0:T(8,128)(2,1)S(1)} all-to-all(bf16[32,32,768]{2,1,0:T(8,128)(2,1)} %bitcast.189), channel_id=1, replica_groups=mesh['mode'=4,'dp'=8] {'mode'}, dimensions={0} | all-to-all | bytes 3145728 | tf_op jit(solution)/shard_map/all_to_all | solution.py:313
  319.4 12.4 %all-to-all-start.5 = ((bf16[32,32,768]{2,1,0:T(8,128)(2,1)}), bf16[32,32,768]{2,1,0:T(8,128)(2,1)S(1)}, u32[]{:S(2)}, u32[]{:S(2)}) async-start(bf16[32,32,768]{2,1,0:T(8,128)(2,1)} %reorder.6), calls=%async_computation.5 | async-start | bytes 3145728 | tf_op jit(solution)/shard_map/all_to_all | solution.py:316
  331.9 7.9 %convolution_convert_fusion.2 = bf16[2048,768]{1,0:T(8,128)(2,1)} fusion(bf16[1024,2048]{1,0:T(8,128)(2,1)} %get-tuple-element.54, bf16[1024,768]{1,0:T(8,128)(2,1)} %bitcast.186), kind=kOutput, calls=%fused_computation.19 | convolution fusion | flops 3222798336 | bytes 8912896 | tf_op jit(solution)/shard_map/dot_general | solution.py:32
  339.8 11.4 %convolution_convert_fusion = bf16[768,4096]{1,0:T(8,128)(2,1)} fusion(bf16[1024,768]{1,0:T(8,128)(2,1)} %bitcast.188, bf16[1024,4096]{1,0:T(8,128)(2,1)} %get-tuple-element.53), kind=kOutput, calls=%fused_computation | convolution fusion | flops 6445596672 | bytes 16252928 | tf_op jit(solution)/shard_map/dot_general | solution.py:32
  351.2 36.5 %all-to-all-done.5 = bf16[32,32,768]{2,1,0:T(8,128)(2,1)S(1)} async-done(((bf16[32,32,768]{2,1,0:T(8,128)(2,1)}), bf16[32,32,768]{2,1,0:T(8,128)(2,1)S(1)}, u32[]{:S(2)}, u32[]{:S(2)}) %all-to-all-start.5) | async-done | bytes 1572896 | tf_op jit(solution)/shard_map/all_to_all | solution.py:316
  397.2 28.9 %attend_memory_back.1 = (bf16[1024,768]{1,0:T(8,128)(2,1)}, bf16[512,768]{1,0:T(8,128)(2,1)}, bf16[512,768]{1,0:T(8,128)(2,1)}) custom-call(s32[2]{0:T(128)} %pad_add_fusion.lens, bf16[1024,768]{1,0:T(8,128)(2,1)} %convolution_convert_fusion.6.q_ref, bf16[512,1536]{1,0:T(8,128)(2,1)} %fusion.17.k_ref.v_ref, bf16[512,1536]{1,0:T(8,128)(2,1)} %fusion.17.k_ref.v_ref, ...), custom_call_target="tpu_custom_call" | custom-call | flops 40000000000 | bytes 12582912 | tf_op jit(solution)/shard_map/attend_memory_back/pallas_call | solution.py:178
  455.2 11.2 %all-to-all-done.6.x_ref = bf16[32,32,768]{2,1,0:T(8,128)(2,1)S(1)} async-done(((bf16[32,32,768]{2,1,0:T(8,128)(2,1)}), bf16[32,32,768]{2,1,0:T(8,128)(2,1)S(1)}, u32[]{:S(2)}, u32[]{:S(2)}) %all-to-all-start.6) | async-done | bytes 1572896 | tf_op jit(solution)/shard_map/all_to_all | solution.py:313
  477.2 37.7 %attend_causal_back.1 = (bf16[1024,768]{1,0:T(8,128)(2,1)}, bf16[1024,768]{1,0:T(8,128)(2,1)}, bf16[1024,768]{1,0:T(8,128)(2,1)}) custom-call(s32[2]{0:T(128)} %pad_add_fusion.lens, bf16[1024,2304]{1,0:T(8,128)(2,1)} %convolution_convert_fusion.1.q_ref.k_ref.v_ref, bf16[1024,2304]{1,0:T(8,128)(2,1)} %convolution_convert_fusion.1.q_ref.k_ref.v_ref, ...), custom_call_target="tpu_custom_call" | custom-call | flops 40000000000 | bytes 12582912 | tf_op jit(solution)/shard_map/attend_causal_back/pallas_call | solution.py:178
  536.8 8.7 %collective-permute-done.22 = bf16[4,24,3840]{2,1,0:T(8,128)(2,1)} collective-permute-done((bf16[4,24,3840]{2,1,0:T(8,128)(2,1)}, bf16[4,24,3840]{2,1,0:T(8,128)(2,1)}, u32[]{:S(2)}, u32[]{:S(2)}) %collective-permute-start.22) | collective-permute-done | bytes 737312 | tf_op jit(solution)/shard_map/ppermute | solution.py:328
  545.5 12.7 %collective-permute-done.24 = bf16[4,24,3840]{2,1,0:T(8,128)(2,1)} collective-permute-done((bf16[4,24,3840]{2,1,0:T(8,128)(2,1)}, bf16[4,24,3840]{2,1,0:T(8,128)(2,1)}, u32[]{:S(2)}, u32[]{:S(2)}) %collective-permute-start.24) | collective-permute-done | bytes 737312 | tf_op jit(solution)/shard_map/ppermute | solution.py:328
  577.3 7.2 %collective-permute-done.26 = bf16[24,3840]{1,0:T(8,128)(2,1)S(1)} collective-permute-done((bf16[24,3840]{1,0:T(8,128)(2,1)S(1)}, bf16[24,3840]{1,0:T(8,128)(2,1)S(1)}, u32[]{:S(2)}, u32[]{:S(2)}) %collective-permute-start.26) | collective-permute-done | bytes 184352 | tf_op jit(solution)/shard_map/ppermute | solution.py:328
  592.4 7.6 %collective-permute-done.16 = bf16[4,24,2432]{2,1,0:T(8,128)(2,1)S(1)} collective-permute-done((bf16[4,24,2432]{2,1,0:T(8,128)(2,1)}, bf16[4,24,2432]{2,1,0:T(8,128)(2,1)S(1)}, u32[]{:S(2)}, u32[]{:S(2)}) %collective-permute-start.16) | collective-permute-done | bytes 466976 | tf_op jit(solution)/shard_map/ppermute | solution.py:328
  599.9 8.1 %collective-permute-done.18 = bf16[4,24,2432]{2,1,0:T(8,128)(2,1)} collective-permute-done((bf16[4,24,2432]{2,1,0:T(8,128)(2,1)}, bf16[4,24,2432]{2,1,0:T(8,128)(2,1)}, u32[]{:S(2)}, u32[]{:S(2)}) %collective-permute-start.18) | collective-permute-done | bytes 466976 | tf_op jit(solution)/shard_map/ppermute | solution.py:328
  (249 shorter events, 200.4 us)
Async XLA Ops:
  7.2 137.4 %all-gather.5.cloned.1.call-start = ((), (), s32[]{:S(2)}) async-start(), calls=%async_computation.10 | async-start | bytes 4866048 | tf_op jit(solution)/shard_map/all_gather | solution.py:480
  8.8 237.3 %all-gather.9.cloned.1.call-start = ((), (), s32[]{:S(2)}) async-start(), calls=%async_computation.14 | async-start | bytes 3538944 | tf_op jit(solution)/shard_map/all_gather | solution.py:493
  9.6 236.5 %all-gather.7.cloned.1.call-start = ((), (), s32[]{:S(2)}) async-start(), calls=%async_computation.11 | async-start | bytes 7077888 | tf_op jit(solution)/shard_map/all_gather | solution.py:490
  27.9 24.0 %collective-permute-start.5 = (bf16[4,24,2432]{2,1,0:T(8,128)(2,1)S(1)}, bf16[4,24,2432]{2,1,0:T(8,128)(2,1)S(1)}, u32[]{:S(2)}, u32[]{:S(2)}) collective-permute-start(bf16[4,24,2432]{2,1,0:T(8,128)(2,1)S(1)} %get-tuple-element.100), channel_id=1, source_target_pairs={{0,24},{1,25},{2,26},{3,27},{4,28},{5,29},{6,30},{7,31},{8,16},{9,... | collective-permute-start | bytes 1400840 | tf_op jit(solution)/shard_map/ppermute | solution.py:328
  70.3 68.5 %all-to-all-start = ((bf16[32,32,768]{2,1,0:T(8,128)(2,1)}), bf16[32,32,768]{2,1,0:T(8,128)(2,1)S(1)}, u32[]{:S(2)}, u32[]{:S(2)}) async-start(bf16[32,32,768]{2,1,0:T(8,128)(2,1)} %bitcast.179), calls=%async_computation | async-start | bytes 3145728 | tf_op jit(solution)/shard_map/all_to_all | solution.py:305
  75.9 17.2 %collective-permute-start.11 = (bf16[4,24,768]{2,1,0:T(8,128)(2,1)S(1)}, bf16[4,24,768]{2,1,0:T(8,128)(2,1)S(1)}, u32[]{:S(2)}, u32[]{:S(2)}) collective-permute-start(bf16[4,24,768]{2,1,0:T(8,128)(2,1)S(1)} %get-tuple-element.110), channel_id=1, source_target_pairs={{0,16},{1,17},{2,18},{3,19},{4,20},{5,21},{6,22},{7,23},{8,24},{9,... | collective-permute-start | bytes 442376 | tf_op jit(solution)/shard_map/ppermute | solution.py:328
  77.5 15.6 %collective-permute-start.10 = (bf16[4,24,768]{2,1,0:T(8,128)(2,1)S(1)}, bf16[4,24,768]{2,1,0:T(8,128)(2,1)S(1)}, u32[]{:S(2)}, u32[]{:S(2)}) collective-permute-start(bf16[4,24,768]{2,1,0:T(8,128)(2,1)S(1)} %get-tuple-element.110), channel_id=1, source_target_pairs={{0,8},{1,9},{2,10},{3,11},{4,12},{5,13},{6,14},{7,15},{8,0},{9,1},... | collective-permute-start | bytes 442376 | tf_op jit(solution)/shard_map/ppermute | solution.py:328
  79.0 18.1 %collective-permute-start.12 = (bf16[4,24,768]{2,1,0:T(8,128)(2,1)S(1)}, bf16[4,24,768]{2,1,0:T(8,128)(2,1)S(1)}, u32[]{:S(2)}, u32[]{:S(2)}) collective-permute-start(bf16[4,24,768]{2,1,0:T(8,128)(2,1)S(1)} %get-tuple-element.110), channel_id=1, source_target_pairs={{0,24},{1,25},{2,26},{3,27},{4,28},{5,29},{6,30},{7,31},{8,16},{9,... | collective-permute-start | bytes 442376 | tf_op jit(solution)/shard_map/ppermute | solution.py:328
  97.2 28.1 %collective-permute-start.13 = (bf16[16,24,768]{2,1,0:T(8,128)(2,1)S(1)}, bf16[16,24,768]{2,1,0:T(8,128)(2,1)S(1)}, u32[]{:S(2)}, u32[]{:S(2)}) collective-permute-start(bf16[16,24,768]{2,1,0:T(8,128)(2,1)S(1)} %bitcast.164), channel_id=1, source_target_pairs={{0,1},{1,0},{2,3},{3,2},{4,5},{5,4},{6,7},{7,6},{8,9},{9,8},{10,11... | collective-permute-start | bytes 1769480 | tf_op jit(solution)/shard_map/ppermute | solution.py:328
  140.8 40.4 %all-to-all-start.1 = ((bf16[32,32,768]{2,1,0:T(8,128)(2,1)}), bf16[32,32,768]{2,1,0:T(8,128)(2,1)S(1)}, u32[]{:S(2)}, u32[]{:S(2)}) async-start(bf16[32,32,768]{2,1,0:T(8,128)(2,1)} %copy-done.3), calls=%async_computation.1 | async-start | bytes 3145728 | tf_op jit(solution)/shard_map/all_to_all | solution.py:306
  242.5 22.1 %all-to-all-start.3 = ((bf16[32,32,768]{2,1,0:T(8,128)(2,1)}), bf16[32,32,768]{2,1,0:T(8,128)(2,1)S(1)}, u32[]{:S(2)}, u32[]{:S(2)}) async-start(bf16[32,32,768]{2,1,0:T(8,128)(2,1)} %reorder.5), calls=%async_computation.3 | async-start | bytes 3145728 | tf_op jit(solution)/shard_map/all_to_all | solution.py:306
  319.4 68.4 %all-to-all-start.5 = ((bf16[32,32,768]{2,1,0:T(8,128)(2,1)}), bf16[32,32,768]{2,1,0:T(8,128)(2,1)S(1)}, u32[]{:S(2)}, u32[]{:S(2)}) async-start(bf16[32,32,768]{2,1,0:T(8,128)(2,1)} %reorder.6), calls=%async_computation.5 | async-start | bytes 3145728 | tf_op jit(solution)/shard_map/all_to_all | solution.py:316
  331.8 140.0 %reduce-scatter.5.cloned.1.call-start = ((), (), s32[]{:S(2)}) async-start(), calls=%async_computation.13 | async-start | bytes 3538944 | tf_op jit(solution)/shard_map/reduce_scatter | solution.py:522
  442.7 31.1 %collective-permute-start.14 = (bf16[16,24,3840]{2,1,0:T(8,128)(2,1)}, bf16[16,24,3840]{2,1,0:T(8,128)(2,1)}, u32[]{:S(2)}, u32[]{:S(2)}) collective-permute-start(bf16[16,24,3840]{2,1,0:T(8,128)(2,1)} %get-tuple-element.63), channel_id=1, source_target_pairs={{0,1},{1,0},{2,3},{3,2},{4,5},{5,4},{6,7},{7,6},{8,9},{9,8},{10,11... | collective-permute-start | bytes 8847368 | tf_op jit(solution)/shard_map/ppermute | solution.py:328
  442.8 23.6 %all-to-all-start.6 = ((bf16[32,32,768]{2,1,0:T(8,128)(2,1)}), bf16[32,32,768]{2,1,0:T(8,128)(2,1)S(1)}, u32[]{:S(2)}, u32[]{:S(2)}) async-start(bf16[32,32,768]{2,1,0:T(8,128)(2,1)} %bitcast.184), calls=%async_computation.6 | async-start | bytes 3145728 | tf_op jit(solution)/shard_map/all_to_all | solution.py:313
  446.4 176.7 %reduce-scatter.3.cloned.1.call-start = ((), (), s32[]{:S(2)}) async-start(), calls=%async_computation.12 | async-start | bytes 7077888 | tf_op jit(solution)/shard_map/reduce_scatter | solution.py:521
  468.3 122.0 %all-to-all-start.7 = ((bf16[32,32,768]{2,1,0:T(8,128)(2,1)}), bf16[32,32,768]{2,1,0:T(8,128)(2,1)}, u32[]{:S(2)}, u32[]{:S(2)}) async-start(bf16[32,32,768]{2,1,0:T(8,128)(2,1)} %reorder.7), calls=%async_computation.7 | async-start | bytes 3145728 | tf_op jit(solution)/shard_map/all_to_all | solution.py:316
  524.8 20.7 %collective-permute-start.22 = (bf16[4,24,3840]{2,1,0:T(8,128)(2,1)}, bf16[4,24,3840]{2,1,0:T(8,128)(2,1)}, u32[]{:S(2)}, u32[]{:S(2)}) collective-permute-start(bf16[4,24,3840]{2,1,0:T(8,128)(2,1)} %get-tuple-element.85), channel_id=1, source_target_pairs={{0,8},{1,9},{2,10},{3,11},{4,12},{5,13},{6,14},{7,15},{8,0},{9,1},... | collective-permute-start | bytes 2211848 | tf_op jit(solution)/shard_map/ppermute | solution.py:328
  524.8 33.5 %collective-permute-start.24 = (bf16[4,24,3840]{2,1,0:T(8,128)(2,1)}, bf16[4,24,3840]{2,1,0:T(8,128)(2,1)}, u32[]{:S(2)}, u32[]{:S(2)}) collective-permute-start(bf16[4,24,3840]{2,1,0:T(8,128)(2,1)} %get-tuple-element.86), channel_id=1, source_target_pairs={{0,24},{1,25},{2,26},{3,27},{4,28},{5,29},{6,30},{7,31},{8,16},{9,... | collective-permute-start | bytes 2211848 | tf_op jit(solution)/shard_map/ppermute | solution.py:328
  524.8 37.7 %collective-permute-start.23 = (bf16[4,24,3840]{2,1,0:T(8,128)(2,1)}, bf16[4,24,3840]{2,1,0:T(8,128)(2,1)}, u32[]{:S(2)}, u32[]{:S(2)}) collective-permute-start(bf16[4,24,3840]{2,1,0:T(8,128)(2,1)} %get-tuple-element.87), channel_id=1, source_target_pairs={{0,16},{1,17},{2,18},{3,19},{4,20},{5,21},{6,22},{7,23},{8,24},{9,... | collective-permute-start | bytes 2211848 | tf_op jit(solution)/shard_map/ppermute | solution.py:328
  536.8 47.7 %collective-permute-start.15 = (bf16[16,24,2432]{2,1,0:T(8,128)(2,1)}, bf16[16,24,2432]{2,1,0:T(8,128)(2,1)S(1)}, u32[]{:S(2)}, u32[]{:S(2)}) collective-permute-start(bf16[16,24,2432]{2,1,0:T(8,128)(2,1)} %get-tuple-element.71), channel_id=1, source_target_pairs={{0,1},{1,0},{2,3},{3,2},{4,5},{5,4},{6,7},{7,6},{8,9},{9,8},{10,11... | collective-permute-start | bytes 5603336 | tf_op jit(solution)/shard_map/ppermute | solution.py:328
  567.8 16.6 %collective-permute-start.26 = (bf16[24,3840]{1,0:T(8,128)(2,1)S(1)}, bf16[24,3840]{1,0:T(8,128)(2,1)S(1)}, u32[]{:S(2)}, u32[]{:S(2)}) collective-permute-start(bf16[24,3840]{1,0:T(8,128)(2,1)S(1)} %get-tuple-element.95), channel_id=1, source_target_pairs={{0,4},{1,5},{2,6},{3,7},{4,0},{5,1},{6,2},{7,3},{8,12},{9,13},{10,... | collective-permute-start | bytes 552968 | tf_op jit(solution)/shard_map/ppermute | solution.py:328
  586.7 21.4 %collective-permute-start.18 = (bf16[4,24,2432]{2,1,0:T(8,128)(2,1)}, bf16[4,24,2432]{2,1,0:T(8,128)(2,1)}, u32[]{:S(2)}, u32[]{:S(2)}) collective-permute-start(bf16[4,24,2432]{2,1,0:T(8,128)(2,1)} %get-tuple-element.89), channel_id=1, source_target_pairs={{0,24},{1,25},{2,26},{3,27},{4,28},{5,29},{6,30},{7,31},{8,16},{9,... | collective-permute-start | bytes 1400840 | tf_op jit(solution)/shard_map/ppermute | solution.py:328
  587.8 21.6 %collective-permute-start.17 = (bf16[4,24,2432]{2,1,0:T(8,128)(2,1)}, bf16[4,24,2432]{2,1,0:T(8,128)(2,1)}, u32[]{:S(2)}, u32[]{:S(2)}) collective-permute-start(bf16[4,24,2432]{2,1,0:T(8,128)(2,1)} %get-tuple-element.90), channel_id=1, source_target_pairs={{0,16},{1,17},{2,18},{3,19},{4,20},{5,21},{6,22},{7,23},{8,24},{9,... | collective-permute-start | bytes 1400840 | tf_op jit(solution)/shard_map/ppermute | solution.py:328
  (60 other events, 695.7 us)
Sparse Core Ops, SparseCore 0:
  11.6 70.8 all-gather.4
  84.2 56.4 all-gather.8
  143.0 79.8 all-gather.6
  339.9 57.6 reduce-scatter.4
  449.2 92.6 reduce-scatter.2

commit v3 on v2

v3 whole, which is shorter than its diff:
```python
import functools

import jax
import jax.numpy as jnp
from jax import lax
from jax.experimental import pallas as pl
from jax.experimental.pallas import tpu as pltpu
from jax.sharding import PartitionSpec as P

HEADS = 12
HEAD_DIM = 64
PAIR = 2 * HEAD_DIM
EPS = 1e-06
NEG = -1e30
SCALE = HEAD_DIM ** -0.5
QB = 256
ALL = ("mode", "dp")
BF = jnp.bfloat16
F32 = jnp.float32
VMEM = 56 * 2**20
BRIEF = pl.CostEstimate(flops=10**6, bytes_accessed=10**4, transcendentals=0)


def nt(left, right):
    return lax.dot_general(left, right, (((1,), (1,)), ((), ())), preferred_element_type=F32)


def nn(left, right):
    return jnp.dot(left, right, preferred_element_type=F32)


def tn(left, right):
    return lax.dot_general(left, right, (((0,), (0,)), ((), ())), preferred_element_type=F32)


def head_lanes(value, h):
    lane = lax.broadcasted_iota(jnp.int32, value.shape, 1)
    return jnp.where((lane >= HEAD_DIM) == (h == 1), value, jnp.zeros_like(value))


def masks(causal, key_count, qb, limit):
    if causal:
        parts = []
        if qb:
            parts.append((0, qb * QB, None))
        row = lax.broadcasted_iota(jnp.int32, (QB, QB), 0)
        col = lax.broadcasted_iota(jnp.int32, (QB, QB), 1)
        parts.append((qb * QB, QB, row <= col))
        return parts
    row = lax.broadcasted_iota(jnp.int32, (key_count, QB), 0)
    return [(0, key_count, row < limit)]


def attend_fwd_kernel(causal, start, lens, q_ref, k_ref, v_ref, o_ref, lse_ref, vt):
    live, limit = lens[0], lens[1]
    length, key_count = q_ref.shape[0], k_ref.shape[0]
    vt[...] = jnp.swapaxes(v_ref[...].astype(F32), 0, 1).astype(BF)
    for block in range(length // QB):
        at = pl.ds(block * QB, QB)
        qb = start // QB + block

        @pl.when(qb * QB < live)
        def _(qb=qb, at=at):
            query = q_ref[at, :] * jnp.asarray(SCALE, BF)
            parts = masks(causal, key_count, qb, limit)
            outs = []
            for h in range(2):
                mine = head_lanes(query, h)
                scores = []
                for first, count, mask in parts:
                    s = nt(k_ref[pl.ds(first, count), :], mine)
                    scores.append(s if mask is None else jnp.where(mask, s, NEG))
                top = functools.reduce(
                    jnp.maximum, [jnp.max(s, axis=0, keepdims=True) for s in scores]
                )
                total, mixed = 0.0, 0.0
                for (first, count, _), s in zip(parts, scores):
                    p = jnp.exp(s - top)
                    total = total + jnp.sum(p, axis=0, keepdims=True)
                    mixed = mixed + nn(
                        vt[pl.ds(h * HEAD_DIM, HEAD_DIM), pl.ds(first, count)], p.astype(BF)
                    )
                outs.append(mixed / total)
                lse_ref[0, pl.ds(h, 1), at] = top + jnp.log(total)
            o_ref[at, :] = jnp.swapaxes(jnp.concatenate(outs, axis=0), 0, 1).astype(BF)

        @pl.when(qb * QB >= live)
        def _(at=at):
            o_ref[at, :] = jnp.zeros((QB, PAIR), BF)
            lse_ref[0, pl.ds(0, 2), at] = jnp.zeros((2, QB), F32)


def attend_bwd_kernel(causal, start, carried, lens, *refs):
    q_ref, k_ref, v_ref, o_ref, do_ref, lse_ref = refs[:6]
    more, (dq_ref, dk_ref, dv_ref, kt, dk, dv) = refs[6:-6], refs[-6:]
    live, limit = lens[0], lens[1]
    length, key_count = q_ref.shape[0], k_ref.shape[0]
    kt[...] = jnp.swapaxes(k_ref[...].astype(F32), 0, 1).astype(BF)
    if carried < key_count:
        fresh = pl.ds(carried, key_count - carried)
        dk[fresh, :] = jnp.zeros((key_count - carried, PAIR), F32)
        dv[fresh, :] = jnp.zeros((key_count - carried, PAIR), F32)
    if carried:
        dk[pl.ds(0, carried), :] = more[0][...]
        dv[pl.ds(0, carried), :] = more[1][...]
    for block in range(length // QB):
        at = pl.ds(block * QB, QB)
        qb = start // QB + block

        @pl.when(qb * QB < live)
        def _(qb=qb, at=at):
            query = q_ref[at, :] * jnp.asarray(SCALE, BF)
            grad = do_ref[at, :]
            inner = jnp.swapaxes(o_ref[at, :].astype(F32) * grad.astype(F32), 0, 1)
            parts = masks(causal, key_count, qb, limit)
            sums = [[0.0, 0.0] for _ in parts]
            outs = []
            for h in range(2):
                mine = head_lanes(query, h)
                grad_mine = head_lanes(grad, h)
                lse = lse_ref[0, pl.ds(h, 1), at]
                delta = jnp.sum(inner[h * HEAD_DIM : (h + 1) * HEAD_DIM], axis=0, keepdims=True)
                grad_query = 0.0
                for i, (first, count, mask) in enumerate(parts):
                    keys = pl.ds(first, count)
                    p = jnp.exp(nt(k_ref[keys, :], mine) - lse)
                    if mask is not None:
                        p = jnp.where(mask, p, 0.0)
                    dp = nt(v_ref[keys, :], grad_mine)
                    ds = (p * (dp - delta)).astype(BF)
                    sums[i][0] = sums[i][0] + nn(ds, mine)
                    sums[i][1] = sums[i][1] + nn(p.astype(BF), grad_mine)
                    grad_query = grad_query + nn(kt[pl.ds(h * HEAD_DIM, HEAD_DIM), keys], ds)
                outs.append(grad_query * SCALE)
            for (first, count, _), (sum_k, sum_v) in zip(parts, sums):
                dk[pl.ds(first, count), :] += sum_k
                dv[pl.ds(first, count), :] += sum_v
            dq_ref[at, :] = jnp.swapaxes(jnp.concatenate(outs, axis=0), 0, 1).astype(BF)

        @pl.when(qb * QB >= live)
        def _(at=at):
            dq_ref[at, :] = jnp.zeros((QB, PAIR), BF)

    dk_ref[...] = dk[...].astype(dk_ref.dtype)
    dv_ref[...] = dv[...].astype(dv_ref.dtype)


def columns(rows, first, row_block=0):
    at = first if callable(first) else lambda g: first + g
    return pl.BlockSpec((rows, PAIR), lambda g, lens: (row_block, at(g)))


def attend_forward(query, keys, values, lens, causal, start, length, key_count, pairs):
    (qa, q0, rows), (ka, k0), (va, v0) = query, keys, values
    return pl.pallas_call(
        functools.partial(attend_fwd_kernel, causal, start),
        grid_spec=pltpu.PrefetchScalarGridSpec(
            num_scalar_prefetch=1,
            grid=(pairs,),
            in_specs=[
                columns(length, q0, rows),
                columns(key_count, k0),
                columns(key_count, v0),
            ],
            out_specs=[
                columns(length, 0),
                pl.BlockSpec((1, 2, length), lambda g, lens: (g, 0, 0)),
            ],
            scratch_shapes=[pltpu.VMEM((PAIR, key_count), BF)],
        ),
        out_shape=[
            jax.ShapeDtypeStruct((length, pairs * PAIR), BF),
            jax.ShapeDtypeStruct((pairs, 2, length), F32),
        ],
        compiler_params=pltpu.CompilerParams(vmem_limit_bytes=24 * 2**20),
        cost_estimate=BRIEF,
        name="attend_causal" if causal else "attend_memory",
    )(lens, qa, ka, va)


def attend_backward(
    query, keys, values, mixed, grad, lse, lens, causal, start, length, key_count, pairs, carried, last
):
    (qa, q0, rows), (ka, k0), (va, v0) = query, keys, values
    had = carried[0].shape[0] if carried else 0
    kept = BF if last else F32
    return pl.pallas_call(
        functools.partial(attend_bwd_kernel, causal, start, had),
        grid_spec=pltpu.PrefetchScalarGridSpec(
            num_scalar_prefetch=1,
            grid=(pairs,),
            in_specs=[
                columns(length, q0, rows),
                columns(key_count, k0),
                columns(key_count, v0),
                columns(length, mixed[1]),
                columns(length, grad[1]),
                pl.BlockSpec((1, 2, length), lambda g, lens: (mixed[1] + g, 0, 0)),
            ]
            + [columns(had, 0)] * (2 if carried else 0),
            out_specs=[columns(length, 0), columns(key_count, 0), columns(key_count, 0)],
            scratch_shapes=[
                pltpu.VMEM((PAIR, key_count), BF),
                pltpu.VMEM((key_count, PAIR), F32),
                pltpu.VMEM((key_count, PAIR), F32),
            ],
        ),
        out_shape=[
            jax.ShapeDtypeStruct((length, pairs * PAIR), BF),
            jax.ShapeDtypeStruct((key_count, pairs * PAIR), kept),
            jax.ShapeDtypeStruct((key_count, pairs * PAIR), kept),
        ],
        compiler_params=pltpu.CompilerParams(vmem_limit_bytes=32 * 2**20),
        cost_estimate=BRIEF,
        name="attend_causal_back" if causal else "attend_memory_back",
    )(lens, qa, ka, va, mixed[0], grad[0], lse, *(carried or ()))


def normed(value, gain):
    scale = lax.rsqrt(jnp.mean(value * value, axis=-1, keepdims=True) + EPS)
    return value * scale * gain


def norm_back(value, gain, grad):
    scale = lax.rsqrt(jnp.mean(value * value, axis=-1, keepdims=True) + EPS)
    unit = value * scale
    scaled = grad * gain
    inner = jnp.mean(scaled * unit, axis=-1, keepdims=True)
    return scale * (scaled - unit * inner), jnp.sum(grad * unit, axis=0, keepdims=True)


def enter_kernel(x_ref, w0_ref, w1_ref, columns_ref, h_ref, qkv_ref, gain_ref):
    rows = jnp.swapaxes(columns_ref[...].astype(F32), 0, 1)
    gain_ref[...] = rows[:8]
    h = normed(x_ref[...].astype(F32), rows[0:1]).astype(BF)
    h_ref[...] = h
    wide = w0_ref.shape[1]
    qkv_ref[:, pl.ds(0, wide)] = nn(h, w0_ref[...]).astype(BF)
    qkv_ref[:, pl.ds(wide, wide)] = nn(h, w1_ref[...]).astype(BF)


def middle_kernel(x_ref, o_ref, gain_ref, wo_ref, cq_ref, x1_ref, h_ref, q_ref):
    x1 = x_ref[...].astype(F32) + nn(o_ref[...], wo_ref[...])
    h = normed(x1, gain_ref[1:2]).astype(BF)
    x1_ref[...] = x1
    h_ref[...] = h
    q_ref[...] = nn(h, cq_ref[...]).astype(BF)


def outer_kernel(x1_ref, o_ref, gain_ref, co_ref, x2_ref, h_ref):
    x2 = x1_ref[...] + nn(o_ref[...], co_ref[...])
    x2_ref[...] = x2
    h_ref[...] = normed(x2, gain_ref[2:3]).astype(BF)


def add_gain(step, ref, value):
    @pl.when(step == 0)
    def _():
        ref[...] = jnp.zeros_like(ref)

    ref[0:1, :] += value


def outer_back_kernel(dh_ref, x2_ref, g_ref, gain_ref, co_ref, d_ref, dx_ref, do_ref, dgain_ref):
    dx, dgain = norm_back(x2_ref[...], gain_ref[2:3], dh_ref[...].astype(F32))
    dx = g_ref[...].astype(F32) + dx
    d = dx.astype(BF)
    dx_ref[...] = dx
    d_ref[...] = d
    do_ref[...] = nt(d, co_ref[...]).astype(BF)
    add_gain(pl.program_id(0), dgain_ref, dgain)


def middle_back_kernel(
    dq_ref, x1_ref, dx2_ref, gain_ref, cq_ref, wo_ref, dx_ref, d_ref, do_ref, dgain_ref
):
    dx, dgain = norm_back(x1_ref[...], gain_ref[1:2], nt(dq_ref[...], cq_ref[...]))
    dx = dx2_ref[...] + dx
    d = dx.astype(BF)
    dx_ref[...] = dx
    d_ref[...] = d
    do_ref[...] = nt(d, wo_ref[...]).astype(BF)
    add_gain(pl.program_id(0), dgain_ref, dgain)


def enter_back_kernel(x_ref, dx1_ref, *refs):
    grads, gain_ref, weights, (out_ref, dgain_ref) = refs[:3], refs[3], refs[4:10], refs[10:]
    dh = 0.0
    for i, grad in enumerate(grads):
        for g in range(2):
            w = weights[2 * i + g]
            at = pl.ds(g * w.shape[1], w.shape[1])
            dh = dh + nt(grad[:, at], w[...])
    dx, dgain = norm_back(x_ref[...].astype(F32), gain_ref[0:1], dh)
    out_ref[...] = (dx1_ref[...] + dx).astype(BF)
    add_gain(pl.program_id(0), dgain_ref, dgain)


def by_tokens(kernel, tokens, blocked, whole, outs, name, c=0, kept=None):
    width = blocked[0][0].shape[1]
    steps = tokens // QB
    full = tokens if kept is None else 2 * tokens

    def rows(n, first):
        return pl.BlockSpec((QB, n), lambda i, first=first: (first + i, 0))

    def fixed(shape, index):
        return pl.BlockSpec(shape, lambda i, index=index: index)

    kept = kept or ()
    inputs = len(blocked) + len(whole)

    def run(*refs):
        kernel(*refs[:inputs], *refs[inputs + len(kept) :])

    return pl.pallas_call(
        run,
        grid=(steps,),
        in_specs=[rows(a.shape[1], first) for a, first in blocked]
        + [fixed(shape, index) for _, shape, index in whole]
        + [pl.BlockSpec(memory_space=pl.ANY)] * len(kept),
        out_specs=[
            fixed((8, width), (0, 0)) if n is None else rows(n, c * steps) for n, _ in outs
        ],
        out_shape=[
            jax.ShapeDtypeStruct((8, width) if n is None else (full, n), dtype)
            for n, dtype in outs
        ],
        input_output_aliases={inputs + i: i for i in range(len(kept))},
        compiler_params=pltpu.CompilerParams(vmem_limit_bytes=24 * 2**20),
        cost_estimate=BRIEF,
        name=name,
    )(*[a for a, _ in blocked], *[a for a, _, _ in whole], *kept)


def weight_grad_kernel(x_ref, g_ref, o_ref):
    o_ref[...] = tn(x_ref[...], g_ref[...]).astype(BF)


def weight_grad(x, grad, columns_at_once):
    tokens, rows = x.shape
    width = grad.shape[1]
    return pl.pallas_call(
        weight_grad_kernel,
        grid=(rows // columns_at_once,),
        in_specs=[
            pl.BlockSpec((tokens, columns_at_once), lambda i: (0, i)),
            pl.BlockSpec((tokens, width), lambda i: (0, 0)),
        ],
        out_specs=pl.BlockSpec((columns_at_once, width), lambda i: (i, 0)),
        out_shape=jax.ShapeDtypeStruct((rows, width), BF),
        compiler_params=pltpu.CompilerParams(vmem_limit_bytes=40 * 2**20),
        cost_estimate=BRIEF,
        name="weight_grad",
    )(x, grad)


GELU_A = 0.7978845608028654
GELU_B = 0.044715


def feed_kernel(groups, ff, step, *refs):
    h_refs, g_refs, (gu_ref, down_ref) = refs[:groups], refs[groups : 2 * groups], refs[2 * groups : 2 * groups + 2]
    outs = refs[-2 * groups - 4 :]
    y_refs, dh_refs, (hid_ref, dgu_ref, h_ref, g_ref) = outs[:groups], outs[groups:-4], outs[-4:]
    part = h_refs[0].shape[0]
    for j in range(groups):
        h_ref[pl.ds(j * part, part), :] = h_refs[j][...]
        g_ref[pl.ds(j * part, part), :] = g_refs[j][0]
    y, dh = 0.0, 0.0
    for c in range(0, ff, step):
        wg = gu_ref[:, pl.ds(c, step)]
        wu = gu_ref[:, pl.ds(ff + c, step)]
        wd = down_ref[pl.ds(c, step), :]
        gate, up, dhid = nn(h_ref[...], wg), nn(h_ref[...], wu), nt(g_ref[...], wd)
        square = gate * gate
        th = jnp.tanh(gate * (GELU_A + (GELU_A * GELU_B) * square))
        half = 0.5 + 0.5 * th
        act = gate * half
        slope = half + (0.5 * gate) * (1.0 - th * th) * (
            GELU_A + (3.0 * GELU_A * GELU_B) * square
        )
        hidden = (act * up).astype(BF)
        dgate = (dhid * up * slope).astype(BF)
        dup = (dhid * act).astype(BF)
        hid_ref[:, pl.ds(c, step)] = hidden
        dgu_ref[:, pl.ds(c, step)] = dgate
        dgu_ref[:, pl.ds(ff + c, step)] = dup
        y = y + nn(hidden, wd)
        dh = dh + nt(dgate, wg) + nt(dup, wu)
    for j in range(groups):
        y_refs[j][0] = y[j * part : (j + 1) * part].astype(BF)
        dh_refs[j][...] = dh[j * part : (j + 1) * part].astype(BF)


def feed(c, h_parts, g_parts, wgu, wd, kept):
    groups = len(h_parts)
    part, width = h_parts[0].shape
    ff = wd.shape[0]
    tokens = groups * part

    def whole(a):
        return pl.BlockSpec(a.shape, lambda i: (0,) * a.ndim)

    def halves(n):
        return pl.BlockSpec((tokens, n), lambda i: (c, 0))

    wide = (ff, 2 * ff, width, width)
    of_half = pl.BlockSpec((1, part, width), lambda i: (c, 0, 0))
    made = [0 + i for i in range(groups)] + [2 * groups + i for i in range(len(wide))]
    return pl.pallas_call(
        functools.partial(feed_kernel, groups, ff, 512),
        grid=(1,),
        in_specs=[whole(h) for h in h_parts]
        + [of_half] * groups
        + [whole(wgu), whole(wd)]
        + [pl.BlockSpec(memory_space=pl.ANY)] * len(kept),
        out_specs=[of_half] * groups
        + [whole(h) for h in h_parts]
        + [halves(n) for n in wide],
        out_shape=[jax.ShapeDtypeStruct((2, part, width), BF)] * groups
        + [jax.ShapeDtypeStruct((part, width), BF)] * groups
        + [jax.ShapeDtypeStruct((2 * tokens, n), BF) for n in wide],
        input_output_aliases={2 * groups + 2 + i: made[i] for i in range(len(kept))},
        compiler_params=pltpu.CompilerParams(vmem_limit_bytes=VMEM),
        cost_estimate=BRIEF,
        name="feed",
    )(*h_parts, *g_parts, wgu, wd, *kept)


def pick_kernel(modes, halves, source, mode, x_ref, *o_refs):
    per_mode = x_ref.shape[0] // modes
    for j in range(modes):
        first = jnp.bitwise_xor(mode[0], j) * per_mode

        def move(r, carry, j=j, first=first):
            row = source[first + r]
            if halves:
                for c in range(halves):
                    o_refs[j][c, r] = x_ref[row, c]
            else:
                o_refs[j][r] = x_ref[row]
            return carry

        lax.fori_loop(0, per_mode, move, 0)


def put_kernel(modes, halves, source, mode, *refs):
    o_ref = refs[-1]
    per_mode = o_ref.shape[0] // modes
    for j in range(modes):
        first = jnp.bitwise_xor(mode[0], j) * per_mode

        def move(r, carry, j=j, first=first):
            row = source[first + r]
            if halves:
                for c in range(halves):
                    o_ref[row, c] = refs[j][c, r]
            else:
                o_ref[row] = refs[j][r]
            return carry

        lax.fori_loop(0, per_mode, move, 0)


def mode_number():
    return lax.axis_index("mode").astype(jnp.int32)[None]


def by_rows(kernel, source, ins, outs, name):
    def whole(shape):
        return pl.BlockSpec(shape, lambda i, source, mode: (0,) * len(shape))

    return pl.pallas_call(
        kernel,
        grid_spec=pltpu.PrefetchScalarGridSpec(
            num_scalar_prefetch=2,
            grid=(1,),
            in_specs=[whole(a.shape) for a in ins],
            out_specs=[whole(shape) for shape in outs],
        ),
        out_shape=[jax.ShapeDtypeStruct(shape, BF) for shape in outs],
        compiler_params=pltpu.CompilerParams(vmem_limit_bytes=16 * 2**20),
        cost_estimate=pl.CostEstimate(
            flops=0, bytes_accessed=4 * sum(a.size for a in ins), transcendentals=0
        ),
        name=name,
    )(source, mode_number(), *ins)


def to_mode(spread, source):
    per_mode, modes = lax.axis_size("dp"), lax.axis_size("mode")
    piece = spread.shape[-2:]
    if spread.ndim == 4:
        outs = [(spread.shape[1], per_mode) + piece] * modes
    else:
        outs = [(per_mode,) + piece] * modes
    parts = by_rows(
        functools.partial(pick_kernel, modes, spread.shape[1] if spread.ndim == 4 else 0),
        source,
        [spread],
        outs,
        "pick",
    )
    got = [parts[0]] + [swap(parts[j], per_mode * j) for j in range(1, modes)]
    if spread.ndim == 4:
        return [part.reshape(part.shape[0], -1, part.shape[-1]) for part in got]
    return [part.reshape(-1, part.shape[-1]) for part in got]


def swap_modes(parts):
    per_mode = lax.axis_size("dp")
    lead = parts[0].shape[:-2]
    parts = [part.reshape(lead + (per_mode, -1, part.shape[-1])) for part in parts]
    return [parts[0]] + [swap(parts[j], per_mode * j) for j in range(1, len(parts))]


def put_back(parts, source):
    halves = parts[0].shape[0] if parts[0].ndim == 4 else 0
    shape = (lax.axis_size(ALL),) + ((halves,) if halves else ()) + parts[0].shape[-2:]
    return by_rows(
        functools.partial(put_kernel, len(parts), halves), source, parts, [shape], "put"
    )[0]


def dealt(value):
    count = lax.axis_size(ALL)
    return value.reshape(count, -1, value.shape[-1])


def to_all(value):
    return lax.all_to_all(value, ALL, 0, 0, tiled=True)


def swap(value, j):
    count = lax.axis_size(ALL)
    return lax.ppermute(value, ALL, [(i, i ^ j) for i in range(count)])


def device_number():
    return lax.axis_index(ALL).astype(jnp.int32)[None]


def place_kernel(me, even_ref, odd_ref, *o_refs):
    first = 0
    for o_ref in o_refs:
        at = pl.ds(first, o_ref.shape[2])
        first += o_ref.shape[2]
        for t in range(even_ref.shape[0]):
            o_ref[jnp.bitwise_xor(2 * t, me[0])] = even_ref[t, :, at]
            o_ref[jnp.bitwise_xor(2 * t + 1, me[0])] = odd_ref[t, :, at]


def place(even, odd, widths, number):
    count, rows, width = even.shape
    shapes = [(2 * count, rows, w) for w in widths]

    def whole(shape):
        return pl.BlockSpec(shape, lambda i, me: (0, 0, 0))

    return pl.pallas_call(
        place_kernel,
        grid_spec=pltpu.PrefetchScalarGridSpec(
            num_scalar_prefetch=1,
            grid=(1,),
            in_specs=[whole(even.shape)] * 2,
            out_specs=[whole(shape) for shape in shapes],
        ),
        out_shape=[jax.ShapeDtypeStruct(shape, even.dtype) for shape in shapes],
        compiler_params=pltpu.CompilerParams(vmem_limit_bytes=28 * 2**20),
        cost_estimate=BRIEF,
        name="place",
    )(number, even, odd)


def pack_kernel(counts, *refs):
    ins, outs = refs[: sum(counts)], refs[sum(counts) :]
    taken = 0
    for count, o_ref in zip(counts, outs):
        first = 0
        for part in ins[taken : taken + count]:
            o_ref[:, pl.ds(first, part.shape[1])] = part[...]
            first += part.shape[1]
        taken += count


def pack(*lists):
    cut = lambda e: e if not isinstance(e, tuple) else e[0]
    shape = lambda e: e.shape if not isinstance(e, tuple) else (e[0].shape[0], e[2])
    at = lambda e: 0 if not isinstance(e, tuple) else e[1] // e[2]
    entries = [e for group in lists for e in group]
    return pl.pallas_call(
        functools.partial(pack_kernel, [len(group) for group in lists]),
        grid=(1,),
        in_specs=[pl.BlockSpec(shape(e), lambda i, e=e: (0, at(e))) for e in entries],
        out_specs=[
            pl.BlockSpec((shape(group[0])[0], sum(shape(e)[1] for e in group)), lambda i: (0, 0))
            for group in lists
        ],
        out_shape=[
            jax.ShapeDtypeStruct((shape(group[0])[0], sum(shape(e)[1] for e in group)), BF)
            for group in lists
        ],
        name="pack",
    )(*[cut(e) for e in entries])


def gather_column(piece, late=None):
    per_mode = lax.axis_size("dp")
    got = [swap(piece, 2 * j) for j in range(1, per_mode // 2)]
    return jnp.stack([piece] + (got if late is None else tied(got, late)))


def gather_rest(column, widths, late=None):
    per_mode, modes = lax.axis_size("dp"), lax.axis_size("mode")
    got = [swap(column, per_mode * j) for j in range(1, modes)]
    if late is not None:
        got = tied(got, late)
    plane = jnp.stack([column] + got)
    plane = plane.reshape((-1,) + column.shape[1:])
    placed = place(plane, swap(plane, 1), widths, device_number())
    return [a.reshape(-1, a.shape[2]) for a in placed]


def take_kernel(parts, me, *refs):
    ins, (keep_ref, send_ref) = refs[:parts], refs[parts:]
    first = 0
    for in_ref in ins:
        at = pl.ds(first, in_ref.shape[2])
        first += in_ref.shape[2]
        for t in range(keep_ref.shape[0]):
            keep_ref[t, :, at] = in_ref[jnp.bitwise_xor(2 * t, me[0])]
            send_ref[t, :, at] = in_ref[jnp.bitwise_xor(2 * t + 1, me[0])]


def take(parts):
    count, rows = parts[0].shape[:2]
    width = sum(part.shape[2] for part in parts)
    half = jax.ShapeDtypeStruct((count // 2, rows, width), parts[0].dtype)

    def whole(shape):
        return pl.BlockSpec(shape, lambda i, me: (0, 0, 0))

    return pl.pallas_call(
        functools.partial(take_kernel, len(parts)),
        grid_spec=pltpu.PrefetchScalarGridSpec(
            num_scalar_prefetch=1,
            grid=(1,),
            in_specs=[whole(part.shape) for part in parts],
            out_specs=[whole(half.shape)] * 2,
        ),
        out_shape=[half, half],
        compiler_params=pltpu.CompilerParams(vmem_limit_bytes=48 * 2**20),
        cost_estimate=BRIEF,
        name="take",
    )(device_number(), *parts)


def add_up(parts):
    return functools.reduce(jnp.add, [part.astype(F32) for part in parts])


def scatter_pairs(parts):
    count = lax.axis_size(ALL)
    parts = [part.reshape(count, part.shape[0] // count, part.shape[1]) for part in parts]
    keep, send = take(parts)
    return add_up([keep, swap(send, 1)]).astype(BF)


def scatter_plane(pair):
    per_mode, modes = lax.axis_size("dp"), lax.axis_size("mode")
    plane = pair.reshape((modes, per_mode // 2) + pair.shape[1:])
    return add_up([plane[0]] + [swap(plane[j], per_mode * j) for j in range(1, modes)]).astype(BF)


def scatter_column(column):
    per_mode = lax.axis_size("dp")
    return add_up([column[0]] + [swap(column[j], 2 * j) for j in range(1, per_mode // 2)])


def later(lens, tokens):
    return lens - jnp.array([tokens, 0], jnp.int32)


def tied(first, second):
    return lax.optimization_barrier((first, second))[0]


def lanes_of(*vectors):
    columns_ = jnp.stack(vectors, axis=1)
    return jnp.pad(columns_, ((0, 0), (0, 128 - len(vectors))))


def on_device(
    rows,
    memory,
    cotangent,
    mode_ids,
    target_lengths,
    encoder_lengths,
    self_q,
    self_k,
    self_v,
    self_o,
    self_gain,
    cross_q,
    cross_k,
    cross_v,
    cross_o,
    cross_gain,
    ffn_gain,
    ffn_gate,
    ffn_up,
    ffn_down,
):
    devices = lax.axis_size(ALL)
    per_mode = lax.axis_size("dp")
    here = lax.axis_index(ALL)
    width = rows.shape[2]
    ff = ffn_gate.shape[2]
    index = jnp.arange(devices, dtype=jnp.int32)
    same = mode_ids[:, None] == mode_ids[None, :]
    earlier = index[None, :] < index[:, None]
    rank = jnp.sum(jnp.where(same & earlier, 1, 0), axis=1).astype(jnp.int32)
    target = mode_ids * per_mode + rank
    source = jnp.sum(
        jnp.where(target[:, None] == index[None, :], index[:, None], 0), axis=0
    ).astype(jnp.int32)
    live_len = jnp.sum(jnp.where(index == here, target_lengths, 0))
    memory_len = jnp.sum(jnp.where(index == here, encoder_lengths, 0))
    lens = jnp.stack([live_len, memory_len]).astype(jnp.int32)
    tokens, memory_row, incoming = rows[0], memory[0], cotangent[0]
    length = tokens.shape[0]
    half = length // 2
    key_count = memory_row.shape[0]
    valid = (jnp.arange(length, dtype=jnp.int32) < live_len)[:, None]
    grad_low = jnp.where(valid, incoming, jnp.zeros_like(incoming))

    group_pairs = HEADS // 4
    part = group_pairs * PAIR

    def of_group(g):
        return tuple((a, g * part, part) for a in (self_q, self_k, self_v))

    own_piece, rest_piece = pack(
        of_group(0) + of_group(1) + (lanes_of(self_gain, cross_gain, ffn_gain),),
        (self_o, cross_q, cross_k, cross_v, cross_o),
    )
    column = gather_column(own_piece)
    own_0, own_1, gain_columns = gather_rest(column, (3 * part, 3 * part, 128))
    crossing = lax.all_gather(rest_piece, ALL, axis=0, tiled=True)

    def weight(array, i, wide=width):
        return (array, (width, wide), (0, i))

    h1, qkv, gains = by_tokens(
        enter_kernel,
        length,
        [(tokens, 0)],
        [(a, a.shape, (0, 0)) for a in (own_0, own_1, gain_columns)],
        [(width, BF), (6 * part, BF), (None, F32)],
        "enter",
    )
    all_gains = (gains, gains.shape, (0, 0))
    pairs = HEADS // 2

    def of_pair(i):
        return lambda g: (g // group_pairs) * 3 * group_pairs + i * group_pairs + g % group_pairs

    grad_dealt = grad_low.reshape(2, devices, -1, width).swapaxes(0, 1)
    grad_spread = to_all(tied(grad_dealt, h1))

    wgu = lax.all_gather(
        jnp.concatenate([ffn_gate[0], ffn_up[0]], axis=1), "dp", axis=0, tiled=True
    )
    wd = lax.all_gather(ffn_down[0], "dp", axis=0, tiled=True)

    mixed, log_self = attend_forward(
        (qkv, of_pair(0), 0),
        (qkv, of_pair(1)),
        (qkv, of_pair(2)),
        lens,
        True,
        0,
        length,
        length,
        pairs,
    )
    wo, cq, ckv, co = (
        crossing[:, i * width : j * width] for i, j in ((0, 1), (1, 2), (2, 4), (4, 5))
    )

    def forward_middle(c):
        first = c * (half // QB)
        return by_tokens(
            middle_kernel,
            half,
            [(tokens, first), (mixed, first)],
            [all_gains, weight(wo, 0), weight(cq, 0)],
            [(width, F32), (width, BF), (width, BF)],
            "middle",
        )

    def forward_cross(c, query):
        return attend_forward(
            (query, 0, 0),
            (cross_kv, 0),
            (cross_kv, pairs),
            later(lens, c * half),
            False,
            0,
            half,
            key_count,
            pairs,
        )

    def forward_outer(x1, cross_mixed):
        return by_tokens(
            outer_kernel,
            half,
            [(x1, 0), (cross_mixed, 0)],
            [all_gains, weight(co, 0)],
            [(width, F32), (width, BF)],
            "outer",
        )

    x1_a, h2_a, query_a = forward_middle(0)
    cross_kv = nn(memory_row, ckv).astype(BF)
    cross_a, log_cross_a = forward_cross(0, query_a)
    x2_a, h3_a = forward_outer(x1_a, cross_a)
    spread_a = to_all(dealt(tied(h3_a, grad_spread)))
    grad_parts = to_mode(grad_spread, source)
    x1_b, h2_b, query_b = forward_middle(1)
    query_b = tied(query_b, h3_a)
    cross_b, log_cross_b = forward_cross(1, query_b)
    cross_b, grad_parts = lax.optimization_barrier((cross_b, grad_parts))
    x2_b, h3_b = forward_outer(x1_b, cross_b)
    routed_a = to_mode(tied(spread_a, cross_b), source)
    spread_b = to_all(dealt(h3_b))

    modes = len(routed_a)
    fed_a = feed(0, tied(routed_a, h3_b), grad_parts, wgu, wd, ())
    y_a, dh_a, kept_a = fed_a[:modes], fed_a[modes : 2 * modes], fed_a[2 * modes :]
    back_a = put_back(swap_modes(dh_a), source)
    routed_b = to_mode(tied(spread_b, dh_a[0]), source)
    routed_b, back_a = lax.optimization_barrier((routed_b, back_a))
    home_a = to_all(back_a)
    fed_b = feed(1, routed_b, grad_parts, wgu, wd, y_a + kept_a)
    home_a = home_a.reshape(half, width)
    y, dh_b = fed_b[:modes], fed_b[modes : 2 * modes]
    hidden, dgu, routed_h, routed_grad = fed_b[2 * modes :]
    back_b = swap_modes(dh_b)
    grad_wd = weight_grad(tied(hidden, home_a), routed_grad, 512)
    back_b = put_back(tied(back_b, grad_wd), source)
    grad_wgu = weight_grad(routed_h, tied(dgu, back_b), 256)
    sum_wgu = lax.psum_scatter(grad_wgu, "dp", scatter_dimension=0, tiled=True)
    sum_wd = lax.psum_scatter(grad_wd, "dp", scatter_dimension=0, tiled=True)
    home_b = to_all(back_b).reshape(half, width)
    home_a = tied(home_a, grad_wgu)
    y_mode = swap_modes(tied(y, back_b))

    def back_outer(c, dh, x2):
        return by_tokens(
            outer_back_kernel,
            half,
            [(dh, 0), (x2, 0), (grad_low, c * (half // QB))],
            [all_gains, weight(co, 0)],
            [(width, BF), (width, F32), (width, BF), (None, F32)],
            "outer_back",
        )

    def back_middle(c, dq, x1, dx2, kept):
        return by_tokens(
            middle_back_kernel,
            half,
            [(dq, 0), (x1, 0), (dx2, 0)],
            [all_gains, weight(cq, 0), weight(wo, 0)],
            [(width, F32), (width, BF), (width, BF), (None, F32)],
            "middle_back",
            c,
            kept,
        )

    def back_cross(c, query, mixed, grad, lse, carried):
        return attend_backward(
            (query, 0, 0),
            (cross_kv, 0),
            (cross_kv, pairs),
            (mixed, 0),
            (grad, 0),
            lse,
            later(lens, c * half),
            False,
            0,
            half,
            key_count,
            pairs,
            carried,
            c == 1,
        )

    def back_self(grad):
        return attend_backward(
            (qkv, of_pair(0), 0),
            (qkv, of_pair(1)),
            (qkv, of_pair(2)),
            (mixed, 0),
            (grad, 0),
            log_self,
            lens,
            True,
            0,
            length,
            length,
            pairs,
            None,
            True,
        )

    d2_a, dx2_a, do2_a, dgain_ffn_a = back_outer(0, home_a, x2_a)
    dcq_a, dck_a, dcv_a = back_cross(0, query_a, cross_a, do2_a, log_cross_a, None)
    *halves, dgain_cross_a = back_middle(0, dcq_a, x1_a, dx2_a, ())
    home_b, y_mode = lax.optimization_barrier((tied(home_b, halves), y_mode))
    d2_b, dx2_b, do2_b, dgain_ffn_b = back_outer(1, home_b, x2_b)
    y_put, do2_b = lax.optimization_barrier((put_back(y_mode, source), do2_b))
    y_home = to_all(y_put)
    dcq_b, dck, dcv = back_cross(1, query_b, cross_b, do2_b, log_cross_b, (dck_a, dcv_a))
    dx1, d1, do1, dgain_cross_b = back_middle(1, dcq_b, x1_b, dx2_b, halves)
    cross_pair = scatter_pairs(
        [
            (tn(h2_a, dcq_a) + tn(h2_b, dcq_b)).astype(BF),
            tn(memory_row, dck).astype(BF),
            tn(memory_row, dcv).astype(BF),
            (tn(cross_a, d2_a) + tn(cross_b, d2_b)).astype(BF),
            tn(mixed, d1).astype(BF),
        ]
    )
    do1, cross_pair = lax.optimization_barrier((do1, cross_pair))
    cross_plane = scatter_plane(cross_pair)
    grads = back_self(do1)
    grads, cross_plane, y_home, sum_wgu, sum_wd = lax.optimization_barrier(
        (grads, cross_plane, y_home, sum_wgu, sum_wd)
    )
    cross_sum = scatter_column(cross_plane)
    own_pair = scatter_pairs([tn(h1, d).astype(BF) for d in grads])
    own_plane = scatter_plane(own_pair)
    grads, dck, dcv = tied((grads, dck, dcv), own_pair)
    y_home = tied(y_home, own_plane)
    grad_tokens, dgain_self = by_tokens(
        enter_back_kernel,
        length,
        [(tokens, 0), (dx1, 0)] + [(d, 0) for d in grads],
        [all_gains] + [weight(own, i, part) for i in range(3) for own in (own_0, own_1)],
        [(width, BF), (None, F32)],
        "enter_back",
    )
    gain_grads = jnp.stack(
        [dgain_self[0], dgain_cross_a[0] + dgain_cross_b[0], dgain_ffn_a[0] + dgain_ffn_b[0]]
    )
    own_plane, gain_grads = lax.optimization_barrier((own_plane, gain_grads))
    own_sum = scatter_column(own_plane)
    gain_grads = gain_grads.reshape(3, devices, -1).swapaxes(0, 1)
    gain_sums = jnp.sum(to_all(gain_grads), axis=0)
    grad_memory = (nt(dck, ckv[:, :width]) + nt(dcv, ckv[:, width:])).astype(BF)
    y = y_home.swapaxes(0, 1).reshape(length, width)
    result = jnp.where(valid, jnp.concatenate([x2_a, x2_b]) + y.astype(F32), 0.0).astype(BF)

    def block(value, i):
        return value[:, i * width : (i + 1) * width]

    return (
        result[None],
        grad_tokens[None],
        grad_memory[None],
        block(own_sum, 0),
        block(own_sum, 1),
        block(own_sum, 2),
        block(cross_sum, 4),
        gain_sums[0],
        block(cross_sum, 0),
        block(cross_sum, 1),
        block(cross_sum, 2),
        block(cross_sum, 3),
        gain_sums[1],
        gain_sums[2],
        sum_wgu[:, :ff].astype(F32)[None],
        sum_wgu[:, ff:].astype(F32)[None],
        sum_wd.astype(F32)[None],
    )


def solution(mesh):
    rows = P(ALL, None, None)
    weight = P(ALL, None)
    gain = P(ALL)
    feeding = P("mode", "dp", None)
    return jax.shard_map(
        on_device,
        mesh=mesh,
        in_specs=(
            (rows,) * 3
            + (P(),) * 3
            + (weight,) * 4
            + (gain,)
            + (weight,) * 4
            + (gain,) * 2
            + (feeding,) * 3
        ),
        out_specs=(
            (rows,) * 3
            + (weight,) * 4
            + (gain,)
            + (weight,) * 4
            + (gain,) * 2
            + (feeding,) * 3
        ),
        check_vma=False,
    )
```

time: 638 us -> 565 us (0.89)
  blocking collectives: 75.5 us -> 0 us
  matrix products: 83 us -> 22.7 us
  local copies, waits for them, and re-layouts: 19.9 us -> 66.6 us
  starting transfers between devices: 66.3 us -> 102 us
  waiting for transfers between devices: 177 us -> 158 us
  other arithmetic: 31 us -> 24.2 us
    all_to_all x2 -> x0, blocking collectives: 75.5 us -> none  [the longest x1 52.7 us: to_modes(): spread = lax.all_to_all(dealt, ALL, 0, 0, tiled=True)]
    all_to_all x6 -> x7, waiting for transfers between devices: 73.4 us -> 19.6 us  [to_all(): return lax.all_to_all(value, ALL, 0, 0, tiled=True)]
    unnamed x93 -> x264, local copies, waits for them, and re-layouts: 11.9 us -> 58.6 us
    all_gather x3, waiting for transfers between devices: 0.06 us -> 30.2 us  [the longest x1 30.2 us: on_device(): lax.all_gather(jnp.concatenate([ffn_gate[0], ffn_up[0]], axis=1), 'dp', a...]
    ppermute x28 -> x39, starting transfers between devices: 34.2 us -> 61.5 us  [swap(): return lax.ppermute(value, ALL, [(i, i ^ j) for i in range(count)])]
    dot_general x5 -> x1, matrix products: 26.3 us -> 4.17 us  [nn(): return jnp.dot(left, right, preferred_element_type=F32)]
    dot_general x8 -> x2, matrix products: 24.4 us -> 5.04 us  [nt(): lax.dot_general(left, right, (((1,), (1,)), ((), ())), preferred_element_...]
    dot_general x10, matrix products: 32.2 us -> 13.4 us  [tn(): lax.dot_general(left, right, (((0,), (0,)), ((), ())), preferred_element_...]
  transfers between devices with their start and end apart: 39 -> 51, of which waited for: 23 -> 24; matrix products, arithmetic and copies ran while one was open for 19% -> 9% of each run, Pallas kernels for 21% -> 29%
where the time goes in v3:
time: 565 us; the launch traced here: 555 us
  Pallas kernels  165 us (29%)
  waiting for transfers between devices  158 us (28%)
  starting transfers between devices  102 us (18%)
  local copies, waits for them, and re-layouts  66.6 us (12%)
  other arithmetic  24.2 us (4%)
  matrix products  22.7 us (4%)
  between operations  15.4 us (3%)
    ppermute x39, waiting for transfers between devices, swap(): return lax.ppermute(value, ALL, [(i, i ^ j) for i in range(count)])  108 us
    ppermute x39, starting transfers between devices, swap(): return lax.ppermute(value, ALL, [(i, i ^ j) for i in range(count)])  61.5 us
    unnamed x264, local copies, waits for them, and re-layouts  58.6 us
    pallas_call x2, Pallas kernels, feed(): pl.pallas_call(functools.partial(feed_kernel, groups, ff, 512), grid=(1,)...  36.4 us
    pallas_call x3, Pallas kernels, attend_backward(): pl.pallas_call(functools.partial(attend_bwd_kernel, causal, start, had),...  34.2 us
    all_to_all x7, starting transfers between devices, to_all(): return lax.all_to_all(value, ALL, 0, 0, tiled=True)  31.8 us
    pallas_call x10, Pallas kernels, by_tokens(): pl.pallas_call(run, grid=(steps,), in_specs=[rows(a.shape[1], first) for...  31.2 us
    all_gather x1, waiting for transfers between devices, on_device(): lax.all_gather(jnp.concatenate([ffn_gate[0], ffn_up[0]], axis=1), 'dp', a...  30.2 us
  transfers between devices with their start and end apart: 51, of which 24 were waited for; matrix products, arithmetic and copies ran while one was open for 9% of the time, Pallas kernels for 29%

profile of v3, /device:TPU:0, one launch (start us, length us, event | category | flops | bytes accessed | tf_op | source)
XLA Modules:
  0.0 554.7 jit_solution(1186661629888118689)
XLA Ops:
  13.3 5.1 collective-permute-start.2
  33.2 10.3 %collective-permute-done.3 = bf16[4,24,2432]{2,1,0:T(8,128)(2,1)S(1)} collective-permute-done((bf16[4,24,2432]{2,1,0:T(8,128)(2,1)S(1)}, bf16[4,24,2432]{2,1,0:T(8,128)(2,1)S(1)}, u32[]{:S(2)}, u32[]{:S(2)}) %collective-permute-start.3) | collective-permute-done | bytes 466976 | tf_op jit(solution)/shard_map/ppermute | solution.py:537
  43.6 6.7 %collective-permute-done.4 = bf16[4,24,2432]{2,1,0:T(8,128)(2,1)S(1)} collective-permute-done((bf16[4,24,2432]{2,1,0:T(8,128)(2,1)S(1)}, bf16[4,24,2432]{2,1,0:T(8,128)(2,1)S(1)}, u32[]{:S(2)}, u32[]{:S(2)}) %collective-permute-start.4) | collective-permute-done | bytes 466976 | tf_op jit(solution)/shard_map/ppermute | solution.py:537
  50.2 7.0 %collective-permute-done.5 = bf16[4,24,2432]{2,1,0:T(8,128)(2,1)S(1)} collective-permute-done((bf16[4,24,2432]{2,1,0:T(8,128)(2,1)S(1)}, bf16[4,24,2432]{2,1,0:T(8,128)(2,1)S(1)}, u32[]{:S(2)}, u32[]{:S(2)}) %collective-permute-start.5) | collective-permute-done | bytes 466976 | tf_op jit(solution)/shard_map/ppermute | solution.py:537
  66.0 5.3 enter.1
  82.5 12.9 %attend_causal.1 = (bf16[1024,768]{1,0:T(8,128)(2,1)S(1)}, f32[6,2,1024]{2,1,0:T(2,128)S(1)}) custom-call(s32[2]{0:T(128)S(1)} %get-tuple-element.310.lens, bf16[1024,2304]{1,0:T(8,128)(2,1)S(1)} %copy-done.3, bf16[1024,2304]{1,0:T(8,128)(2,1)S(1)} %copy-done.3, bf16[1024,2304]{1,0:T(8,128)(2,1)S(1)} %copy-done.3), custom_call_target="tpu_custom_call" | custom-call | flops 1000000 | bytes 10000 | tf_op jit(solution)/shard_map/attend_causal/pallas_call | solution.py:155
  106.7 14.3 %attend_memory.2 = (bf16[512,768]{1,0:T(8,128)(2,1)S(1)}, f32[6,2,512]{2,1,0:T(2,128)S(1)}) custom-call(s32[2]{0:T(128)S(1)} %get-tuple-element.310.lens, bf16[512,768]{1,0:T(8,128)(2,1)S(1)} %get-tuple-element.172.q_ref.refs_0_, bf16[512,1536]{1,0:T(8,128)(2,1)S(1)} %fusion.2.k_ref.v_ref.refs_1_.refs_2_, bf16[512,1536]{1,0:T(8,128)(2,1)S(1)} %fusion.2.k_ref.v_ref.refs_1_.refs_2_), custom_call_target="tpu_custom_call" | custom-call | flops 1000000 | bytes 10000 | tf_op jit(solution)/shard_map/attend_memory/pallas_call | solution.py:155
  125.8 16.4 %all-to-all-done.x_ref = bf16[32,2,16,768]{3,2,1,0:T(8,128)(2,1)} async-done(((bf16[32,2,16,768]{3,2,1,0:T(8,128)(2,1)}), bf16[32,2,16,768]{3,2,1,0:T(8,128)(2,1)}, u32[]{:S(2)}, u32[]{:S(2)}) %all-to-all-start) | async-done | bytes 1572896 | tf_op jit(solution)/shard_map/all_to_all | solution.py:532
  167.5 7.3 %collective-permute-done.9 = bf16[2,8,16,768]{3,2,1,0:T(8,128)(2,1)S(1)} collective-permute-done((bf16[2,8,16,768]{3,2,1,0:T(8,128)(2,1)S(1)}, bf16[2,8,16,768]{3,2,1,0:T(8,128)(2,1)S(1)}, u32[]{:S(2)}, u32[]{:S(2)}) %collective-permute-start.9) | collective-permute-done | bytes 393248 | tf_op jit(solution)/shard_map/ppermute | solution.py:537
  180.8 6.1 %all-to-all-start.1 = ((bf16[32,16,768]{2,1,0:T(8,128)(2,1)}), bf16[32,16,768]{2,1,0:T(8,128)(2,1)}, u32[]{:S(2)}, u32[]{:S(2)}) async-start(bf16[32,16,768]{2,1,0:T(8,128)(2,1)} %bitcast.169), calls=%async_computation.1 | async-start | bytes 1572864 | tf_op jit(solution)/shard_map/all_to_all | solution.py:532
  193.0 5.4 collective-permute-done.10
  198.4 6.5 %collective-permute-done.11 = bf16[8,16,768]{2,1,0:T(8,128)(2,1)S(1)} collective-permute-done((bf16[8,16,768]{2,1,0:T(8,128)(2,1)S(1)}, bf16[8,16,768]{2,1,0:T(8,128)(2,1)S(1)}, u32[]{:S(2)}, u32[]{:S(2)}) %collective-permute-start.11) | collective-permute-done | bytes 196640 | tf_op jit(solution)/shard_map/ppermute | solution.py:537
  205.7 30.2 %all-gather.7.cloned.1.call-done.refs_8_ = bf16[768,4096]{1,0:T(8,128)(2,1)} async-done(((bf16[96,4096]{1,0:T(8,128)(2,1)}), bf16[768,4096]{1,0:T(8,128)(2,1)}) %all-gather.7.cloned.1.call-update) | async-done | bytes 6291472 | tf_op jit(solution)/shard_map/all_gather | solution.py:773
  235.9 18.1 %feed.2 = (bf16[2,128,768]{2,1,0:T(8,128)(2,1)}, bf16[2,128,768]{2,1,0:T(8,128)(2,1)}, bf16[2,128,768]{2,1,0:T(8,128)(2,1)}, bf16[2,128,768]{2,1,0:T(8,128)(2,1)...) custom-call(bf16[128,768]{1,0:T(8,128)(2,1)} %bitcast.174, ...), custom_call_target="tpu_custom_call" | custom-call | flops 1000000 | bytes 10000 | tf_op jit(solution)/shard_map/feed/pallas_call | solution.py:411
  279.2 8.3 %reduce-scatter.5.cloned.1.call-start = ((), (), s32[]{:S(2)}) async-start(), calls=%async_computation.12 | async-start | bytes 3538944 | tf_op jit(solution)/shard_map/reduce_scatter | solution.py:857
  287.5 18.4 %feed.3 = (bf16[2,128,768]{2,1,0:T(8,128)(2,1)}, bf16[2,128,768]{2,1,0:T(8,128)(2,1)}, bf16[2,128,768]{2,1,0:T(8,128)(2,1)}, bf16[2,128,768]{2,1,0:T(8,128)(2,1)...) custom-call(bf16[128,768]{1,0:T(8,128)(2,1)} %bitcast.171, ...), custom_call_target="tpu_custom_call", output_to_operand_aliasing={{0}: (10, {}), {1}: (11, {}), {2}: (12, {}), {3}: (13, {}),... | custom-call | flops 1000000 | bytes 10000 | tf_op jit(solution)/shard_map/feed/pallas_call | solution.py:411
  331.2 10.7 %weight_grad.3 = bf16[768,4096]{1,0:T(8,128)(2,1)S(1)} custom-call(bf16[1024,768]{1,0:T(8,128)(2,1)S(1)} %copy-done.41, bf16[1024,4096]{1,0:T(8,128)(2,1)} %get-tuple-element.238.g_ref), custom_call_target="tpu_custom_call" | custom-call | flops 1000000 | bytes 10000 | tf_op jit(solution)/shard_map/weight_grad/pallas_call | solution.py:343
  361.0 14.8 %attend_memory_back.2 = (bf16[512,768]{1,0:T(8,128)(2,1)S(1)}, f32[512,768]{1,0:T(8,128)S(1)}, f32[512,768]{1,0:T(8,128)S(1)}) custom-call(s32[2]{0:T(128)S(1)} %get-tuple-element.310.lens, bf16[512,768]{1,0:T(8,128)(2,1)S(1)} %copy-done.62, bf16[512,1536]{1,0:T(8,128)(2,1)S(1)} %fusion.2.k_ref.v_ref.refs_1_.refs_2_, ...), custom_call_target="tpu_custom_call" | custom-call | flops 1000000 | bytes 10000 | tf_op jit(solution)/shard_map/attend_memory_back/pallas_call | solution.py:187
  415.0 11.5 %collective-permute-start.25 = (bf16[16,24,3840]{2,1,0:T(8,128)(2,1)}, bf16[16,24,3840]{2,1,0:T(8,128)(2,1)}, u32[]{:S(2)}, u32[]{:S(2)}) collective-permute-start(bf16[16,24,3840]{2,1,0:T(8,128)(2,1)} %get-tuple-element.277), channel_id=1, source_target_pairs={{0,1},{1,0},{2,3},{3,2},{4,5},{5,4},{6,7},{7,6},{8,9},{9,8},{10,11... | collective-permute-start | bytes 8847368 | tf_op jit(solution)/shard_map/ppermute | solution.py:537
  426.5 6.6 %all-to-all-start.5 = ((bf16[32,2,16,768]{3,2,1,0:T(8,128)(2,1)}), bf16[32,2,16,768]{3,2,1,0:T(8,128)(2,1)}, u32[]{:S(2)}, u32[]{:S(2)}) async-start(bf16[32,2,16,768]{3,2,1,0:T(8,128)(2,1)} %copy-done.44), calls=%async_computation.5 | async-start | bytes 3145728 | tf_op jit(solution)/shard_map/all_to_all | solution.py:532
  441.0 16.2 %attend_causal_back.1 = (bf16[1024,768]{1,0:T(8,128)(2,1)S(1)}, bf16[1024,768]{1,0:T(8,128)(2,1)S(1)}, bf16[1024,768]{1,0:T(8,128)(2,1)S(1)}) custom-call(s32[2]{0:T(128)S(1)} %get-tuple-element.310.lens, bf16[1024,2304]{1,0:T(8,128)(2,1)S(1)} %bitcast.141, bf16[1024,2304]{1,0:T(8,128)(2,1)S(1)} %bitcast.141, bf16[1024,2304]{1,0:T(8,128)(2,1)S(1)} %bitcast.141, ...), custom_call_target="tpu_custom_call" | custom-call | flops 1000000 | bytes 10000 | tf_op jit(solution)/shard_map/attend_causal_back/pallas_call | solution.py:187
  460.8 6.6 %collective-permute-done.26 = bf16[4,24,3840]{2,1,0:T(8,128)(2,1)S(1)} collective-permute-done((bf16[4,24,3840]{2,1,0:T(8,128)(2,1)S(1)}, bf16[4,24,3840]{2,1,0:T(8,128)(2,1)S(1)}, u32[]{:S(2)}, u32[]{:S(2)}) %collective-permute-start.26) | collective-permute-done | bytes 737312 | tf_op jit(solution)/shard_map/ppermute | solution.py:537
  467.3 18.1 %collective-permute-done.28 = bf16[4,24,3840]{2,1,0:T(8,128)(2,1)S(1)} collective-permute-done((bf16[4,24,3840]{2,1,0:T(8,128)(2,1)S(1)}, bf16[4,24,3840]{2,1,0:T(8,128)(2,1)S(1)}, u32[]{:S(2)}, u32[]{:S(2)}) %collective-permute-start.28) | collective-permute-done | bytes 737312 | tf_op jit(solution)/shard_map/ppermute | solution.py:537
  513.5 7.5 %enter_back.1 = (bf16[1024,768]{1,0:T(8,128)(2,1)}, f32[8,768]{1,0:T(8,128)S(1)}) custom-call(bf16[1024,768]{1,0:T(8,128)(2,1)S(1)} %bitcast.153, f32[1024,768]{1,0:T(8,128)S(1)} %copy-done.33, bf16[1024,768]{1,0:T(8,128)(2,1)S(1)} %copy-done.81, bf16[1024,768]{1,0:T(8,128)(2,1)S(1)} %copy-done.83, bf16[1024,768]{1,0:T(8,128)(2,1)S(1)} %copy-done.86, ...), custom_call_target="tpu_custom_call" | custom-call | flops 1000000 | bytes 10000 | tf_op jit(solution)/shard_map/enter_back/pallas_call | solution.py:316
  (432 shorter events, 269.0 us)
Async XLA Ops:
  7.2 89.9 %all-gather.5.cloned.1.call-start = ((), (), s32[]{:S(2)}) async-start(), calls=%async_computation.9 | async-start | bytes 6082560 | tf_op jit(solution)/shard_map/all_gather | solution.py:751
  10.4 195.3 %all-gather.9.cloned.1.call-start = ((), (), s32[]{:S(2)}) async-start(), calls=%async_computation.13 | async-start | bytes 3538944 | tf_op jit(solution)/shard_map/all_gather | solution.py:776
  11.2 224.7 %all-gather.7.cloned.1.call-start = ((), (), s32[]{:S(2)}) async-start(), calls=%async_computation.10 | async-start | bytes 7077888 | tf_op jit(solution)/shard_map/all_gather | solution.py:773
  31.2 19.0 %collective-permute-start.4 = (bf16[4,24,2432]{2,1,0:T(8,128)(2,1)S(1)}, bf16[4,24,2432]{2,1,0:T(8,128)(2,1)S(1)}, u32[]{:S(2)}, u32[]{:S(2)}) collective-permute-start(bf16[4,24,2432]{2,1,0:T(8,128)(2,1)S(1)} %get-tuple-element.326), channel_id=1, source_target_pairs={{0,16},{1,17},{2,18},{3,19},{4,20},{5,21},{6,22},{7,23},{8,24},{9,... | collective-permute-start | bytes 1400840 | tf_op jit(solution)/shard_map/ppermute | solution.py:537
  32.8 24.5 %collective-permute-start.5 = (bf16[4,24,2432]{2,1,0:T(8,128)(2,1)S(1)}, bf16[4,24,2432]{2,1,0:T(8,128)(2,1)S(1)}, u32[]{:S(2)}, u32[]{:S(2)}) collective-permute-start(bf16[4,24,2432]{2,1,0:T(8,128)(2,1)S(1)} %get-tuple-element.326), channel_id=1, source_target_pairs={{0,24},{1,25},{2,26},{3,27},{4,28},{5,29},{6,30},{7,31},{8,16},{9,... | collective-permute-start | bytes 1400840 | tf_op jit(solution)/shard_map/ppermute | solution.py:537
  75.3 66.9 %all-to-all-start = ((bf16[32,2,16,768]{3,2,1,0:T(8,128)(2,1)}), bf16[32,2,16,768]{3,2,1,0:T(8,128)(2,1)}, u32[]{:S(2)}, u32[]{:S(2)}) async-start(bf16[32,2,16,768]{3,2,1,0:T(8,128)(2,1)} %fusion.4), calls=%async_computation | async-start | bytes 3145728 | tf_op jit(solution)/shard_map/all_to_all | solution.py:532
  142.2 38.6 %all-to-all-start.2 = ((bf16[32,16,768]{2,1,0:T(8,128)(2,1)}), bf16[32,16,768]{2,1,0:T(8,128)(2,1)}, u32[]{:S(2)}, u32[]{:S(2)}) async-start(bf16[32,16,768]{2,1,0:T(8,128)(2,1)} %bitcast.170), calls=%async_computation.2 | async-start | bytes 1572864 | tf_op jit(solution)/shard_map/all_to_all | solution.py:532
  152.9 21.9 %collective-permute-start.9 = (bf16[2,8,16,768]{3,2,1,0:T(8,128)(2,1)S(1)}, bf16[2,8,16,768]{3,2,1,0:T(8,128)(2,1)S(1)}, u32[]{:S(2)}, u32[]{:S(2)}) collective-permute-start(bf16[2,8,16,768]{3,2,1,0:T(8,128)(2,1)S(1)} %get-tuple-element.185), channel_id=1, source_target_pairs={{0,24},{1,25},{2,26},{3,27},{4,28},{5,29},{6,30},{7,31},{8,16},{9,... | collective-permute-start | bytes 1179656 | tf_op jit(solution)/shard_map/ppermute | solution.py:537
  180.8 76.7 %all-to-all-start.1 = ((bf16[32,16,768]{2,1,0:T(8,128)(2,1)}), bf16[32,16,768]{2,1,0:T(8,128)(2,1)}, u32[]{:S(2)}, u32[]{:S(2)}) async-start(bf16[32,16,768]{2,1,0:T(8,128)(2,1)} %bitcast.169), calls=%async_computation.1 | async-start | bytes 1572864 | tf_op jit(solution)/shard_map/all_to_all | solution.py:532
  275.9 30.0 %all-to-all-start.3 = ((bf16[32,16,768]{2,1,0:T(8,128)(2,1)}), bf16[32,16,768]{2,1,0:T(8,128)(2,1)}, u32[]{:S(2)}, u32[]{:S(2)}) async-start(bf16[32,16,768]{2,1,0:T(8,128)(2,1)} %copy-done.60), calls=%async_computation.3 | async-start | bytes 1572864 | tf_op jit(solution)/shard_map/all_to_all | solution.py:532
  279.2 207.5 %reduce-scatter.5.cloned.1.call-start = ((), (), s32[]{:S(2)}) async-start(), calls=%async_computation.12 | async-start | bytes 3538944 | tf_op jit(solution)/shard_map/reduce_scatter | solution.py:857
  315.6 171.1 %reduce-scatter.3.cloned.1.call-start = ((), (), s32[]{:S(2)}) async-start(), calls=%async_computation.11 | async-start | bytes 7077888 | tf_op jit(solution)/shard_map/reduce_scatter | solution.py:856
  344.6 40.9 %all-to-all-start.4 = ((bf16[32,16,768]{2,1,0:T(8,128)(2,1)}), bf16[32,16,768]{2,1,0:T(8,128)(2,1)}, u32[]{:S(2)}, u32[]{:S(2)}) async-start(bf16[32,16,768]{2,1,0:T(8,128)(2,1)} %copy-done.59), calls=%async_computation.4 | async-start | bytes 1572864 | tf_op jit(solution)/shard_map/all_to_all | solution.py:532
  351.9 33.6 %collective-permute-start.22 = (bf16[2,8,16,768]{3,2,1,0:T(8,128)(2,1)}, bf16[2,8,16,768]{3,2,1,0:T(8,128)(2,1)}, u32[]{:S(2)}, u32[]{:S(2)}) collective-permute-start(bf16[2,8,16,768]{3,2,1,0:T(8,128)(2,1)} %bitcast.55), channel_id=1, source_target_pairs={{0,8},{1,9},{2,10},{3,11},{4,12},{5,13},{6,14},{7,15},{8,0},{9,1},... | collective-permute-start | bytes 1179656 | tf_op jit(solution)/shard_map/ppermute | solution.py:537
  353.7 31.8 %collective-permute-start.23 = (bf16[2,8,16,768]{3,2,1,0:T(8,128)(2,1)}, bf16[2,8,16,768]{3,2,1,0:T(8,128)(2,1)}, u32[]{:S(2)}, u32[]{:S(2)}) collective-permute-start(bf16[2,8,16,768]{3,2,1,0:T(8,128)(2,1)} %bitcast.56), channel_id=1, source_target_pairs={{0,16},{1,17},{2,18},{3,19},{4,20},{5,21},{6,22},{7,23},{8,24},{9,... | collective-permute-start | bytes 1179656 | tf_op jit(solution)/shard_map/ppermute | solution.py:537
  355.2 30.4 %collective-permute-start.24 = (bf16[2,8,16,768]{3,2,1,0:T(8,128)(2,1)}, bf16[2,8,16,768]{3,2,1,0:T(8,128)(2,1)}, u32[]{:S(2)}, u32[]{:S(2)}) collective-permute-start(bf16[2,8,16,768]{3,2,1,0:T(8,128)(2,1)} %bitcast.57), channel_id=1, source_target_pairs={{0,24},{1,25},{2,26},{3,27},{4,28},{5,29},{6,30},{7,31},{8,16},{9,... | collective-permute-start | bytes 1179656 | tf_op jit(solution)/shard_map/ppermute | solution.py:537
  415.0 18.0 %collective-permute-start.25 = (bf16[16,24,3840]{2,1,0:T(8,128)(2,1)}, bf16[16,24,3840]{2,1,0:T(8,128)(2,1)}, u32[]{:S(2)}, u32[]{:S(2)}) collective-permute-start(bf16[16,24,3840]{2,1,0:T(8,128)(2,1)} %get-tuple-element.277), channel_id=1, source_target_pairs={{0,1},{1,0},{2,3},{3,2},{4,5},{5,4},{6,7},{7,6},{8,9},{9,8},{10,11... | collective-permute-start | bytes 8847368 | tf_op jit(solution)/shard_map/ppermute | solution.py:537
  426.5 60.2 %all-to-all-start.5 = ((bf16[32,2,16,768]{3,2,1,0:T(8,128)(2,1)}), bf16[32,2,16,768]{3,2,1,0:T(8,128)(2,1)}, u32[]{:S(2)}, u32[]{:S(2)}) async-start(bf16[32,2,16,768]{3,2,1,0:T(8,128)(2,1)} %copy-done.44), calls=%async_computation.5 | async-start | bytes 3145728 | tf_op jit(solution)/shard_map/all_to_all | solution.py:532
  435.9 31.4 %collective-permute-start.26 = (bf16[4,24,3840]{2,1,0:T(8,128)(2,1)S(1)}, bf16[4,24,3840]{2,1,0:T(8,128)(2,1)S(1)}, u32[]{:S(2)}, u32[]{:S(2)}) collective-permute-start(bf16[4,24,3840]{2,1,0:T(8,128)(2,1)S(1)} %get-tuple-element.314), channel_id=1, source_target_pairs={{0,8},{1,9},{2,10},{3,11},{4,12},{5,13},{6,14},{7,15},{8,0},{9,1},... | collective-permute-start | bytes 2211848 | tf_op jit(solution)/shard_map/ppermute | solution.py:537
  437.7 29.6 %collective-permute-start.27 = (bf16[4,24,3840]{2,1,0:T(8,128)(2,1)S(1)}, bf16[4,24,3840]{2,1,0:T(8,128)(2,1)S(1)}, u32[]{:S(2)}, u32[]{:S(2)}) collective-permute-start(bf16[4,24,3840]{2,1,0:T(8,128)(2,1)S(1)} %get-tuple-element.316), channel_id=1, source_target_pairs={{0,16},{1,17},{2,18},{3,19},{4,20},{5,21},{6,22},{7,23},{8,24},{9,... | collective-permute-start | bytes 2211848 | tf_op jit(solution)/shard_map/ppermute | solution.py:537
  439.2 46.3 %collective-permute-start.28 = (bf16[4,24,3840]{2,1,0:T(8,128)(2,1)S(1)}, bf16[4,24,3840]{2,1,0:T(8,128)(2,1)S(1)}, u32[]{:S(2)}, u32[]{:S(2)}) collective-permute-start(bf16[4,24,3840]{2,1,0:T(8,128)(2,1)S(1)} %get-tuple-element.315), channel_id=1, source_target_pairs={{0,24},{1,25},{2,26},{3,27},{4,28},{5,29},{6,30},{7,31},{8,16},{9,... | collective-permute-start | bytes 2211848 | tf_op jit(solution)/shard_map/ppermute | solution.py:537
  508.4 18.9 %collective-permute-start.31 = (bf16[4,24,2304]{2,1,0:T(8,128)(2,1)S(1)}, bf16[4,24,2304]{2,1,0:T(8,128)(2,1)S(1)}, u32[]{:S(2)}, u32[]{:S(2)}) collective-permute-start(bf16[4,24,2304]{2,1,0:T(8,128)(2,1)S(1)} %get-tuple-element.319), channel_id=1, source_target_pairs={{0,16},{1,17},{2,18},{3,19},{4,20},{5,21},{6,22},{7,23},{8,24},{9,... | collective-permute-start | bytes 1327112 | tf_op jit(solution)/shard_map/ppermute | solution.py:537
  509.0 18.3 %collective-permute-start.32 = (bf16[4,24,2304]{2,1,0:T(8,128)(2,1)S(1)}, bf16[4,24,2304]{2,1,0:T(8,128)(2,1)S(1)}, u32[]{:S(2)}, u32[]{:S(2)}) collective-permute-start(bf16[4,24,2304]{2,1,0:T(8,128)(2,1)S(1)} %get-tuple-element.318), channel_id=1, source_target_pairs={{0,24},{1,25},{2,26},{3,27},{4,28},{5,29},{6,30},{7,31},{8,16},{9,... | collective-permute-start | bytes 1327112 | tf_op jit(solution)/shard_map/ppermute | solution.py:537
  528.1 19.1 %collective-permute-start.33 = (bf16[24,2304]{1,0:T(8,128)(2,1)}, bf16[24,2304]{1,0:T(8,128)(2,1)S(1)}, u32[]{:S(2)}, u32[]{:S(2)}) collective-permute-start(bf16[24,2304]{1,0:T(8,128)(2,1)} %get-tuple-element.327), channel_id=1, source_target_pairs={{0,2},{1,3},{2,0},{3,1},{4,6},{5,7},{6,4},{7,5},{8,10},{9,11},{10,... | collective-permute-start | bytes 331784 | tf_op jit(solution)/shard_map/ppermute | solution.py:537
  (159 other events, 942.6 us)
Sparse Core Ops, SparseCore 0:
  11.6 79.5 all-gather.4
  92.8 53.2 all-gather.8
  148.4 87.4 all-gather.6
  315.7 43.4 reduce-scatter.4
  361.4 71.9 reduce-scatter.2

commit v4 on v3

--- a/solution.py
+++ b/solution.py
@@ -14,6 +14,7 @@
 NEG = -1e30
 SCALE = HEAD_DIM ** -0.5
 QB = 256
+AB = 512
 ALL = ("mode", "dp")
 BF = jnp.bfloat16
 F32 = jnp.float32
@@ -42,52 +43,60 @@
     if causal:
         parts = []
         if qb:
-            parts.append((0, qb * QB, None))
-        row = lax.broadcasted_iota(jnp.int32, (QB, QB), 0)
-        col = lax.broadcasted_iota(jnp.int32, (QB, QB), 1)
-        parts.append((qb * QB, QB, row <= col))
+            parts.append((0, qb * AB, None))
+        row = lax.broadcasted_iota(jnp.int32, (AB, AB), 0)
+        col = lax.broadcasted_iota(jnp.int32, (AB, AB), 1)
+        parts.append((qb * AB, AB, row <= col))
         return parts
-    row = lax.broadcasted_iota(jnp.int32, (key_count, QB), 0)
+    row = lax.broadcasted_iota(jnp.int32, (key_count, AB), 0)
     return [(0, key_count, row < limit)]
 
 
-def attend_fwd_kernel(causal, start, lens, q_ref, k_ref, v_ref, o_ref, lse_ref, vt):
+def attend_fwd_kernel(causal, lens, q_ref, k_ref, v_ref, o_ref, lse_ref):
     live, limit = lens[0], lens[1]
     length, key_count = q_ref.shape[0], k_ref.shape[0]
-    vt[...] = jnp.swapaxes(v_ref[...].astype(F32), 0, 1).astype(BF)
-    for block in range(length // QB):
-        at = pl.ds(block * QB, QB)
-        qb = start // QB + block
-
-        @pl.when(qb * QB < live)
-        def _(qb=qb, at=at):
+    block = min(AB, length)
+    first_head = lax.broadcasted_iota(jnp.int32, (1, PAIR), 1) < HEAD_DIM
+    for start in range(0, length, block):
+        at = pl.ds(start, block)
+
+        @pl.when(start < live)
+        def _(start=start, at=at):
             query = q_ref[at, :] * jnp.asarray(SCALE, BF)
-            parts = masks(causal, key_count, qb, limit)
-            outs = []
+            if causal:
+                row = lax.broadcasted_iota(jnp.int32, (block, block), 0)
+                col = lax.broadcasted_iota(jnp.int32, (block, block), 1)
+                parts = [(0, start, None)] if start else []
+                parts.append((start, block, col <= row))
+            else:
+                col = lax.broadcasted_iota(jnp.int32, (block, key_count), 1)
+                parts = [(0, key_count, col < limit)]
+            outs, logs = [], []
             for h in range(2):
                 mine = head_lanes(query, h)
                 scores = []
                 for first, count, mask in parts:
-                    s = nt(k_ref[pl.ds(first, count), :], mine)
+                    s = nt(mine, k_ref[pl.ds(first, count), :])
                     scores.append(s if mask is None else jnp.where(mask, s, NEG))
                 top = functools.reduce(
-                    jnp.maximum, [jnp.max(s, axis=0, keepdims=True) for s in scores]
+                    jnp.maximum, [jnp.max(s, axis=1, keepdims=True) for s in scores]
                 )
                 total, mixed = 0.0, 0.0
                 for (first, count, _), s in zip(parts, scores):
                     p = jnp.exp(s - top)
-                    total = total + jnp.sum(p, axis=0, keepdims=True)
-                    mixed = mixed + nn(
-                        vt[pl.ds(h * HEAD_DIM, HEAD_DIM), pl.ds(first, count)], p.astype(BF)
-                    )
+                    total = total + jnp.sum(p, axis=1, keepdims=True)
+                    mixed = mixed + nn(p.astype(BF), v_ref[pl.ds(first, count), :])
                 outs.append(mixed / total)
-                lse_ref[0, pl.ds(h, 1), at] = top + jnp.log(total)
-            o_ref[at, :] = jnp.swapaxes(jnp.concatenate(outs, axis=0), 0, 1).astype(BF)
-
-        @pl.when(qb * QB >= live)
+                logs.append(top + jnp.log(total))
+            o_ref[at, :] = jnp.where(first_head, outs[0], outs[1]).astype(BF)
+            rows = jnp.swapaxes(jnp.where(first_head, logs[0], logs[1]), 0, 1)
+            lse_ref[0, pl.ds(0, 1), at] = rows[0:1]
+            lse_ref[0, pl.ds(1, 1), at] = rows[HEAD_DIM : HEAD_DIM + 1]
+
+        @pl.when(start >= live)
         def _(at=at):
-            o_ref[at, :] = jnp.zeros((QB, PAIR), BF)
-            lse_ref[0, pl.ds(0, 2), at] = jnp.zeros((2, QB), F32)
+            o_ref[at, :] = jnp.zeros((block, PAIR), BF)
+            lse_ref[0, pl.ds(0, 2), at] = jnp.zeros((2, block), F32)
 
 
 def attend_bwd_kernel(causal, start, carried, lens, *refs):
@@ -103,11 +112,11 @@
     if carried:
         dk[pl.ds(0, carried), :] = more[0][...]
         dv[pl.ds(0, carried), :] = more[1][...]
-    for block in range(length // QB):
-        at = pl.ds(block * QB, QB)
-        qb = start // QB + block
-
-        @pl.when(qb * QB < live)
+    for block in range(length // AB):
+        at = pl.ds(block * AB, AB)
+        qb = start // AB + block
+
+        @pl.when(qb * AB < live)
         def _(qb=qb, at=at):
             query = q_ref[at, :] * jnp.asarray(SCALE, BF)
             grad = do_ref[at, :]
@@ -137,9 +146,9 @@
                 dv[pl.ds(first, count), :] += sum_v
             dq_ref[at, :] = jnp.swapaxes(jnp.concatenate(outs, axis=0), 0, 1).astype(BF)
 
-        @pl.when(qb * QB >= live)
+        @pl.when(qb * AB >= live)
         def _(at=at):
-            dq_ref[at, :] = jnp.zeros((QB, PAIR), BF)
+            dq_ref[at, :] = jnp.zeros((AB, PAIR), BF)
 
     dk_ref[...] = dk[...].astype(dk_ref.dtype)
     dv_ref[...] = dv[...].astype(dv_ref.dtype)
@@ -150,10 +159,10 @@
     return pl.BlockSpec((rows, PAIR), lambda g, lens: (row_block, at(g)))
 
 
-def attend_forward(query, keys, values, lens, causal, start, length, key_count, pairs):
+def attend_forward(query, keys, values, lens, causal, length, key_count, pairs):
     (qa, q0, rows), (ka, k0), (va, v0) = query, keys, values
     return pl.pallas_call(
-        functools.partial(attend_fwd_kernel, causal, start),
+        functools.partial(attend_fwd_kernel, causal),
         grid_spec=pltpu.PrefetchScalarGridSpec(
             num_scalar_prefetch=1,
             grid=(pairs,),
@@ -166,7 +175,6 @@
                 columns(length, 0),
                 pl.BlockSpec((1, 2, length), lambda g, lens: (g, 0, 0)),
             ],
-            scratch_shapes=[pltpu.VMEM((PAIR, key_count), BF)],
         ),
         out_shape=[
             jax.ShapeDtypeStruct((length, pairs * PAIR), BF),
@@ -239,6 +247,10 @@
     qkv_ref[:, pl.ds(wide, wide)] = nn(h, w1_ref[...]).astype(BF)
 
 
+def product_kernel(x_ref, w_ref, o_ref):
+    o_ref[...] = nn(x_ref[...], w_ref[...]).astype(BF)
+
+
 def middle_kernel(x_ref, o_ref, gain_ref, wo_ref, cq_ref, x1_ref, h_ref, q_ref):
     x1 = x_ref[...].astype(F32) + nn(o_ref[...], wo_ref[...])
     h = normed(x1, gain_ref[1:2]).astype(BF)
@@ -333,26 +345,32 @@
     )(*[a for a, _ in blocked], *[a for a, _, _ in whole], *kept)
 
 
-def weight_grad_kernel(x_ref, g_ref, o_ref):
-    o_ref[...] = tn(x_ref[...], g_ref[...]).astype(BF)
-
-
-def weight_grad(x, grad, columns_at_once):
-    tokens, rows = x.shape
-    width = grad.shape[1]
+def weight_grad_kernel(*refs):
+    *ins, o_ref = refs
+    total = tn(ins[0][...], ins[1][...])
+    for i in range(2, len(ins), 2):
+        total = total + tn(ins[i][...], ins[i + 1][...])
+    o_ref[...] = total.astype(BF)
+
+
+def weight_grad(pairs, columns_at_once):
+    rows, width = pairs[0][0].shape[1], pairs[0][1].shape[1]
+    specs = []
+    for x, grad in pairs:
+        specs.append(pl.BlockSpec((x.shape[0], columns_at_once), lambda i: (0, i)))
+        specs.append(pl.BlockSpec(grad.shape, lambda i: (0, 0)))
     return pl.pallas_call(
         weight_grad_kernel,
         grid=(rows // columns_at_once,),
-        in_specs=[
-            pl.BlockSpec((tokens, columns_at_once), lambda i: (0, i)),
-            pl.BlockSpec((tokens, width), lambda i: (0, 0)),
-        ],
+        in_specs=specs,
         out_specs=pl.BlockSpec((columns_at_once, width), lambda i: (i, 0)),
         out_shape=jax.ShapeDtypeStruct((rows, width), BF),
-        compiler_params=pltpu.CompilerParams(vmem_limit_bytes=40 * 2**20),
+        compiler_params=pltpu.CompilerParams(
+            vmem_limit_bytes=(40 if width > 768 else 24) * 2**20
+        ),
         cost_estimate=BRIEF,
         name="weight_grad",
-    )(x, grad)
+    )(*[a for pair in pairs for a in pair])
 
 
 GELU_A = 0.7978845608028654
@@ -768,7 +786,7 @@
         return lambda g: (g // group_pairs) * 3 * group_pairs + i * group_pairs + g % group_pairs
 
     grad_dealt = grad_low.reshape(2, devices, -1, width).swapaxes(0, 1)
-    grad_spread = to_all(tied(grad_dealt, h1))
+    grad_spread = to_all(grad_dealt)
 
     wgu = lax.all_gather(
         jnp.concatenate([ffn_gate[0], ffn_up[0]], axis=1), "dp", axis=0, tiled=True
@@ -781,7 +799,6 @@
         (qkv, of_pair(2)),
         lens,
         True,
-        0,
         length,
         length,
         pairs,
@@ -808,7 +825,6 @@
             (cross_kv, pairs),
             later(lens, c * half),
             False,
-            0,
             half,
             key_count,
             pairs,
@@ -825,7 +841,14 @@
         )
 
     x1_a, h2_a, query_a = forward_middle(0)
-    cross_kv = nn(memory_row, ckv).astype(BF)
+    (cross_kv,) = by_tokens(
+        product_kernel,
+        key_count,
+        [(memory_row, 0)],
+        [(ckv, ckv.shape, (0, 0))],
+        [(2 * width, BF)],
+        "memory",
+    )
     cross_a, log_cross_a = forward_cross(0, query_a)
     x2_a, h3_a = forward_outer(x1_a, cross_a)
     spread_a = to_all(dealt(tied(h3_a, grad_spread)))
@@ -839,24 +862,23 @@
     spread_b = to_all(dealt(h3_b))
 
     modes = len(routed_a)
-    fed_a = feed(0, tied(routed_a, h3_b), grad_parts, wgu, wd, ())
+    routed_b = to_mode(spread_b, source)
+    fed_a = feed(0, tied(routed_a, routed_b), grad_parts, wgu, wd, ())
     y_a, dh_a, kept_a = fed_a[:modes], fed_a[modes : 2 * modes], fed_a[2 * modes :]
     back_a = put_back(swap_modes(dh_a), source)
-    routed_b = to_mode(tied(spread_b, dh_a[0]), source)
     routed_b, back_a = lax.optimization_barrier((routed_b, back_a))
-    home_a = to_all(back_a)
+    home_a = to_all(back_a).reshape(half, width)
     fed_b = feed(1, routed_b, grad_parts, wgu, wd, y_a + kept_a)
-    home_a = home_a.reshape(half, width)
     y, dh_b = fed_b[:modes], fed_b[modes : 2 * modes]
     hidden, dgu, routed_h, routed_grad = fed_b[2 * modes :]
     back_b = swap_modes(dh_b)
-    grad_wd = weight_grad(tied(hidden, home_a), routed_grad, 512)
-    back_b = put_back(tied(back_b, grad_wd), source)
-    grad_wgu = weight_grad(routed_h, tied(dgu, back_b), 256)
+    grad_wd = weight_grad([(tied(hidden, home_a), routed_grad)], 512)
+    grad_wgu = weight_grad([(routed_h, dgu)], 256)
+    back_b = put_back(tied(back_b, (grad_wd, grad_wgu)), source)
     sum_wgu = lax.psum_scatter(grad_wgu, "dp", scatter_dimension=0, tiled=True)
     sum_wd = lax.psum_scatter(grad_wd, "dp", scatter_dimension=0, tiled=True)
     home_b = to_all(back_b).reshape(half, width)
-    home_a = tied(home_a, grad_wgu)
+    home_a = tied(home_a, back_b)
     y_mode = swap_modes(tied(y, back_b))
 
     def back_outer(c, dh, x2):
@@ -928,11 +950,11 @@
     dx1, d1, do1, dgain_cross_b = back_middle(1, dcq_b, x1_b, dx2_b, halves)
     cross_pair = scatter_pairs(
         [
-            (tn(h2_a, dcq_a) + tn(h2_b, dcq_b)).astype(BF),
-            tn(memory_row, dck).astype(BF),
-            tn(memory_row, dcv).astype(BF),
-            (tn(cross_a, d2_a) + tn(cross_b, d2_b)).astype(BF),
-            tn(mixed, d1).astype(BF),
+            weight_grad([(h2_a, dcq_a), (h2_b, dcq_b)], 256),
+            weight_grad([(memory_row, dck)], 256),
+            weight_grad([(memory_row, dcv)], 256),
+            weight_grad([(cross_a, d2_a), (cross_b, d2_b)], 256),
+            weight_grad([(mixed, d1)], 256),
         ]
     )
     do1, cross_pair = lax.optimization_barrier((do1, cross_pair))

time: 565 us -> 543 us (0.961)
  Pallas kernels: 165 us -> 205 us
  waiting for transfers between devices: 158 us -> 131 us
  starting transfers between devices: 102 us -> 89.7 us
  matrix products: 22.7 us -> 11 us
    all_gather x1, waiting for transfers between devices: 30.2 us -> 2.34 us  [on_device(): lax.all_gather(jnp.concatenate([ffn_gate[0], ffn_up[0]], axis=1), 'dp', a...]
    pallas_call x3, Pallas kernels: 34.2 us -> 56.7 us  [attend_backward(): pl.pallas_call(functools.partial(attend_bwd_kernel, causal, start, had),...]
    all_to_all x7, waiting for transfers between devices: 19.6 us -> 38.7 us  [to_all(): return lax.all_to_all(value, ALL, 0, 0, tiled=True)]
    ppermute x39, waiting for transfers between devices: 108 us -> 88.9 us  [swap(): return lax.ppermute(value, ALL, [(i, i ^ j) for i in range(count)])]
    ppermute x39, starting transfers between devices: 61.5 us -> 49.2 us  [swap(): return lax.ppermute(value, ALL, [(i, i ^ j) for i in range(count)])]
    pallas_call x2 -> x7, Pallas kernels: 15.2 us -> 23.8 us  [weight_grad(): pl.pallas_call(weight_grad_kernel, grid=(rows // columns_at_once,), in_sp...]
    pallas_call x3, Pallas kernels: 29.2 us -> 36.9 us  [attend_forward(): pl.pallas_call(functools.partial(attend_fwd_kernel, causal), grid_spec=pl...]
    dot_general x10 -> x3, matrix products: 13.4 us -> 5.9 us  [tn(): lax.dot_general(left, right, (((0,), (0,)), ((), ())), preferred_element_...]
  transfers between devices with their start and end apart: 51 -> 51, of which waited for: 24 -> 21; matrix products, arithmetic and copies ran while one was open for 9% -> 7% of each run, Pallas kernels for 29% -> 33%
where the time goes in v4:
time: 543 us; the launch traced here: 538 us
  Pallas kernels  205 us (38%)
  waiting for transfers between devices  131 us (24%)
  starting transfers between devices  89.7 us (17%)
  local copies, waits for them, and re-layouts  63.4 us (12%)
  other arithmetic  22.5 us (4%)
  between operations  15.4 us (3%)
  matrix products  11 us (2%)
    ppermute x39, waiting for transfers between devices, swap(): return lax.ppermute(value, ALL, [(i, i ^ j) for i in range(count)])  88.9 us
    unnamed x244, local copies, waits for them, and re-layouts  57.3 us
    pallas_call x3, Pallas kernels, attend_backward(): pl.pallas_call(functools.partial(attend_bwd_kernel, causal, start, had),...  56.7 us
    ppermute x39, starting transfers between devices, swap(): return lax.ppermute(value, ALL, [(i, i ^ j) for i in range(count)])  49.2 us
    all_to_all x7, waiting for transfers between devices, to_all(): return lax.all_to_all(value, ALL, 0, 0, tiled=True)  38.7 us
    pallas_call x3, Pallas kernels, attend_forward(): pl.pallas_call(functools.partial(attend_fwd_kernel, causal), grid_spec=pl...  36.9 us
    pallas_call x2, Pallas kernels, feed(): pl.pallas_call(functools.partial(feed_kernel, groups, ff, 512), grid=(1,)...  36.6 us
    pallas_call x11, Pallas kernels, by_tokens(): pl.pallas_call(run, grid=(steps,), in_specs=[rows(a.shape[1], first) for...  32.7 us
  transfers between devices with their start and end apart: 51, of which 21 were waited for; matrix products, arithmetic and copies ran while one was open for 7% of the time, Pallas kernels for 33%

profile of v4, /device:TPU:0, one launch (start us, length us, event | category | flops | bytes accessed | tf_op | source)
XLA Modules:
  0.0 537.7 jit_solution(2327952602422750465)
XLA Ops:
  13.4 5.1 collective-permute-start.2
  35.4 5.2 all-to-all-start
  40.6 5.1 collective-permute-done.3
  45.7 15.5 %collective-permute-done.4 = bf16[4,24,2432]{2,1,0:T(8,128)(2,1)S(1)} collective-permute-done((bf16[4,24,2432]{2,1,0:T(8,128)(2,1)}, bf16[4,24,2432]{2,1,0:T(8,128)(2,1)S(1)}, u32[]{:S(2)}, u32[]{:S(2)}) %collective-permute-start.4) | collective-permute-done | bytes 466976 | tf_op jit(solution)/shard_map/ppermute | solution.py:555
  61.2 7.0 %collective-permute-done.5 = bf16[4,24,2432]{2,1,0:T(8,128)(2,1)S(1)} collective-permute-done((bf16[4,24,2432]{2,1,0:T(8,128)(2,1)}, bf16[4,24,2432]{2,1,0:T(8,128)(2,1)S(1)}, u32[]{:S(2)}, u32[]{:S(2)}) %collective-permute-start.5) | collective-permute-done | bytes 466976 | tf_op jit(solution)/shard_map/ppermute | solution.py:555
  74.2 5.3 enter.1
  81.4 21.1 %attend_causal.1 = (bf16[1024,768]{1,0:T(8,128)(2,1)S(1)}, f32[6,2,1024]{2,1,0:T(2,128)S(1)}) custom-call(s32[2]{0:T(128)S(1)} %get-tuple-element.304.lens, bf16[1024,2304]{1,0:T(8,128)(2,1)S(1)} %get-tuple-element.164.q_ref.k_ref.v_ref.refs_0_.refs_1_.refs_2_, bf16[1024,2304]{1,0:T(8,128)(2,1)S(1)} %get-tuple-element.164.q_ref.k_ref.v_ref.refs_0_.refs_1_.refs_2_, ...), custom_call_target="tpu_custom_call" | custom-call | flops 1000000 | bytes 10000 | tf_op jit(solution)/shard_map/attend_causal/pallas_call | solution.py:164
  115.6 7.9 %attend_memory.2 = (bf16[512,768]{1,0:T(8,128)(2,1)S(1)}, f32[6,2,512]{2,1,0:T(2,128)S(1)}) custom-call(s32[2]{0:T(128)S(1)} %get-tuple-element.304.lens, bf16[512,768]{1,0:T(8,128)(2,1)S(1)} %get-tuple-element.169.q_ref.refs_0_, bf16[512,1536]{1,0:T(8,128)(2,1)S(1)} %memory.1.k_ref.v_ref.refs_1_.refs_2_, bf16[512,1536]{1,0:T(8,128)(2,1)S(1)} %memory.1.k_ref.v_ref.refs_1_.refs_2_), custom_call_target="tpu_custom_call" | custom-call | flops 1000000 | bytes 10000 | tf_op jit(solution)/shard_map/attend_memory/pallas_call | solution.py:164
  145.8 7.9 %attend_memory.3 = (bf16[512,768]{1,0:T(8,128)(2,1)S(1)}, f32[6,2,512]{2,1,0:T(2,128)S(1)}) custom-call(s32[2]{0:T(128)S(1)} %get-tuple-element.303.lens, bf16[512,768]{1,0:T(8,128)(2,1)S(1)} %get-tuple-element.175.q_ref.refs_0_, bf16[512,1536]{1,0:T(8,128)(2,1)S(1)} %memory.1.k_ref.v_ref.refs_1_.refs_2_, bf16[512,1536]{1,0:T(8,128)(2,1)S(1)} %memory.1.k_ref.v_ref.refs_1_.refs_2_), custom_call_target="tpu_custom_call" | custom-call | flops 1000000 | bytes 10000 | tf_op jit(solution)/shard_map/attend_memory/pallas_call | solution.py:164
  157.7 5.1 collective-permute-done.9
  178.9 36.5 %all-to-all-done.1.x_ref = bf16[32,16,768]{2,1,0:T(8,128)(2,1)} async-done(((bf16[32,16,768]{2,1,0:T(8,128)(2,1)}), bf16[32,16,768]{2,1,0:T(8,128)(2,1)}, u32[]{:S(2)}, u32[]{:S(2)}) %all-to-all-start.1) | async-done | bytes 786464 | tf_op jit(solution)/shard_map/all_to_all | solution.py:550
  232.7 18.2 %feed.2 = (bf16[2,128,768]{2,1,0:T(8,128)(2,1)}, bf16[2,128,768]{2,1,0:T(8,128)(2,1)}, bf16[2,128,768]{2,1,0:T(8,128)(2,1)}, bf16[2,128,768]{2,1,0:T(8,128)(2,1)...) custom-call(bf16[128,768]{1,0:T(8,128)(2,1)} %bitcast.153, ...), custom_call_target="tpu_custom_call" | custom-call | flops 1000000 | bytes 10000 | tf_op jit(solution)/shard_map/feed/pallas_call | solution.py:429
  258.9 4.7 collective-permute-done.17.refs_2_
  269.6 8.3 %reduce-scatter.5.cloned.1.call-start = ((), (), s32[]{:S(2)}) async-start(), calls=%async_computation.12 | async-start | bytes 3538944 | tf_op jit(solution)/shard_map/reduce_scatter | solution.py:879
  277.9 18.4 %feed.3 = (bf16[2,128,768]{2,1,0:T(8,128)(2,1)}, bf16[2,128,768]{2,1,0:T(8,128)(2,1)}, bf16[2,128,768]{2,1,0:T(8,128)(2,1)}, bf16[2,128,768]{2,1,0:T(8,128)(2,1)...) custom-call(bf16[128,768]{1,0:T(8,128)(2,1)} %bitcast.150, ...), custom_call_target="tpu_custom_call", output_to_operand_aliasing={{0}: (10, {}), {1}: (11, {}), {2}: (12, {}), {3}: (13, {}),... | custom-call | flops 1000000 | bytes 10000 | tf_op jit(solution)/shard_map/feed/pallas_call | solution.py:429
  308.0 10.6 %weight_grad.8 = bf16[768,4096]{1,0:T(8,128)(2,1)S(1)} custom-call(bf16[1024,768]{1,0:T(8,128)(2,1)S(1)} %copy-done.37, bf16[1024,4096]{1,0:T(8,128)(2,1)} %get-tuple-element.227.refs_1_), custom_call_target="tpu_custom_call" | custom-call | flops 1000000 | bytes 10000 | tf_op jit(solution)/shard_map/weight_grad/pallas_call | solution.py:362
  329.4 4.7 collective-permute-done.20.refs_2_
  336.7 4.9 all-to-all-start.4
  352.3 12.4 %attend_memory_back.2 = (bf16[512,768]{1,0:T(8,128)(2,1)S(1)}, f32[512,768]{1,0:T(8,128)S(1)}, f32[512,768]{1,0:T(8,128)S(1)}) custom-call(s32[2]{0:T(128)S(1)} %get-tuple-element.304.lens, bf16[512,768]{1,0:T(8,128)(2,1)S(1)} %copy-done.61, bf16[512,1536]{1,0:T(8,128)(2,1)S(1)} %memory.1.k_ref.v_ref.refs_1_.refs_2_, ...), custom_call_target="tpu_custom_call" | custom-call | flops 1000000 | bytes 10000 | tf_op jit(solution)/shard_map/attend_memory_back/pallas_call | solution.py:195
  384.7 12.8 %attend_memory_back.3 = (bf16[512,768]{1,0:T(8,128)(2,1)S(1)}, bf16[512,768]{1,0:T(8,128)(2,1)S(1)}, bf16[512,768]{1,0:T(8,128)(2,1)S(1)}) custom-call(s32[2]{0:T(128)S(1)} %get-tuple-element.303.lens, bf16[512,768]{1,0:T(8,128)(2,1)S(1)} %copy-done.55, bf16[512,1536]{1,0:T(8,128)(2,1)S(1)} %memory.1.k_ref.v_ref.refs_1_.refs_2_, ...), custom_call_target="tpu_custom_call" | custom-call | flops 1000000 | bytes 10000 | tf_op jit(solution)/shard_map/attend_memory_back/pallas_call | solution.py:195
  413.2 6.2 %all-to-all-start.5 = ((bf16[32,2,16,768]{3,2,1,0:T(8,128)(2,1)}), bf16[32,2,16,768]{3,2,1,0:T(8,128)(2,1)}, u32[]{:S(2)}, u32[]{:S(2)}) async-start(bf16[32,2,16,768]{3,2,1,0:T(8,128)(2,1)} %put.5), calls=%async_computation.5 | async-start | bytes 3145728 | tf_op jit(solution)/shard_map/all_to_all | solution.py:550
  428.3 31.5 %attend_causal_back.1 = (bf16[1024,768]{1,0:T(8,128)(2,1)S(1)}, bf16[1024,768]{1,0:T(8,128)(2,1)S(1)}, bf16[1024,768]{1,0:T(8,128)(2,1)S(1)}) custom-call(s32[2]{0:T(128)S(1)} %get-tuple-element.304.lens, bf16[1024,2304]{1,0:T(8,128)(2,1)S(1)} %bitcast.117, bf16[1024,2304]{1,0:T(8,128)(2,1)S(1)} %bitcast.117, bf16[1024,2304]{1,0:T(8,128)(2,1)S(1)} %bitcast.117, ...), custom_call_target="tpu_custom_call" | custom-call | flops 1000000 | bytes 10000 | tf_op jit(solution)/shard_map/attend_causal_back/pallas_call | solution.py:195
  463.4 8.4 %collective-permute-done.28 = bf16[4,24,3840]{2,1,0:T(8,128)(2,1)S(1)} collective-permute-done((bf16[4,24,3840]{2,1,0:T(8,128)(2,1)S(1)}, bf16[4,24,3840]{2,1,0:T(8,128)(2,1)S(1)}, u32[]{:S(2)}, u32[]{:S(2)}) %collective-permute-start.28) | collective-permute-done | bytes 737312 | tf_op jit(solution)/shard_map/ppermute | solution.py:555
  497.0 7.6 %enter_back.1 = (bf16[1024,768]{1,0:T(8,128)(2,1)}, f32[8,768]{1,0:T(8,128)S(1)}) custom-call(bf16[1024,768]{1,0:T(8,128)(2,1)S(1)} %bitcast.129, f32[1024,768]{1,0:T(8,128)S(1)} %copy-done.29, bf16[1024,768]{1,0:T(8,128)(2,1)S(1)} %copy-done.75, bf16[1024,768]{1,0:T(8,128)(2,1)S(1)} %copy-done.77, bf16[1024,768]{1,0:T(8,128)(2,1)S(1)} %copy-done.79, ...), custom_call_target="tpu_custom_call" | custom-call | flops 1000000 | bytes 10000 | tf_op jit(solution)/shard_map/enter_back/pallas_call | solution.py:328
  (411 shorter events, 251.9 us)
Async XLA Ops:
  7.2 99.3 %all-gather.5.cloned.1.call-start = ((), (), s32[]{:S(2)}) async-start(), calls=%async_computation.9 | async-start | bytes 6082560 | tf_op jit(solution)/shard_map/all_gather | solution.py:769
  10.3 220.0 %all-gather.9.cloned.1.call-start = ((), (), s32[]{:S(2)}) async-start(), calls=%async_computation.13 | async-start | bytes 3538944 | tf_op jit(solution)/shard_map/all_gather | solution.py:794
  11.1 221.6 %all-gather.7.cloned.1.call-start = ((), (), s32[]{:S(2)}) async-start(), calls=%async_computation.10 | async-start | bytes 7077888 | tf_op jit(solution)/shard_map/all_gather | solution.py:791
  32.0 29.2 %collective-permute-start.4 = (bf16[4,24,2432]{2,1,0:T(8,128)(2,1)}, bf16[4,24,2432]{2,1,0:T(8,128)(2,1)S(1)}, u32[]{:S(2)}, u32[]{:S(2)}) collective-permute-start(bf16[4,24,2432]{2,1,0:T(8,128)(2,1)} %get-tuple-element.320), channel_id=1, source_target_pairs={{0,16},{1,17},{2,18},{3,19},{4,20},{5,21},{6,22},{7,23},{8,24},{9,... | collective-permute-start | bytes 1400840 | tf_op jit(solution)/shard_map/ppermute | solution.py:555
  33.7 34.6 %collective-permute-start.5 = (bf16[4,24,2432]{2,1,0:T(8,128)(2,1)}, bf16[4,24,2432]{2,1,0:T(8,128)(2,1)S(1)}, u32[]{:S(2)}, u32[]{:S(2)}) collective-permute-start(bf16[4,24,2432]{2,1,0:T(8,128)(2,1)} %get-tuple-element.320), channel_id=1, source_target_pairs={{0,24},{1,25},{2,26},{3,27},{4,28},{5,29},{6,30},{7,31},{8,16},{9,... | collective-permute-start | bytes 1400840 | tf_op jit(solution)/shard_map/ppermute | solution.py:555
  35.4 92.9 %all-to-all-start = ((bf16[32,2,16,768]{3,2,1,0:T(8,128)(2,1)}), bf16[32,2,16,768]{3,2,1,0:T(8,128)(2,1)}, u32[]{:S(2)}, u32[]{:S(2)}) async-start(bf16[32,2,16,768]{3,2,1,0:T(8,128)(2,1)} %fusion.2), calls=%async_computation | async-start | bytes 3145728 | tf_op jit(solution)/shard_map/all_to_all | solution.py:550
  128.3 39.4 %all-to-all-start.2 = ((bf16[32,16,768]{2,1,0:T(8,128)(2,1)}), bf16[32,16,768]{2,1,0:T(8,128)(2,1)}, u32[]{:S(2)}, u32[]{:S(2)}) async-start(bf16[32,16,768]{2,1,0:T(8,128)(2,1)} %bitcast.148), calls=%async_computation.2 | async-start | bytes 1572864 | tf_op jit(solution)/shard_map/all_to_all | solution.py:550
  137.8 20.0 %collective-permute-start.8 = (bf16[2,8,16,768]{3,2,1,0:T(8,128)(2,1)S(1)}, bf16[2,8,16,768]{3,2,1,0:T(8,128)(2,1)S(1)}, u32[]{:S(2)}, u32[]{:S(2)}) collective-permute-start(bf16[2,8,16,768]{3,2,1,0:T(8,128)(2,1)S(1)} %get-tuple-element.179), channel_id=1, source_target_pairs={{0,16},{1,17},{2,18},{3,19},{4,20},{5,21},{6,22},{7,23},{8,24},{9,... | collective-permute-start | bytes 1179656 | tf_op jit(solution)/shard_map/ppermute | solution.py:555
  139.2 23.6 %collective-permute-start.9 = (bf16[2,8,16,768]{3,2,1,0:T(8,128)(2,1)S(1)}, bf16[2,8,16,768]{3,2,1,0:T(8,128)(2,1)S(1)}, u32[]{:S(2)}, u32[]{:S(2)}) collective-permute-start(bf16[2,8,16,768]{3,2,1,0:T(8,128)(2,1)S(1)} %get-tuple-element.180), channel_id=1, source_target_pairs={{0,24},{1,25},{2,26},{3,27},{4,28},{5,29},{6,30},{7,31},{8,16},{9,... | collective-permute-start | bytes 1179656 | tf_op jit(solution)/shard_map/ppermute | solution.py:555
  167.6 47.7 %all-to-all-start.1 = ((bf16[32,16,768]{2,1,0:T(8,128)(2,1)}), bf16[32,16,768]{2,1,0:T(8,128)(2,1)}, u32[]{:S(2)}, u32[]{:S(2)}) async-start(bf16[32,16,768]{2,1,0:T(8,128)(2,1)} %bitcast.149), calls=%async_computation.1 | async-start | bytes 1572864 | tf_op jit(solution)/shard_map/all_to_all | solution.py:550
  175.4 43.7 %collective-permute-start.13 = (bf16[8,16,768]{2,1,0:T(8,128)(2,1)}, bf16[8,16,768]{2,1,0:T(8,128)(2,1)}, u32[]{:S(2)}, u32[]{:S(2)}) collective-permute-start(bf16[8,16,768]{2,1,0:T(8,128)(2,1)} %get-tuple-element.191), channel_id=1, source_target_pairs={{0,8},{1,9},{2,10},{3,11},{4,12},{5,13},{6,14},{7,15},{8,0},{9,1},... | collective-permute-start | bytes 589832 | tf_op jit(solution)/shard_map/ppermute | solution.py:555
  177.1 44.3 %collective-permute-start.14 = (bf16[8,16,768]{2,1,0:T(8,128)(2,1)}, bf16[8,16,768]{2,1,0:T(8,128)(2,1)}, u32[]{:S(2)}, u32[]{:S(2)}) collective-permute-start(bf16[8,16,768]{2,1,0:T(8,128)(2,1)} %get-tuple-element.192), channel_id=1, source_target_pairs={{0,16},{1,17},{2,18},{3,19},{4,20},{5,21},{6,22},{7,23},{8,24},{9,... | collective-permute-start | bytes 589832 | tf_op jit(solution)/shard_map/ppermute | solution.py:555
  178.6 42.9 %collective-permute-start.15 = (bf16[8,16,768]{2,1,0:T(8,128)(2,1)}, bf16[8,16,768]{2,1,0:T(8,128)(2,1)}, u32[]{:S(2)}, u32[]{:S(2)}) collective-permute-start(bf16[8,16,768]{2,1,0:T(8,128)(2,1)} %get-tuple-element.193), channel_id=1, source_target_pairs={{0,24},{1,25},{2,26},{3,27},{4,28},{5,29},{6,30},{7,31},{8,16},{9,... | collective-permute-start | bytes 589832 | tf_op jit(solution)/shard_map/ppermute | solution.py:555
  266.2 30.1 %all-to-all-start.3 = ((bf16[32,16,768]{2,1,0:T(8,128)(2,1)}), bf16[32,16,768]{2,1,0:T(8,128)(2,1)}, u32[]{:S(2)}, u32[]{:S(2)}) async-start(bf16[32,16,768]{2,1,0:T(8,128)(2,1)} %copy-done.57), calls=%async_computation.3 | async-start | bytes 1572864 | tf_op jit(solution)/shard_map/all_to_all | solution.py:550
  269.6 202.6 %reduce-scatter.5.cloned.1.call-start = ((), (), s32[]{:S(2)}) async-start(), calls=%async_computation.12 | async-start | bytes 3538944 | tf_op jit(solution)/shard_map/reduce_scatter | solution.py:879
  306.2 166.1 %reduce-scatter.3.cloned.1.call-start = ((), (), s32[]{:S(2)}) async-start(), calls=%async_computation.11 | async-start | bytes 7077888 | tf_op jit(solution)/shard_map/reduce_scatter | solution.py:878
  336.7 38.4 %all-to-all-start.4 = ((bf16[32,16,768]{2,1,0:T(8,128)(2,1)}), bf16[32,16,768]{2,1,0:T(8,128)(2,1)}, u32[]{:S(2)}, u32[]{:S(2)}) async-start(bf16[32,16,768]{2,1,0:T(8,128)(2,1)} %copy-done.56), calls=%async_computation.4 | async-start | bytes 1572864 | tf_op jit(solution)/shard_map/all_to_all | solution.py:550
  341.6 33.6 %collective-permute-start.22 = (bf16[2,8,16,768]{3,2,1,0:T(8,128)(2,1)}, bf16[2,8,16,768]{3,2,1,0:T(8,128)(2,1)}, u32[]{:S(2)}, u32[]{:S(2)}) collective-permute-start(bf16[2,8,16,768]{3,2,1,0:T(8,128)(2,1)} %bitcast.168), channel_id=1, source_target_pairs={{0,8},{1,9},{2,10},{3,11},{4,12},{5,13},{6,14},{7,15},{8,0},{9,1},... | collective-permute-start | bytes 1179656 | tf_op jit(solution)/shard_map/ppermute | solution.py:555
  343.3 31.8 %collective-permute-start.23 = (bf16[2,8,16,768]{3,2,1,0:T(8,128)(2,1)}, bf16[2,8,16,768]{3,2,1,0:T(8,128)(2,1)}, u32[]{:S(2)}, u32[]{:S(2)}) collective-permute-start(bf16[2,8,16,768]{3,2,1,0:T(8,128)(2,1)} %bitcast.169), channel_id=1, source_target_pairs={{0,16},{1,17},{2,18},{3,19},{4,20},{5,21},{6,22},{7,23},{8,24},{9,... | collective-permute-start | bytes 1179656 | tf_op jit(solution)/shard_map/ppermute | solution.py:555
  344.8 30.4 %collective-permute-start.24 = (bf16[2,8,16,768]{3,2,1,0:T(8,128)(2,1)}, bf16[2,8,16,768]{3,2,1,0:T(8,128)(2,1)}, u32[]{:S(2)}, u32[]{:S(2)}) collective-permute-start(bf16[2,8,16,768]{3,2,1,0:T(8,128)(2,1)} %bitcast.170), channel_id=1, source_target_pairs={{0,24},{1,25},{2,26},{3,27},{4,28},{5,29},{6,30},{7,31},{8,16},{9,... | collective-permute-start | bytes 1179656 | tf_op jit(solution)/shard_map/ppermute | solution.py:555
  413.2 59.0 %all-to-all-start.5 = ((bf16[32,2,16,768]{3,2,1,0:T(8,128)(2,1)}), bf16[32,2,16,768]{3,2,1,0:T(8,128)(2,1)}, u32[]{:S(2)}, u32[]{:S(2)}) async-start(bf16[32,2,16,768]{3,2,1,0:T(8,128)(2,1)} %put.5), calls=%async_computation.5 | async-start | bytes 3145728 | tf_op jit(solution)/shard_map/all_to_all | solution.py:550
  423.2 40.2 %collective-permute-start.26 = (bf16[4,24,3840]{2,1,0:T(8,128)(2,1)S(1)}, bf16[4,24,3840]{2,1,0:T(8,128)(2,1)S(1)}, u32[]{:S(2)}, u32[]{:S(2)}) collective-permute-start(bf16[4,24,3840]{2,1,0:T(8,128)(2,1)S(1)} %get-tuple-element.308), channel_id=1, source_target_pairs={{0,8},{1,9},{2,10},{3,11},{4,12},{5,13},{6,14},{7,15},{8,0},{9,1},... | collective-permute-start | bytes 2211848 | tf_op jit(solution)/shard_map/ppermute | solution.py:555
  425.2 38.3 %collective-permute-start.27 = (bf16[4,24,3840]{2,1,0:T(8,128)(2,1)S(1)}, bf16[4,24,3840]{2,1,0:T(8,128)(2,1)S(1)}, u32[]{:S(2)}, u32[]{:S(2)}) collective-permute-start(bf16[4,24,3840]{2,1,0:T(8,128)(2,1)S(1)} %get-tuple-element.310), channel_id=1, source_target_pairs={{0,16},{1,17},{2,18},{3,19},{4,20},{5,21},{6,22},{7,23},{8,24},{9,... | collective-permute-start | bytes 2211848 | tf_op jit(solution)/shard_map/ppermute | solution.py:555
  426.6 45.2 %collective-permute-start.28 = (bf16[4,24,3840]{2,1,0:T(8,128)(2,1)S(1)}, bf16[4,24,3840]{2,1,0:T(8,128)(2,1)S(1)}, u32[]{:S(2)}, u32[]{:S(2)}) collective-permute-start(bf16[4,24,3840]{2,1,0:T(8,128)(2,1)S(1)} %get-tuple-element.309), channel_id=1, source_target_pairs={{0,24},{1,25},{2,26},{3,27},{4,28},{5,29},{6,30},{7,31},{8,16},{9,... | collective-permute-start | bytes 2211848 | tf_op jit(solution)/shard_map/ppermute | solution.py:555
  (149 other events, 843.4 us)
Sparse Core Ops, SparseCore 0:
  11.6 91.7 all-gather.4
  105.1 42.3 all-gather.8
  149.7 82.9 all-gather.6
  306.3 41.9 reduce-scatter.4
  350.4 70.2 reduce-scatter.2

commit v5 on v4

--- a/solution.py
+++ b/solution.py
@@ -180,7 +180,7 @@
             jax.ShapeDtypeStruct((length, pairs * PAIR), BF),
             jax.ShapeDtypeStruct((pairs, 2, length), F32),
         ],
-        compiler_params=pltpu.CompilerParams(vmem_limit_bytes=24 * 2**20),
+        compiler_params=pltpu.CompilerParams(vmem_limit_bytes=41943040),
         cost_estimate=BRIEF,
         name="attend_causal" if causal else "attend_memory",
     )(lens, qa, ka, va)
@@ -218,7 +218,7 @@
             jax.ShapeDtypeStruct((key_count, pairs * PAIR), kept),
             jax.ShapeDtypeStruct((key_count, pairs * PAIR), kept),
         ],
-        compiler_params=pltpu.CompilerParams(vmem_limit_bytes=32 * 2**20),
+        compiler_params=pltpu.CompilerParams(vmem_limit_bytes=50331648),
         cost_estimate=BRIEF,
         name="attend_causal_back" if causal else "attend_memory_back",
     )(lens, qa, ka, va, mixed[0], grad[0], lse, *(carried or ()))
@@ -339,7 +339,7 @@
             for n, dtype in outs
         ],
         input_output_aliases={inputs + i: i for i in range(len(kept))},
-        compiler_params=pltpu.CompilerParams(vmem_limit_bytes=24 * 2**20),
+        compiler_params=pltpu.CompilerParams(vmem_limit_bytes=25165824),
         cost_estimate=BRIEF,
         name=name,
     )(*[a for a, _ in blocked], *[a for a, _, _ in whole], *kept)
@@ -366,7 +366,7 @@
         out_specs=pl.BlockSpec((columns_at_once, width), lambda i: (i, 0)),
         out_shape=jax.ShapeDtypeStruct((rows, width), BF),
         compiler_params=pltpu.CompilerParams(
-            vmem_limit_bytes=(40 if width > 768 else 24) * 2**20
+            vmem_limit_bytes=41943040 if width > 768 or rows > 768 else 25165824
         ),
         cost_estimate=BRIEF,
         name="weight_grad",
@@ -440,7 +440,7 @@
         + [jax.ShapeDtypeStruct((part, width), BF)] * groups
         + [jax.ShapeDtypeStruct((2 * tokens, n), BF) for n in wide],
         input_output_aliases={2 * groups + 2 + i: made[i] for i in range(len(kept))},
-        compiler_params=pltpu.CompilerParams(vmem_limit_bytes=VMEM),
+        compiler_params=pltpu.CompilerParams(vmem_limit_bytes=58720256),
         cost_estimate=BRIEF,
         name="feed",
     )(*h_parts, *g_parts, wgu, wd, *kept)
@@ -498,7 +498,7 @@
             out_specs=[whole(shape) for shape in outs],
         ),
         out_shape=[jax.ShapeDtypeStruct(shape, BF) for shape in outs],
-        compiler_params=pltpu.CompilerParams(vmem_limit_bytes=16 * 2**20),
+        compiler_params=pltpu.CompilerParams(vmem_limit_bytes=16777216),
         cost_estimate=pl.CostEstimate(
             flops=0, bytes_accessed=4 * sum(a.size for a in ins), transcendentals=0
         ),
@@ -585,7 +585,7 @@
             out_specs=[whole(shape) for shape in shapes],
         ),
         out_shape=[jax.ShapeDtypeStruct(shape, even.dtype) for shape in shapes],
-        compiler_params=pltpu.CompilerParams(vmem_limit_bytes=28 * 2**20),
+        compiler_params=pltpu.CompilerParams(vmem_limit_bytes=29360128),
         cost_estimate=BRIEF,
         name="place",
     )(number, even, odd)
@@ -668,7 +668,7 @@
             out_specs=[whole(half.shape)] * 2,
         ),
         out_shape=[half, half],
-        compiler_params=pltpu.CompilerParams(vmem_limit_bytes=48 * 2**20),
+        compiler_params=pltpu.CompilerParams(vmem_limit_bytes=50331648),
         cost_estimate=BRIEF,
         name="take",
     )(device_number(), *parts)
@@ -874,7 +874,8 @@
     back_b = swap_modes(dh_b)
     grad_wd = weight_grad([(tied(hidden, home_a), routed_grad)], 512)
     grad_wgu = weight_grad([(routed_h, dgu)], 256)
-    back_b = put_back(tied(back_b, (grad_wd, grad_wgu)), source)
+    grad_wgu, back_b = lax.optimization_barrier((tied(grad_wgu, grad_wd), back_b))
+    back_b = put_back(back_b, source)
     sum_wgu = lax.psum_scatter(grad_wgu, "dp", scatter_dimension=0, tiled=True)
     sum_wd = lax.psum_scatter(grad_wd, "dp", scatter_dimension=0, tiled=True)
     home_b = to_all(back_b).reshape(half, width)

time: 543 us -> 537 us (0.989)
    ppermute x39, waiting for transfers between devices: 88.9 us -> 80.6 us  [swap(): return lax.ppermute(value, ALL, [(i, i ^ j) for i in range(count)])]
    unnamed x244 -> x228, local copies, waits for them, and re-layouts: 57.3 us -> 54.2 us
  transfers between devices with their start and end apart: 51 -> 51, of which waited for: 21 -> 20; matrix products, arithmetic and copies ran while one was open for 7% -> 7% of each run, Pallas kernels for 33% -> 35%
where the time goes in v5:
time: 537 us; the launch traced here: 532 us
  Pallas kernels  210 us (39%)
  waiting for transfers between devices  126 us (23%)
  starting transfers between devices  88.9 us (17%)
  local copies, waits for them, and re-layouts  60.3 us (11%)
  other arithmetic  20.9 us (4%)
  between operations  15.3 us (3%)
  matrix products  11.4 us (2%)
    ppermute x39, waiting for transfers between devices, swap(): return lax.ppermute(value, ALL, [(i, i ^ j) for i in range(count)])  80.6 us
    pallas_call x3, Pallas kernels, attend_backward(): pl.pallas_call(functools.partial(attend_bwd_kernel, causal, start, had),...  60 us
    unnamed x228, local copies, waits for them, and re-layouts  54.2 us
    ppermute x39, starting transfers between devices, swap(): return lax.ppermute(value, ALL, [(i, i ^ j) for i in range(count)])  48.3 us
    all_to_all x7, waiting for transfers between devices, to_all(): return lax.all_to_all(value, ALL, 0, 0, tiled=True)  42 us
    pallas_call x3, Pallas kernels, attend_forward(): pl.pallas_call(functools.partial(attend_fwd_kernel, causal), grid_spec=pl...  36.9 us
    pallas_call x2, Pallas kernels, feed(): pl.pallas_call(functools.partial(feed_kernel, groups, ff, 512), grid=(1,)...  36.4 us
    all_to_all x7, starting transfers between devices, to_all(): return lax.all_to_all(value, ALL, 0, 0, tiled=True)  31.7 us
  transfers between devices with their start and end apart: 51, of which 20 were waited for; matrix products, arithmetic and copies ran while one was open for 7% of the time, Pallas kernels for 35%

profile of v5, /device:TPU:0, one launch (start us, length us, event | category | flops | bytes accessed | tf_op | source)
XLA Modules:
  0.0 532.0 jit_solution(11123887690249341209)
XLA Ops:
  13.4 5.1 collective-permute-start.2
  35.4 5.2 all-to-all-start
  40.6 5.1 collective-permute-done.3
  45.7 15.5 %collective-permute-done.4 = bf16[4,24,2432]{2,1,0:T(8,128)(2,1)S(1)} collective-permute-done((bf16[4,24,2432]{2,1,0:T(8,128)(2,1)}, bf16[4,24,2432]{2,1,0:T(8,128)(2,1)S(1)}, u32[]{:S(2)}, u32[]{:S(2)}) %collective-permute-start.4) | collective-permute-done | bytes 466976 | tf_op jit(solution)/shard_map/ppermute | solution.py:555
  61.2 7.0 %collective-permute-done.5 = bf16[4,24,2432]{2,1,0:T(8,128)(2,1)S(1)} collective-permute-done((bf16[4,24,2432]{2,1,0:T(8,128)(2,1)}, bf16[4,24,2432]{2,1,0:T(8,128)(2,1)S(1)}, u32[]{:S(2)}, u32[]{:S(2)}) %collective-permute-start.5) | collective-permute-done | bytes 466976 | tf_op jit(solution)/shard_map/ppermute | solution.py:555
  74.3 5.3 enter.1
  81.3 21.1 %attend_causal.1 = (bf16[1024,768]{1,0:T(8,128)(2,1)S(1)}, f32[6,2,1024]{2,1,0:T(2,128)S(1)}) custom-call(s32[2]{0:T(128)S(1)} %get-tuple-element.308.lens, bf16[1024,2304]{1,0:T(8,128)(2,1)S(1)} %get-tuple-element.166.q_ref.k_ref.v_ref.refs_0_.refs_1_.refs_2_, bf16[1024,2304]{1,0:T(8,128)(2,1)S(1)} %get-tuple-element.166.q_ref.k_ref.v_ref.refs_0_.refs_1_.refs_2_, ...), custom_call_target="tpu_custom_call" | custom-call | flops 1000000 | bytes 10000 | tf_op jit(solution)/shard_map/attend_causal/pallas_call | solution.py:164
  116.8 7.9 %attend_memory.2 = (bf16[512,768]{1,0:T(8,128)(2,1)S(1)}, f32[6,2,512]{2,1,0:T(2,128)S(1)}) custom-call(s32[2]{0:T(128)S(1)} %get-tuple-element.308.lens, bf16[512,768]{1,0:T(8,128)(2,1)S(1)} %get-tuple-element.171.q_ref.refs_0_, bf16[512,1536]{1,0:T(8,128)(2,1)S(1)} %memory.1.k_ref.v_ref.refs_1_.refs_2_, bf16[512,1536]{1,0:T(8,128)(2,1)S(1)} %memory.1.k_ref.v_ref.refs_1_.refs_2_), custom_call_target="tpu_custom_call" | custom-call | flops 1000000 | bytes 10000 | tf_op jit(solution)/shard_map/attend_memory/pallas_call | solution.py:164
  148.2 7.9 %attend_memory.3 = (bf16[512,768]{1,0:T(8,128)(2,1)S(1)}, f32[6,2,512]{2,1,0:T(2,128)S(1)}) custom-call(s32[2]{0:T(128)S(1)} %get-tuple-element.307.lens, bf16[512,768]{1,0:T(8,128)(2,1)S(1)} %get-tuple-element.177.q_ref.refs_0_, bf16[512,1536]{1,0:T(8,128)(2,1)S(1)} %memory.1.k_ref.v_ref.refs_1_.refs_2_, bf16[512,1536]{1,0:T(8,128)(2,1)S(1)} %memory.1.k_ref.v_ref.refs_1_.refs_2_), custom_call_target="tpu_custom_call" | custom-call | flops 1000000 | bytes 10000 | tf_op jit(solution)/shard_map/attend_memory/pallas_call | solution.py:164
  156.7 7.7 %collective-permute-done.9 = bf16[2,8,16,768]{3,2,1,0:T(8,128)(2,1)S(1)} collective-permute-done((bf16[2,8,16,768]{3,2,1,0:T(8,128)(2,1)S(1)}, bf16[2,8,16,768]{3,2,1,0:T(8,128)(2,1)S(1)}, u32[]{:S(2)}, u32[]{:S(2)}) %collective-permute-start.9) | collective-permute-done | bytes 393248 | tf_op jit(solution)/shard_map/ppermute | solution.py:555
  179.3 36.4 %all-to-all-done.1.x_ref = bf16[32,16,768]{2,1,0:T(8,128)(2,1)} async-done(((bf16[32,16,768]{2,1,0:T(8,128)(2,1)}), bf16[32,16,768]{2,1,0:T(8,128)(2,1)}, u32[]{:S(2)}, u32[]{:S(2)}) %all-to-all-start.1) | async-done | bytes 786464 | tf_op jit(solution)/shard_map/all_to_all | solution.py:550
  231.5 18.0 %feed.2 = (bf16[2,128,768]{2,1,0:T(8,128)(2,1)}, bf16[2,128,768]{2,1,0:T(8,128)(2,1)}, bf16[2,128,768]{2,1,0:T(8,128)(2,1)}, bf16[2,128,768]{2,1,0:T(8,128)(2,1)...) custom-call(bf16[128,768]{1,0:T(8,128)(2,1)} %bitcast.152, ...), custom_call_target="tpu_custom_call" | custom-call | flops 1000000 | bytes 10000 | tf_op jit(solution)/shard_map/feed/pallas_call | solution.py:429
  257.6 4.7 collective-permute-done.17.refs_2_
  267.5 8.3 %reduce-scatter.5.cloned.1.call-start = ((), (), s32[]{:S(2)}) async-start(), calls=%async_computation.12 | async-start | bytes 3538944 | tf_op jit(solution)/shard_map/reduce_scatter | solution.py:880
  275.8 18.4 %feed.3 = (bf16[2,128,768]{2,1,0:T(8,128)(2,1)}, bf16[2,128,768]{2,1,0:T(8,128)(2,1)}, bf16[2,128,768]{2,1,0:T(8,128)(2,1)}, bf16[2,128,768]{2,1,0:T(8,128)(2,1)...) custom-call(bf16[128,768]{1,0:T(8,128)(2,1)} %bitcast.149, ...), custom_call_target="tpu_custom_call", output_to_operand_aliasing={{0}: (10, {}), {1}: (11, {}), {2}: (12, {}), {3}: (13, {}),... | custom-call | flops 1000000 | bytes 10000 | tf_op jit(solution)/shard_map/feed/pallas_call | solution.py:429
  298.7 4.5 weight_grad.8
  308.9 10.6 %weight_grad.7 = bf16[768,4096]{1,0:T(8,128)(2,1)S(1)} custom-call(bf16[1024,768]{1,0:T(8,128)(2,1)S(1)} %copy-done.38, bf16[1024,4096]{1,0:T(8,128)(2,1)} %get-tuple-element.221.refs_1_), custom_call_target="tpu_custom_call" | custom-call | flops 1000000 | bytes 10000 | tf_op jit(solution)/shard_map/weight_grad/pallas_call | solution.py:362
  325.9 5.9 %all-to-all-start.4 = ((bf16[32,16,768]{2,1,0:T(8,128)(2,1)}), bf16[32,16,768]{2,1,0:T(8,128)(2,1)}, u32[]{:S(2)}, u32[]{:S(2)}) async-start(bf16[32,16,768]{2,1,0:T(8,128)(2,1)} %put.4), calls=%async_computation.4 | async-start | bytes 1572864 | tf_op jit(solution)/shard_map/all_to_all | solution.py:550
  340.8 14.3 %attend_memory_back.2 = (bf16[512,768]{1,0:T(8,128)(2,1)S(1)}, f32[512,768]{1,0:T(8,128)S(1)}, f32[512,768]{1,0:T(8,128)}) custom-call(s32[2]{0:T(128)S(1)} %get-tuple-element.308.lens, bf16[512,768]{1,0:T(8,128)(2,1)S(1)} %copy-done.61, bf16[512,1536]{1,0:T(8,128)(2,1)} %copy-done.1, bf16[512,1536]{1,0:T(8,128)(2,1)} %copy-done.1, ...), custom_call_target="tpu_custom_call" | custom-call | flops 1000000 | bytes 10000 | tf_op jit(solution)/shard_map/attend_memory_back/pallas_call | solution.py:195
  371.1 14.0 %attend_memory_back.3 = (bf16[512,768]{1,0:T(8,128)(2,1)S(1)}, bf16[512,768]{1,0:T(8,128)(2,1)S(1)}, bf16[512,768]{1,0:T(8,128)(2,1)S(1)}) custom-call(s32[2]{0:T(128)S(1)} %get-tuple-element.307.lens, bf16[512,768]{1,0:T(8,128)(2,1)S(1)} %copy-done.57, bf16[512,1536]{1,0:T(8,128)(2,1)} %copy-done.1, bf16[512,1536]{1,0:T(8,128)(2,1)} %copy-done.1, ...), custom_call_target="tpu_custom_call" | custom-call | flops 1000000 | bytes 10000 | tf_op jit(solution)/shard_map/attend_memory_back/pallas_call | solution.py:195
  405.6 6.1 %all-to-all-start.5 = ((bf16[32,2,16,768]{3,2,1,0:T(8,128)(2,1)}), bf16[32,2,16,768]{3,2,1,0:T(8,128)(2,1)}, u32[]{:S(2)}, u32[]{:S(2)}) async-start(bf16[32,2,16,768]{3,2,1,0:T(8,128)(2,1)} %put.5), calls=%async_computation.5 | async-start | bytes 3145728 | tf_op jit(solution)/shard_map/all_to_all | solution.py:550
  418.9 31.7 %attend_causal_back.1 = (bf16[1024,768]{1,0:T(8,128)(2,1)S(1)}, bf16[1024,768]{1,0:T(8,128)(2,1)S(1)}, bf16[1024,768]{1,0:T(8,128)(2,1)S(1)}) custom-call(s32[2]{0:T(128)S(1)} %get-tuple-element.308.lens, bf16[1024,2304]{1,0:T(8,128)(2,1)} %copy-done, bf16[1024,2304]{1,0:T(8,128)(2,1)} %copy-done, bf16[1024,2304]{1,0:T(8,128)(2,1)} %copy-done, ...), custom_call_target="tpu_custom_call" | custom-call | flops 1000000 | bytes 10000 | tf_op jit(solution)/shard_map/attend_causal_back/pallas_call | solution.py:195
  454.4 9.2 %collective-permute-done.28 = bf16[4,24,3840]{2,1,0:T(8,128)(2,1)S(1)} collective-permute-done((bf16[4,24,3840]{2,1,0:T(8,128)(2,1)S(1)}, bf16[4,24,3840]{2,1,0:T(8,128)(2,1)S(1)}, u32[]{:S(2)}, u32[]{:S(2)}) %collective-permute-start.28) | collective-permute-done | bytes 737312 | tf_op jit(solution)/shard_map/ppermute | solution.py:555
  491.0 7.6 %enter_back.1 = (bf16[1024,768]{1,0:T(8,128)(2,1)}, f32[8,768]{1,0:T(8,128)S(1)}) custom-call(bf16[1024,768]{1,0:T(8,128)(2,1)S(1)} %bitcast.127, f32[1024,768]{1,0:T(8,128)S(1)} %copy-done.29, bf16[1024,768]{1,0:T(8,128)(2,1)S(1)} %get-tuple-element.291.refs_2_, bf16[1024,768]{1,0:T(8,128)(2,1)S(1)} %copy-done.70, bf16[1024,768]{1,0:T(8,128)(2,1)S(1)} %copy-done.72, ...), custom_call_target="tpu_custom_call" | custom-call | flops 1000000 | bytes 10000 | tf_op jit(solution)/shard_map/enter_back/pallas_call | solution.py:328
  (394 shorter events, 239.1 us)
Async XLA Ops:
  7.2 99.2 %all-gather.5.cloned.1.call-start = ((), (), s32[]{:S(2)}) async-start(), calls=%async_computation.9 | async-start | bytes 6082560 | tf_op jit(solution)/shard_map/all_gather | solution.py:769
  10.3 219.0 %all-gather.9.cloned.1.call-start = ((), (), s32[]{:S(2)}) async-start(), calls=%async_computation.13 | async-start | bytes 3538944 | tf_op jit(solution)/shard_map/all_gather | solution.py:794
  11.1 220.4 %all-gather.7.cloned.1.call-start = ((), (), s32[]{:S(2)}) async-start(), calls=%async_computation.10 | async-start | bytes 7077888 | tf_op jit(solution)/shard_map/all_gather | solution.py:791
  32.0 29.2 %collective-permute-start.4 = (bf16[4,24,2432]{2,1,0:T(8,128)(2,1)}, bf16[4,24,2432]{2,1,0:T(8,128)(2,1)S(1)}, u32[]{:S(2)}, u32[]{:S(2)}) collective-permute-start(bf16[4,24,2432]{2,1,0:T(8,128)(2,1)} %get-tuple-element.324), channel_id=1, source_target_pairs={{0,16},{1,17},{2,18},{3,19},{4,20},{5,21},{6,22},{7,23},{8,24},{9,... | collective-permute-start | bytes 1400840 | tf_op jit(solution)/shard_map/ppermute | solution.py:555
  33.7 34.6 %collective-permute-start.5 = (bf16[4,24,2432]{2,1,0:T(8,128)(2,1)}, bf16[4,24,2432]{2,1,0:T(8,128)(2,1)S(1)}, u32[]{:S(2)}, u32[]{:S(2)}) collective-permute-start(bf16[4,24,2432]{2,1,0:T(8,128)(2,1)} %get-tuple-element.324), channel_id=1, source_target_pairs={{0,24},{1,25},{2,26},{3,27},{4,28},{5,29},{6,30},{7,31},{8,16},{9,... | collective-permute-start | bytes 1400840 | tf_op jit(solution)/shard_map/ppermute | solution.py:555
  35.4 94.1 %all-to-all-start = ((bf16[32,2,16,768]{3,2,1,0:T(8,128)(2,1)}), bf16[32,2,16,768]{3,2,1,0:T(8,128)(2,1)}, u32[]{:S(2)}, u32[]{:S(2)}) async-start(bf16[32,2,16,768]{3,2,1,0:T(8,128)(2,1)} %fusion.2), calls=%async_computation | async-start | bytes 3145728 | tf_op jit(solution)/shard_map/all_to_all | solution.py:550
  129.5 38.7 %all-to-all-start.2 = ((bf16[32,16,768]{2,1,0:T(8,128)(2,1)}), bf16[32,16,768]{2,1,0:T(8,128)(2,1)}, u32[]{:S(2)}, u32[]{:S(2)}) async-start(bf16[32,16,768]{2,1,0:T(8,128)(2,1)} %bitcast.147), calls=%async_computation.2 | async-start | bytes 1572864 | tf_op jit(solution)/shard_map/all_to_all | solution.py:550
  137.3 19.4 %collective-permute-start.7 = (bf16[2,8,16,768]{3,2,1,0:T(8,128)(2,1)S(1)}, bf16[2,8,16,768]{3,2,1,0:T(8,128)(2,1)S(1)}, u32[]{:S(2)}, u32[]{:S(2)}) collective-permute-start(bf16[2,8,16,768]{3,2,1,0:T(8,128)(2,1)S(1)} %get-tuple-element.180), channel_id=1, source_target_pairs={{0,8},{1,9},{2,10},{3,11},{4,12},{5,13},{6,14},{7,15},{8,0},{9,1},... | collective-permute-start | bytes 1179656 | tf_op jit(solution)/shard_map/ppermute | solution.py:555
  140.7 23.8 %collective-permute-start.9 = (bf16[2,8,16,768]{3,2,1,0:T(8,128)(2,1)S(1)}, bf16[2,8,16,768]{3,2,1,0:T(8,128)(2,1)S(1)}, u32[]{:S(2)}, u32[]{:S(2)}) collective-permute-start(bf16[2,8,16,768]{3,2,1,0:T(8,128)(2,1)S(1)} %get-tuple-element.182), channel_id=1, source_target_pairs={{0,24},{1,25},{2,26},{3,27},{4,28},{5,29},{6,30},{7,31},{8,16},{9,... | collective-permute-start | bytes 1179656 | tf_op jit(solution)/shard_map/ppermute | solution.py:555
  168.2 47.4 %all-to-all-start.1 = ((bf16[32,16,768]{2,1,0:T(8,128)(2,1)}), bf16[32,16,768]{2,1,0:T(8,128)(2,1)}, u32[]{:S(2)}, u32[]{:S(2)}) async-start(bf16[32,16,768]{2,1,0:T(8,128)(2,1)} %bitcast.148), calls=%async_computation.1 | async-start | bytes 1572864 | tf_op jit(solution)/shard_map/all_to_all | solution.py:550
  175.8 43.6 %collective-permute-start.13 = (bf16[8,16,768]{2,1,0:T(8,128)(2,1)}, bf16[8,16,768]{2,1,0:T(8,128)(2,1)}, u32[]{:S(2)}, u32[]{:S(2)}) collective-permute-start(bf16[8,16,768]{2,1,0:T(8,128)(2,1)} %get-tuple-element.193), channel_id=1, source_target_pairs={{0,8},{1,9},{2,10},{3,11},{4,12},{5,13},{6,14},{7,15},{8,0},{9,1},... | collective-permute-start | bytes 589832 | tf_op jit(solution)/shard_map/ppermute | solution.py:555
  177.5 44.3 %collective-permute-start.14 = (bf16[8,16,768]{2,1,0:T(8,128)(2,1)}, bf16[8,16,768]{2,1,0:T(8,128)(2,1)}, u32[]{:S(2)}, u32[]{:S(2)}) collective-permute-start(bf16[8,16,768]{2,1,0:T(8,128)(2,1)} %get-tuple-element.194), channel_id=1, source_target_pairs={{0,16},{1,17},{2,18},{3,19},{4,20},{5,21},{6,22},{7,23},{8,24},{9,... | collective-permute-start | bytes 589832 | tf_op jit(solution)/shard_map/ppermute | solution.py:555
  178.9 42.8 %collective-permute-start.15 = (bf16[8,16,768]{2,1,0:T(8,128)(2,1)}, bf16[8,16,768]{2,1,0:T(8,128)(2,1)}, u32[]{:S(2)}, u32[]{:S(2)}) collective-permute-start(bf16[8,16,768]{2,1,0:T(8,128)(2,1)} %get-tuple-element.195), channel_id=1, source_target_pairs={{0,24},{1,25},{2,26},{3,27},{4,28},{5,29},{6,30},{7,31},{8,16},{9,... | collective-permute-start | bytes 589832 | tf_op jit(solution)/shard_map/ppermute | solution.py:555
  264.9 29.3 %all-to-all-start.3 = ((bf16[32,16,768]{2,1,0:T(8,128)(2,1)}), bf16[32,16,768]{2,1,0:T(8,128)(2,1)S(1)}, u32[]{:S(2)}, u32[]{:S(2)}) async-start(bf16[32,16,768]{2,1,0:T(8,128)(2,1)} %put.3), calls=%async_computation.3 | async-start | bytes 1572864 | tf_op jit(solution)/shard_map/all_to_all | solution.py:550
  267.5 199.9 %reduce-scatter.5.cloned.1.call-start = ((), (), s32[]{:S(2)}) async-start(), calls=%async_computation.12 | async-start | bytes 3538944 | tf_op jit(solution)/shard_map/reduce_scatter | solution.py:880
  304.9 162.5 %reduce-scatter.3.cloned.1.call-start = ((), (), s32[]{:S(2)}) async-start(), calls=%async_computation.11 | async-start | bytes 7077888 | tf_op jit(solution)/shard_map/reduce_scatter | solution.py:879
  325.9 37.8 %all-to-all-start.4 = ((bf16[32,16,768]{2,1,0:T(8,128)(2,1)}), bf16[32,16,768]{2,1,0:T(8,128)(2,1)}, u32[]{:S(2)}, u32[]{:S(2)}) async-start(bf16[32,16,768]{2,1,0:T(8,128)(2,1)} %put.4), calls=%async_computation.4 | async-start | bytes 1572864 | tf_op jit(solution)/shard_map/all_to_all | solution.py:550
  331.8 31.9 %collective-permute-start.22 = (bf16[2,8,16,768]{3,2,1,0:T(8,128)(2,1)}, bf16[2,8,16,768]{3,2,1,0:T(8,128)(2,1)}, u32[]{:S(2)}, u32[]{:S(2)}) collective-permute-start(bf16[2,8,16,768]{3,2,1,0:T(8,128)(2,1)} %bitcast.54), channel_id=1, source_target_pairs={{0,8},{1,9},{2,10},{3,11},{4,12},{5,13},{6,14},{7,15},{8,0},{9,1},... | collective-permute-start | bytes 1179656 | tf_op jit(solution)/shard_map/ppermute | solution.py:555
  333.6 30.1 %collective-permute-start.23 = (bf16[2,8,16,768]{3,2,1,0:T(8,128)(2,1)}, bf16[2,8,16,768]{3,2,1,0:T(8,128)(2,1)}, u32[]{:S(2)}, u32[]{:S(2)}) collective-permute-start(bf16[2,8,16,768]{3,2,1,0:T(8,128)(2,1)} %bitcast.55), channel_id=1, source_target_pairs={{0,16},{1,17},{2,18},{3,19},{4,20},{5,21},{6,22},{7,23},{8,24},{9,... | collective-permute-start | bytes 1179656 | tf_op jit(solution)/shard_map/ppermute | solution.py:555
  335.1 28.6 %collective-permute-start.24 = (bf16[2,8,16,768]{3,2,1,0:T(8,128)(2,1)}, bf16[2,8,16,768]{3,2,1,0:T(8,128)(2,1)}, u32[]{:S(2)}, u32[]{:S(2)}) collective-permute-start(bf16[2,8,16,768]{3,2,1,0:T(8,128)(2,1)} %bitcast.56), channel_id=1, source_target_pairs={{0,24},{1,25},{2,26},{3,27},{4,28},{5,29},{6,30},{7,31},{8,16},{9,... | collective-permute-start | bytes 1179656 | tf_op jit(solution)/shard_map/ppermute | solution.py:555
  405.6 61.8 %all-to-all-start.5 = ((bf16[32,2,16,768]{3,2,1,0:T(8,128)(2,1)}), bf16[32,2,16,768]{3,2,1,0:T(8,128)(2,1)}, u32[]{:S(2)}, u32[]{:S(2)}) async-start(bf16[32,2,16,768]{3,2,1,0:T(8,128)(2,1)} %put.5), calls=%async_computation.5 | async-start | bytes 3145728 | tf_op jit(solution)/shard_map/all_to_all | solution.py:550
  415.4 37.6 %collective-permute-start.26 = (bf16[4,24,3840]{2,1,0:T(8,128)(2,1)S(1)}, bf16[4,24,3840]{2,1,0:T(8,128)(2,1)S(1)}, u32[]{:S(2)}, u32[]{:S(2)}) collective-permute-start(bf16[4,24,3840]{2,1,0:T(8,128)(2,1)S(1)} %get-tuple-element.312), channel_id=1, source_target_pairs={{0,8},{1,9},{2,10},{3,11},{4,12},{5,13},{6,14},{7,15},{8,0},{9,1},... | collective-permute-start | bytes 2211848 | tf_op jit(solution)/shard_map/ppermute | solution.py:555
  417.3 37.1 %collective-permute-start.27 = (bf16[4,24,3840]{2,1,0:T(8,128)(2,1)S(1)}, bf16[4,24,3840]{2,1,0:T(8,128)(2,1)S(1)}, u32[]{:S(2)}, u32[]{:S(2)}) collective-permute-start(bf16[4,24,3840]{2,1,0:T(8,128)(2,1)S(1)} %get-tuple-element.314), channel_id=1, source_target_pairs={{0,16},{1,17},{2,18},{3,19},{4,20},{5,21},{6,22},{7,23},{8,24},{9,... | collective-permute-start | bytes 2211848 | tf_op jit(solution)/shard_map/ppermute | solution.py:555
  418.8 44.9 %collective-permute-start.28 = (bf16[4,24,3840]{2,1,0:T(8,128)(2,1)S(1)}, bf16[4,24,3840]{2,1,0:T(8,128)(2,1)S(1)}, u32[]{:S(2)}, u32[]{:S(2)}) collective-permute-start(bf16[4,24,3840]{2,1,0:T(8,128)(2,1)S(1)} %get-tuple-element.313), channel_id=1, source_target_pairs={{0,24},{1,25},{2,26},{3,27},{4,28},{5,29},{6,30},{7,31},{8,16},{9,... | collective-permute-start | bytes 2211848 | tf_op jit(solution)/shard_map/ppermute | solution.py:555
  (141 other events, 909.3 us)
Sparse Core Ops, SparseCore 0:
  11.6 91.7 all-gather.4
  105.1 40.4 all-gather.8
  147.8 83.6 all-gather.6
  305.1 50.0 reduce-scatter.4
  357.3 90.6 reduce-scatter.2

commit v6 on v5

--- a/solution.py
+++ b/solution.py
@@ -15,6 +15,7 @@
 SCALE = HEAD_DIM ** -0.5
 QB = 256
 AB = 512
+FS = 512
 ALL = ("mode", "dp")
 BF = jnp.bfloat16
 F32 = jnp.float32
@@ -377,38 +378,43 @@
 GELU_B = 0.044715
 
 
-def feed_kernel(groups, ff, step, *refs):
+def feed_kernel(groups, *refs):
     h_refs, g_refs, (gu_ref, down_ref) = refs[:groups], refs[groups : 2 * groups], refs[2 * groups : 2 * groups + 2]
-    outs = refs[-2 * groups - 4 :]
+    outs, (y_sum, dh_sum) = refs[-2 * groups - 6 : -2], refs[-2:]
     y_refs, dh_refs, (hid_ref, dgu_ref, h_ref, g_ref) = outs[:groups], outs[groups:-4], outs[-4:]
     part = h_refs[0].shape[0]
-    for j in range(groups):
-        h_ref[pl.ds(j * part, part), :] = h_refs[j][...]
-        g_ref[pl.ds(j * part, part), :] = g_refs[j][0]
-    y, dh = 0.0, 0.0
-    for c in range(0, ff, step):
-        wg = gu_ref[:, pl.ds(c, step)]
-        wu = gu_ref[:, pl.ds(ff + c, step)]
-        wd = down_ref[pl.ds(c, step), :]
-        gate, up, dhid = nn(h_ref[...], wg), nn(h_ref[...], wu), nt(g_ref[...], wd)
-        square = gate * gate
-        th = jnp.tanh(gate * (GELU_A + (GELU_A * GELU_B) * square))
-        half = 0.5 + 0.5 * th
-        act = gate * half
-        slope = half + (0.5 * gate) * (1.0 - th * th) * (
-            GELU_A + (3.0 * GELU_A * GELU_B) * square
-        )
-        hidden = (act * up).astype(BF)
-        dgate = (dhid * up * slope).astype(BF)
-        dup = (dhid * act).astype(BF)
-        hid_ref[:, pl.ds(c, step)] = hidden
-        dgu_ref[:, pl.ds(c, step)] = dgate
-        dgu_ref[:, pl.ds(ff + c, step)] = dup
-        y = y + nn(hidden, wd)
-        dh = dh + nt(dgate, wg) + nt(dup, wu)
-    for j in range(groups):
-        y_refs[j][0] = y[j * part : (j + 1) * part].astype(BF)
-        dh_refs[j][...] = dh[j * part : (j + 1) * part].astype(BF)
+    step = down_ref.shape[0]
+
+    @pl.when(pl.program_id(0) == 0)
+    def _():
+        for j in range(groups):
+            h_ref[pl.ds(j * part, part), :] = h_refs[j][...]
+            g_ref[pl.ds(j * part, part), :] = g_refs[j][0]
+        y_sum[...] = jnp.zeros_like(y_sum)
+        dh_sum[...] = jnp.zeros_like(dh_sum)
+
+    wg, wu, wd = gu_ref[:, pl.ds(0, step)], gu_ref[:, pl.ds(step, step)], down_ref[...]
+    gate, up, dhid = nn(h_ref[...], wg), nn(h_ref[...], wu), nt(g_ref[...], wd)
+    square = gate * gate
+    th = jnp.tanh(gate * (GELU_A + (GELU_A * GELU_B) * square))
+    half = 0.5 + 0.5 * th
+    act = gate * half
+    slope = half + (0.5 * gate) * (1.0 - th * th) * (GELU_A + (3.0 * GELU_A * GELU_B) * square)
+    hidden = (act * up).astype(BF)
+    dgate = (dhid * up * slope).astype(BF)
+    dup = (dhid * act).astype(BF)
+    hid_ref[...] = hidden
+    dgu_ref[:, pl.ds(0, step)] = dgate
+    dgu_ref[:, pl.ds(step, step)] = dup
+    y_sum[...] += nn(hidden, wd)
+    dh_sum[...] += nt(dgate, wg) + nt(dup, wu)
+
+    @pl.when(pl.program_id(0) == pl.num_programs(0) - 1)
+    def _():
+        for j in range(groups):
+            at = pl.ds(j * part, part)
+            y_refs[j][0] = y_sum[at, :].astype(BF)
+            dh_refs[j][...] = dh_sum[at, :].astype(BF)
 
 
 def feed(c, h_parts, g_parts, wgu, wd, kept):
@@ -420,27 +426,33 @@
     def whole(a):
         return pl.BlockSpec(a.shape, lambda i: (0,) * a.ndim)
 
-    def halves(n):
-        return pl.BlockSpec((tokens, n), lambda i: (c, 0))
-
-    wide = (ff, 2 * ff, width, width)
+    def halves(n, columns_at_once):
+        if columns_at_once == n:
+            return pl.BlockSpec((tokens, n), lambda i: (c, 0))
+        return pl.BlockSpec((tokens, columns_at_once), lambda i: (c, i))
+
+    wide = ((ff, FS), (2 * ff, 2 * FS), (width, width), (width, width))
     of_half = pl.BlockSpec((1, part, width), lambda i: (c, 0, 0))
     made = [0 + i for i in range(groups)] + [2 * groups + i for i in range(len(wide))]
     return pl.pallas_call(
-        functools.partial(feed_kernel, groups, ff, 512),
-        grid=(1,),
+        functools.partial(feed_kernel, groups),
+        grid=(ff // FS,),
         in_specs=[whole(h) for h in h_parts]
         + [of_half] * groups
-        + [whole(wgu), whole(wd)]
+        + [
+            pl.BlockSpec((width, 2 * FS), lambda i: (0, i)),
+            pl.BlockSpec((FS, width), lambda i: (i, 0)),
+        ]
         + [pl.BlockSpec(memory_space=pl.ANY)] * len(kept),
         out_specs=[of_half] * groups
         + [whole(h) for h in h_parts]
-        + [halves(n) for n in wide],
+        + [halves(*n) for n in wide],
         out_shape=[jax.ShapeDtypeStruct((2, part, width), BF)] * groups
         + [jax.ShapeDtypeStruct((part, width), BF)] * groups
-        + [jax.ShapeDtypeStruct((2 * tokens, n), BF) for n in wide],
+        + [jax.ShapeDtypeStruct((2 * tokens, n), BF) for n, _ in wide],
+        scratch_shapes=[pltpu.VMEM((tokens, width), F32)] * 2,
         input_output_aliases={2 * groups + 2 + i: made[i] for i in range(len(kept))},
-        compiler_params=pltpu.CompilerParams(vmem_limit_bytes=58720256),
+        compiler_params=pltpu.CompilerParams(vmem_limit_bytes=VMEM),
         cost_estimate=BRIEF,
         name="feed",
     )(*h_parts, *g_parts, wgu, wd, *kept)
@@ -789,7 +801,12 @@
     grad_spread = to_all(grad_dealt)
 
     wgu = lax.all_gather(
-        jnp.concatenate([ffn_gate[0], ffn_up[0]], axis=1), "dp", axis=0, tiled=True
+        jnp.concatenate(
+            [a[0][:, i : i + FS] for i in range(0, ff, FS) for a in (ffn_gate, ffn_up)], axis=1
+        ),
+        "dp",
+        axis=0,
+        tiled=True,
     )
     wd = lax.all_gather(ffn_down[0], "dp", axis=0, tiled=True)
 
@@ -988,6 +1005,10 @@
     y = y_home.swapaxes(0, 1).reshape(length, width)
     result = jnp.where(valid, jnp.concatenate([x2_a, x2_b]) + y.astype(F32), 0.0).astype(BF)
 
+    def turns(which):
+        picked = [sum_wgu[:, i : i + FS] for i in range(which * FS, 2 * ff, 2 * FS)]
+        return jnp.concatenate(picked, axis=1).astype(F32)[None]
+
     def block(value, i):
         return value[:, i * width : (i + 1) * width]
 
@@ -1006,8 +1027,8 @@
         block(cross_sum, 3),
         gain_sums[1],
         gain_sums[2],
-        sum_wgu[:, :ff].astype(F32)[None],
-        sum_wgu[:, ff:].astype(F32)[None],
+        turns(0),
+        turns(1),
         sum_wd.astype(F32)[None],
     )
 

time: 537 us -> 531 us (0.989)
  Pallas kernels: 210 us -> 204 us
  starting transfers between devices: 88.9 us -> 83.3 us
    reduce_scatter x1, starting transfers between devices: 8.3 us -> 0.04 us  [on_device(): sum_wd = lax.psum_scatter(grad_wd, 'dp', scatter_dimension=0, tiled=True)]
    unnamed x228 -> x249, local copies, waits for them, and re-layouts: 54.2 us -> 57.4 us
  transfers between devices with their start and end apart: 51 -> 51, of which waited for: 20 -> 18; matrix products, arithmetic and copies ran while one was open for 7% -> 7% of each run, Pallas kernels for 35% -> 34%
where the time goes in v6:
time: 531 us; the launch traced here: 525 us
  Pallas kernels  204 us (38%)
  waiting for transfers between devices  125 us (24%)
  starting transfers between devices  83.3 us (16%)
  local copies, waits for them, and re-layouts  64.8 us (12%)
  other arithmetic  20.5 us (4%)
  between operations  15.4 us (3%)
  matrix products  11.4 us (2%)
    ppermute x39, waiting for transfers between devices, swap(): return lax.ppermute(value, ALL, [(i, i ^ j) for i in range(count)])  80.9 us
    pallas_call x3, Pallas kernels, attend_backward(): pl.pallas_call(functools.partial(attend_bwd_kernel, causal, start, had),...  59.8 us
    unnamed x249, local copies, waits for them, and re-layouts  57.4 us
    ppermute x39, starting transfers between devices, swap(): return lax.ppermute(value, ALL, [(i, i ^ j) for i in range(count)])  51.1 us
    all_to_all x7, waiting for transfers between devices, to_all(): return lax.all_to_all(value, ALL, 0, 0, tiled=True)  43.2 us
    pallas_call x3, Pallas kernels, attend_forward(): pl.pallas_call(functools.partial(attend_fwd_kernel, causal), grid_spec=pl...  36.9 us
    pallas_call x2, Pallas kernels, feed(): pl.pallas_call(functools.partial(feed_kernel, groups), grid=(ff // FS,),...  32.5 us
    pallas_call x11, Pallas kernels, by_tokens(): pl.pallas_call(run, grid=(steps,), in_specs=[rows(a.shape[1], first) for...  32.1 us
  transfers between devices with their start and end apart: 51, of which 18 were waited for; matrix products, arithmetic and copies ran while one was open for 7% of the time, Pallas kernels for 34%

profile of v6, /device:TPU:0, one launch (start us, length us, event | category | flops | bytes accessed | tf_op | source)
XLA Modules:
  0.0 524.8 jit_solution(10942966668435595837)
XLA Ops:
  15.0 5.1 collective-permute-start.2
  27.6 5.1 collective-permute-done.1
  42.8 8.8 %collective-permute-done.3 = bf16[4,24,2432]{2,1,0:T(8,128)(2,1)S(1)} collective-permute-done((bf16[4,24,2432]{2,1,0:T(8,128)(2,1)}, bf16[4,24,2432]{2,1,0:T(8,128)(2,1)S(1)}, u32[]{:S(2)}, u32[]{:S(2)}) %collective-permute-start.3) | collective-permute-done | bytes 466976 | tf_op jit(solution)/shard_map/ppermute | solution.py:567
  51.6 10.4 %collective-permute-done.4 = bf16[4,24,2432]{2,1,0:T(8,128)(2,1)S(1)} collective-permute-done((bf16[4,24,2432]{2,1,0:T(8,128)(2,1)}, bf16[4,24,2432]{2,1,0:T(8,128)(2,1)S(1)}, u32[]{:S(2)}, u32[]{:S(2)}) %collective-permute-start.4) | collective-permute-done | bytes 466976 | tf_op jit(solution)/shard_map/ppermute | solution.py:567
  62.0 8.1 %collective-permute-done.5 = bf16[4,24,2432]{2,1,0:T(8,128)(2,1)} collective-permute-done((bf16[4,24,2432]{2,1,0:T(8,128)(2,1)}, bf16[4,24,2432]{2,1,0:T(8,128)(2,1)}, u32[]{:S(2)}, u32[]{:S(2)}) %collective-permute-start.5) | collective-permute-done | bytes 466976 | tf_op jit(solution)/shard_map/ppermute | solution.py:567
  77.2 5.3 %enter.1 = (bf16[1024,768]{1,0:T(8,128)(2,1)S(1)}, bf16[1024,2304]{1,0:T(8,128)(2,1)S(1)}, f32[8,768]{1,0:T(8,128)S(1)}) custom-call(bf16[1024,768]{1,0:T(8,128)(2,1)S(1)} %bitcast.134, bf16[768,1152]{1,0:T(8,128)(2,1)S(1)} %bitcast.126, bf16[768,1152]{1,0:T(8,128)(2,1)S(1)} %bitcast.130, bf16[768,128]{1,0:T(8,128)(2,1)S(1)} %bitcast.162), custom_call_target="tpu_custom_call" | custom-call | flops 1000000 | bytes 10000 | tf_op jit(solution)/shard_map/enter/pallas_call | solution.py:329
  83.6 21.1 %attend_causal.1 = (bf16[1024,768]{1,0:T(8,128)(2,1)S(1)}, f32[6,2,1024]{2,1,0:T(2,128)S(1)}) custom-call(s32[2]{0:T(128)S(1)} %get-tuple-element.308.lens, bf16[1024,2304]{1,0:T(8,128)(2,1)S(1)} %get-tuple-element.166.q_ref.k_ref.v_ref.refs_0_.refs_1_.refs_2_, bf16[1024,2304]{1,0:T(8,128)(2,1)S(1)} %get-tuple-element.166.q_ref.k_ref.v_ref.refs_0_.refs_1_.refs_2_, ...), custom_call_target="tpu_custom_call" | custom-call | flops 1000000 | bytes 10000 | tf_op jit(solution)/shard_map/attend_causal/pallas_call | solution.py:165
  118.5 7.9 %attend_memory.2 = (bf16[512,768]{1,0:T(8,128)(2,1)S(1)}, f32[6,2,512]{2,1,0:T(2,128)S(1)}) custom-call(s32[2]{0:T(128)S(1)} %get-tuple-element.308.lens, bf16[512,768]{1,0:T(8,128)(2,1)S(1)} %get-tuple-element.171.q_ref.refs_0_, bf16[512,1536]{1,0:T(8,128)(2,1)S(1)} %memory.1.k_ref.v_ref.refs_1_.refs_2_, bf16[512,1536]{1,0:T(8,128)(2,1)S(1)} %memory.1.k_ref.v_ref.refs_1_.refs_2_), custom_call_target="tpu_custom_call" | custom-call | flops 1000000 | bytes 10000 | tf_op jit(solution)/shard_map/attend_memory/pallas_call | solution.py:165
  131.1 7.6 %all-to-all-start.2 = ((bf16[32,16,768]{2,1,0:T(8,128)(2,1)}), bf16[32,16,768]{2,1,0:T(8,128)(2,1)}, u32[]{:S(2)}, u32[]{:S(2)}) async-start(bf16[32,16,768]{2,1,0:T(8,128)(2,1)} %bitcast.157), calls=%async_computation.2 | async-start | bytes 1572864 | tf_op jit(solution)/shard_map/all_to_all | solution.py:562
  152.9 7.9 %attend_memory.3 = (bf16[512,768]{1,0:T(8,128)(2,1)S(1)}, f32[6,2,512]{2,1,0:T(2,128)S(1)}) custom-call(s32[2]{0:T(128)S(1)} %get-tuple-element.307.lens, bf16[512,768]{1,0:T(8,128)(2,1)S(1)} %get-tuple-element.177.q_ref.refs_0_, bf16[512,1536]{1,0:T(8,128)(2,1)S(1)} %memory.1.k_ref.v_ref.refs_1_.refs_2_, bf16[512,1536]{1,0:T(8,128)(2,1)S(1)} %memory.1.k_ref.v_ref.refs_1_.refs_2_), custom_call_target="tpu_custom_call" | custom-call | flops 1000000 | bytes 10000 | tf_op jit(solution)/shard_map/attend_memory/pallas_call | solution.py:165
  161.4 6.3 %collective-permute-done.9 = bf16[2,8,16,768]{3,2,1,0:T(8,128)(2,1)S(1)} collective-permute-done((bf16[2,8,16,768]{3,2,1,0:T(8,128)(2,1)S(1)}, bf16[2,8,16,768]{3,2,1,0:T(8,128)(2,1)S(1)}, u32[]{:S(2)}, u32[]{:S(2)}) %collective-permute-start.9) | collective-permute-done | bytes 393248 | tf_op jit(solution)/shard_map/ppermute | solution.py:567
  182.6 35.3 %all-to-all-done.1.x_ref = bf16[32,16,768]{2,1,0:T(8,128)(2,1)S(1)} async-done(((bf16[32,16,768]{2,1,0:T(8,128)(2,1)}), bf16[32,16,768]{2,1,0:T(8,128)(2,1)S(1)}, u32[]{:S(2)}, u32[]{:S(2)}) %all-to-all-start.1) | async-done | bytes 786464 | tf_op jit(solution)/shard_map/all_to_all | solution.py:562
  229.5 16.2 %feed.2 = (bf16[2,128,768]{2,1,0:T(8,128)(2,1)}, bf16[2,128,768]{2,1,0:T(8,128)(2,1)}, bf16[2,128,768]{2,1,0:T(8,128)(2,1)}, bf16[2,128,768]{2,1,0:T(8,128)(2,1)...) custom-call(bf16[128,768]{1,0:T(8,128)(2,1)} %bitcast.161, ...), custom_call_target="tpu_custom_call" | custom-call | flops 1000000 | bytes 10000 | tf_op jit(solution)/shard_map/feed/pallas_call | solution.py:437
  255.5 5.2 collective-permute-done.17.refs_2_
  266.0 16.2 %feed.3 = (bf16[2,128,768]{2,1,0:T(8,128)(2,1)}, bf16[2,128,768]{2,1,0:T(8,128)(2,1)}, bf16[2,128,768]{2,1,0:T(8,128)(2,1)}, bf16[2,128,768]{2,1,0:T(8,128)(2,1)...) custom-call(bf16[128,768]{1,0:T(8,128)(2,1)} %bitcast.158, ...), custom_call_target="tpu_custom_call", output_to_operand_aliasing={{0}: (10, {}), {1}: (11, {}), {2}: (12, {}), {3}: (13, {}),... | custom-call | flops 1000000 | bytes 10000 | tf_op jit(solution)/shard_map/feed/pallas_call | solution.py:437
  282.2 5.7 %all-to-all-done.3 = bf16[32,16,768]{2,1,0:T(8,128)(2,1)S(1)} async-done(((bf16[32,16,768]{2,1,0:T(8,128)(2,1)}), bf16[32,16,768]{2,1,0:T(8,128)(2,1)S(1)}, u32[]{:S(2)}, u32[]{:S(2)}) %all-to-all-start.3) | async-done | bytes 786464 | tf_op jit(solution)/shard_map/all_to_all | solution.py:562
  291.8 4.5 weight_grad.8
  302.1 10.6 %weight_grad.7 = bf16[768,4096]{1,0:T(8,128)(2,1)S(1)} custom-call(bf16[1024,768]{1,0:T(8,128)(2,1)S(1)} %copy-done.37, bf16[1024,4096]{1,0:T(8,128)(2,1)} %get-tuple-element.221.refs_1_), custom_call_target="tpu_custom_call" | custom-call | flops 1000000 | bytes 10000 | tf_op jit(solution)/shard_map/weight_grad/pallas_call | solution.py:363
  331.3 14.3 %attend_memory_back.2 = (bf16[512,768]{1,0:T(8,128)(2,1)S(1)}, f32[512,768]{1,0:T(8,128)S(1)}, f32[512,768]{1,0:T(8,128)}) custom-call(s32[2]{0:T(128)S(1)} %get-tuple-element.308.lens, bf16[512,768]{1,0:T(8,128)(2,1)S(1)} %copy-done.60, bf16[512,1536]{1,0:T(8,128)(2,1)} %copy-done.1, bf16[512,1536]{1,0:T(8,128)(2,1)} %copy-done.1, ...), custom_call_target="tpu_custom_call" | custom-call | flops 1000000 | bytes 10000 | tf_op jit(solution)/shard_map/attend_memory_back/pallas_call | solution.py:196
  363.6 13.8 %attend_memory_back.3 = (bf16[512,768]{1,0:T(8,128)(2,1)S(1)}, bf16[512,768]{1,0:T(8,128)(2,1)S(1)}, bf16[512,768]{1,0:T(8,128)(2,1)S(1)}) custom-call(s32[2]{0:T(128)S(1)} %get-tuple-element.307.lens, bf16[512,768]{1,0:T(8,128)(2,1)S(1)} %copy-done.56, bf16[512,1536]{1,0:T(8,128)(2,1)} %copy-done.1, bf16[512,1536]{1,0:T(8,128)(2,1)} %copy-done.1, ...), custom_call_target="tpu_custom_call" | custom-call | flops 1000000 | bytes 10000 | tf_op jit(solution)/shard_map/attend_memory_back/pallas_call | solution.py:196
  396.9 6.2 %all-to-all-start.5 = ((bf16[32,2,16,768]{3,2,1,0:T(8,128)(2,1)}), bf16[32,2,16,768]{3,2,1,0:T(8,128)(2,1)}, u32[]{:S(2)}, u32[]{:S(2)}) async-start(bf16[32,2,16,768]{3,2,1,0:T(8,128)(2,1)} %put.5), calls=%async_computation.5 | async-start | bytes 3145728 | tf_op jit(solution)/shard_map/all_to_all | solution.py:562
  410.3 31.7 %attend_causal_back.1 = (bf16[1024,768]{1,0:T(8,128)(2,1)S(1)}, bf16[1024,768]{1,0:T(8,128)(2,1)S(1)}, bf16[1024,768]{1,0:T(8,128)(2,1)S(1)}) custom-call(s32[2]{0:T(128)S(1)} %get-tuple-element.308.lens, bf16[1024,2304]{1,0:T(8,128)(2,1)} %copy-done, bf16[1024,2304]{1,0:T(8,128)(2,1)} %copy-done, bf16[1024,2304]{1,0:T(8,128)(2,1)} %copy-done, ...), custom_call_target="tpu_custom_call" | custom-call | flops 1000000 | bytes 10000 | tf_op jit(solution)/shard_map/attend_causal_back/pallas_call | solution.py:196
  445.6 10.9 %collective-permute-done.28 = bf16[4,24,3840]{2,1,0:T(8,128)(2,1)S(1)} collective-permute-done((bf16[4,24,3840]{2,1,0:T(8,128)(2,1)S(1)}, bf16[4,24,3840]{2,1,0:T(8,128)(2,1)S(1)}, u32[]{:S(2)}, u32[]{:S(2)}) %collective-permute-start.28) | collective-permute-done | bytes 737312 | tf_op jit(solution)/shard_map/ppermute | solution.py:567
  483.4 7.6 %enter_back.1 = (bf16[1024,768]{1,0:T(8,128)(2,1)}, f32[8,768]{1,0:T(8,128)S(1)}) custom-call(bf16[1024,768]{1,0:T(8,128)(2,1)S(1)} %bitcast.137, f32[1024,768]{1,0:T(8,128)S(1)} %copy-done.29, bf16[1024,768]{1,0:T(8,128)(2,1)S(1)} %copy-done.73, bf16[1024,768]{1,0:T(8,128)(2,1)S(1)} %copy-done.75, bf16[1024,768]{1,0:T(8,128)(2,1)S(1)} %copy-done.77, ...), custom_call_target="tpu_custom_call" | custom-call | flops 1000000 | bytes 10000 | tf_op jit(solution)/shard_map/enter_back/pallas_call | solution.py:329
  (417 shorter events, 237.7 us)
Async XLA Ops:
  7.2 100.8 %all-gather.5.cloned.1.call-start = ((), (), s32[]{:S(2)}) async-start(), calls=%async_computation.9 | async-start | bytes 6082560 | tf_op jit(solution)/shard_map/all_gather | solution.py:781
  10.5 219.0 %all-gather.9.cloned.1.call-start = ((), (), s32[]{:S(2)}) async-start(), calls=%async_computation.13 | async-start | bytes 3538944 | tf_op jit(solution)/shard_map/all_gather | solution.py:811
  11.2 218.2 %all-gather.7.cloned.1.call-start = ((), (), s32[]{:S(2)}) async-start(), calls=%async_computation.10 | async-start | bytes 7077888 | tf_op jit(solution)/shard_map/all_gather | solution.py:803
  35.0 27.0 %collective-permute-start.4 = (bf16[4,24,2432]{2,1,0:T(8,128)(2,1)}, bf16[4,24,2432]{2,1,0:T(8,128)(2,1)S(1)}, u32[]{:S(2)}, u32[]{:S(2)}) collective-permute-start(bf16[4,24,2432]{2,1,0:T(8,128)(2,1)} %get-tuple-element.330), channel_id=1, source_target_pairs={{0,16},{1,17},{2,18},{3,19},{4,20},{5,21},{6,22},{7,23},{8,24},{9,... | collective-permute-start | bytes 1400840 | tf_op jit(solution)/shard_map/ppermute | solution.py:567
  36.6 33.5 %collective-permute-start.5 = (bf16[4,24,2432]{2,1,0:T(8,128)(2,1)}, bf16[4,24,2432]{2,1,0:T(8,128)(2,1)}, u32[]{:S(2)}, u32[]{:S(2)}) collective-permute-start(bf16[4,24,2432]{2,1,0:T(8,128)(2,1)} %get-tuple-element.330), channel_id=1, source_target_pairs={{0,24},{1,25},{2,26},{3,27},{4,28},{5,29},{6,30},{7,31},{8,16},{9,... | collective-permute-start | bytes 1400840 | tf_op jit(solution)/shard_map/ppermute | solution.py:567
  38.4 92.8 %all-to-all-start = ((bf16[32,2,16,768]{3,2,1,0:T(8,128)(2,1)}), bf16[32,2,16,768]{3,2,1,0:T(8,128)(2,1)}, u32[]{:S(2)}, u32[]{:S(2)}) async-start(bf16[32,2,16,768]{3,2,1,0:T(8,128)(2,1)} %fusion.2), calls=%async_computation | async-start | bytes 3145728 | tf_op jit(solution)/shard_map/all_to_all | solution.py:562
  131.1 41.3 %all-to-all-start.2 = ((bf16[32,16,768]{2,1,0:T(8,128)(2,1)}), bf16[32,16,768]{2,1,0:T(8,128)(2,1)}, u32[]{:S(2)}, u32[]{:S(2)}) async-start(bf16[32,16,768]{2,1,0:T(8,128)(2,1)} %bitcast.157), calls=%async_computation.2 | async-start | bytes 1572864 | tf_op jit(solution)/shard_map/all_to_all | solution.py:562
  142.0 19.4 %collective-permute-start.7 = (bf16[2,8,16,768]{3,2,1,0:T(8,128)(2,1)S(1)}, bf16[2,8,16,768]{3,2,1,0:T(8,128)(2,1)S(1)}, u32[]{:S(2)}, u32[]{:S(2)}) collective-permute-start(bf16[2,8,16,768]{3,2,1,0:T(8,128)(2,1)S(1)} %get-tuple-element.180), channel_id=1, source_target_pairs={{0,8},{1,9},{2,10},{3,11},{4,12},{5,13},{6,14},{7,15},{8,0},{9,1},... | collective-permute-start | bytes 1179656 | tf_op jit(solution)/shard_map/ppermute | solution.py:567
  145.3 22.3 %collective-permute-start.9 = (bf16[2,8,16,768]{3,2,1,0:T(8,128)(2,1)S(1)}, bf16[2,8,16,768]{3,2,1,0:T(8,128)(2,1)S(1)}, u32[]{:S(2)}, u32[]{:S(2)}) collective-permute-start(bf16[2,8,16,768]{3,2,1,0:T(8,128)(2,1)S(1)} %get-tuple-element.182), channel_id=1, source_target_pairs={{0,24},{1,25},{2,26},{3,27},{4,28},{5,29},{6,30},{7,31},{8,16},{9,... | collective-permute-start | bytes 1179656 | tf_op jit(solution)/shard_map/ppermute | solution.py:567
  172.4 45.4 %all-to-all-start.1 = ((bf16[32,16,768]{2,1,0:T(8,128)(2,1)}), bf16[32,16,768]{2,1,0:T(8,128)(2,1)S(1)}, u32[]{:S(2)}, u32[]{:S(2)}) async-start(bf16[32,16,768]{2,1,0:T(8,128)(2,1)} %bitcast.29), calls=%async_computation.1 | async-start | bytes 1572864 | tf_op jit(solution)/shard_map/all_to_all | solution.py:562
  179.1 40.8 %collective-permute-start.13 = (bf16[8,16,768]{2,1,0:T(8,128)(2,1)S(1)}, bf16[8,16,768]{2,1,0:T(8,128)(2,1)}, u32[]{:S(2)}, u32[]{:S(2)}) collective-permute-start(bf16[8,16,768]{2,1,0:T(8,128)(2,1)S(1)} %get-tuple-element.193), channel_id=1, source_target_pairs={{0,8},{1,9},{2,10},{3,11},{4,12},{5,13},{6,14},{7,15},{8,0},{9,1},... | collective-permute-start | bytes 589832 | tf_op jit(solution)/shard_map/ppermute | solution.py:567
  180.8 41.4 %collective-permute-start.14 = (bf16[8,16,768]{2,1,0:T(8,128)(2,1)S(1)}, bf16[8,16,768]{2,1,0:T(8,128)(2,1)}, u32[]{:S(2)}, u32[]{:S(2)}) collective-permute-start(bf16[8,16,768]{2,1,0:T(8,128)(2,1)S(1)} %get-tuple-element.194), channel_id=1, source_target_pairs={{0,16},{1,17},{2,18},{3,19},{4,20},{5,21},{6,22},{7,23},{8,24},{9,... | collective-permute-start | bytes 589832 | tf_op jit(solution)/shard_map/ppermute | solution.py:567
  182.3 39.9 %collective-permute-start.15 = (bf16[8,16,768]{2,1,0:T(8,128)(2,1)S(1)}, bf16[8,16,768]{2,1,0:T(8,128)(2,1)}, u32[]{:S(2)}, u32[]{:S(2)}) collective-permute-start(bf16[8,16,768]{2,1,0:T(8,128)(2,1)S(1)} %get-tuple-element.195), channel_id=1, source_target_pairs={{0,24},{1,25},{2,26},{3,27},{4,28},{5,29},{6,30},{7,31},{8,16},{9,... | collective-permute-start | bytes 589832 | tf_op jit(solution)/shard_map/ppermute | solution.py:567
  263.3 24.6 %all-to-all-start.3 = ((bf16[32,16,768]{2,1,0:T(8,128)(2,1)}), bf16[32,16,768]{2,1,0:T(8,128)(2,1)S(1)}, u32[]{:S(2)}, u32[]{:S(2)}) async-start(bf16[32,16,768]{2,1,0:T(8,128)(2,1)} %put.3), calls=%async_computation.3 | async-start | bytes 1572864 | tf_op jit(solution)/shard_map/all_to_all | solution.py:562
  265.9 190.9 %reduce-scatter.5.cloned.1.call-start = ((), (), s32[]{:S(2)}) async-start(), calls=%async_computation.12 | async-start | bytes 3538944 | tf_op jit(solution)/shard_map/reduce_scatter | solution.py:897
  298.1 158.8 %reduce-scatter.3.cloned.1.call-start = ((), (), s32[]{:S(2)}) async-start(), calls=%async_computation.11 | async-start | bytes 7077888 | tf_op jit(solution)/shard_map/reduce_scatter | solution.py:896
  319.0 35.1 %all-to-all-start.4 = ((bf16[32,16,768]{2,1,0:T(8,128)(2,1)}), bf16[32,16,768]{2,1,0:T(8,128)(2,1)}, u32[]{:S(2)}, u32[]{:S(2)}) async-start(bf16[32,16,768]{2,1,0:T(8,128)(2,1)} %put.4), calls=%async_computation.4 | async-start | bytes 1572864 | tf_op jit(solution)/shard_map/all_to_all | solution.py:562
  322.4 31.8 %collective-permute-start.22 = (bf16[2,8,16,768]{3,2,1,0:T(8,128)(2,1)}, bf16[2,8,16,768]{3,2,1,0:T(8,128)(2,1)}, u32[]{:S(2)}, u32[]{:S(2)}) collective-permute-start(bf16[2,8,16,768]{3,2,1,0:T(8,128)(2,1)} %bitcast.54), channel_id=1, source_target_pairs={{0,8},{1,9},{2,10},{3,11},{4,12},{5,13},{6,14},{7,15},{8,0},{9,1},... | collective-permute-start | bytes 1179656 | tf_op jit(solution)/shard_map/ppermute | solution.py:567
  324.0 30.1 %collective-permute-start.23 = (bf16[2,8,16,768]{3,2,1,0:T(8,128)(2,1)}, bf16[2,8,16,768]{3,2,1,0:T(8,128)(2,1)}, u32[]{:S(2)}, u32[]{:S(2)}) collective-permute-start(bf16[2,8,16,768]{3,2,1,0:T(8,128)(2,1)} %bitcast.55), channel_id=1, source_target_pairs={{0,16},{1,17},{2,18},{3,19},{4,20},{5,21},{6,22},{7,23},{8,24},{9,... | collective-permute-start | bytes 1179656 | tf_op jit(solution)/shard_map/ppermute | solution.py:567
  325.5 28.6 %collective-permute-start.24 = (bf16[2,8,16,768]{3,2,1,0:T(8,128)(2,1)}, bf16[2,8,16,768]{3,2,1,0:T(8,128)(2,1)}, u32[]{:S(2)}, u32[]{:S(2)}) collective-permute-start(bf16[2,8,16,768]{3,2,1,0:T(8,128)(2,1)} %bitcast.56), channel_id=1, source_target_pairs={{0,24},{1,25},{2,26},{3,27},{4,28},{5,29},{6,30},{7,31},{8,16},{9,... | collective-permute-start | bytes 1179656 | tf_op jit(solution)/shard_map/ppermute | solution.py:567
  396.9 59.9 %all-to-all-start.5 = ((bf16[32,2,16,768]{3,2,1,0:T(8,128)(2,1)}), bf16[32,2,16,768]{3,2,1,0:T(8,128)(2,1)}, u32[]{:S(2)}, u32[]{:S(2)}) async-start(bf16[32,2,16,768]{3,2,1,0:T(8,128)(2,1)} %put.5), calls=%async_computation.5 | async-start | bytes 3145728 | tf_op jit(solution)/shard_map/all_to_all | solution.py:562
  406.8 38.8 %collective-permute-start.26 = (bf16[4,24,3840]{2,1,0:T(8,128)(2,1)S(1)}, bf16[4,24,3840]{2,1,0:T(8,128)(2,1)S(1)}, u32[]{:S(2)}, u32[]{:S(2)}) collective-permute-start(bf16[4,24,3840]{2,1,0:T(8,128)(2,1)S(1)} %get-tuple-element.312), channel_id=1, source_target_pairs={{0,8},{1,9},{2,10},{3,11},{4,12},{5,13},{6,14},{7,15},{8,0},{9,1},... | collective-permute-start | bytes 2211848 | tf_op jit(solution)/shard_map/ppermute | solution.py:567
  408.7 36.9 %collective-permute-start.27 = (bf16[4,24,3840]{2,1,0:T(8,128)(2,1)S(1)}, bf16[4,24,3840]{2,1,0:T(8,128)(2,1)S(1)}, u32[]{:S(2)}, u32[]{:S(2)}) collective-permute-start(bf16[4,24,3840]{2,1,0:T(8,128)(2,1)S(1)} %get-tuple-element.314), channel_id=1, source_target_pairs={{0,16},{1,17},{2,18},{3,19},{4,20},{5,21},{6,22},{7,23},{8,24},{9,... | collective-permute-start | bytes 2211848 | tf_op jit(solution)/shard_map/ppermute | solution.py:567
  410.2 46.3 %collective-permute-start.28 = (bf16[4,24,3840]{2,1,0:T(8,128)(2,1)S(1)}, bf16[4,24,3840]{2,1,0:T(8,128)(2,1)S(1)}, u32[]{:S(2)}, u32[]{:S(2)}) collective-permute-start(bf16[4,24,3840]{2,1,0:T(8,128)(2,1)S(1)} %get-tuple-element.313), channel_id=1, source_target_pairs={{0,24},{1,25},{2,26},{3,27},{4,28},{5,29},{6,30},{7,31},{8,16},{9,... | collective-permute-start | bytes 2211848 | tf_op jit(solution)/shard_map/ppermute | solution.py:567
  (148 other events, 937.2 us)
Sparse Core Ops, SparseCore 0:
  11.6 92.8 all-gather.4
  106.2 36.6 all-gather.8
  145.1 83.1 all-gather.6
  298.2 45.4 reduce-scatter.4
  345.8 88.6 reduce-scatter.2

commit v7 on v6

--- a/solution.py
+++ b/solution.py
@@ -978,12 +978,11 @@
     do1, cross_pair = lax.optimization_barrier((do1, cross_pair))
     cross_plane = scatter_plane(cross_pair)
     grads = back_self(do1)
-    grads, cross_plane, y_home, sum_wgu, sum_wd = lax.optimization_barrier(
-        (grads, cross_plane, y_home, sum_wgu, sum_wd)
-    )
+    grads, y_home, sum_wgu, sum_wd = lax.optimization_barrier((grads, y_home, sum_wgu, sum_wd))
+    own_pair = scatter_pairs([tn(h1, d).astype(BF) for d in grads])
+    own_pair, cross_plane = lax.optimization_barrier((own_pair, cross_plane))
+    own_plane = scatter_plane(own_pair)
     cross_sum = scatter_column(cross_plane)
-    own_pair = scatter_pairs([tn(h1, d).astype(BF) for d in grads])
-    own_plane = scatter_plane(own_pair)
     grads, dck, dcv = tied((grads, dck, dcv), own_pair)
     y_home = tied(y_home, own_plane)
     grad_tokens, dgain_self = by_tokens(

time: 531 us -> 532 us (level)
  starting transfers between devices: 83.3 us -> 76.5 us
    all_to_all x7, waiting for transfers between devices: 43.2 us -> 54.4 us  [to_all(): return lax.all_to_all(value, ALL, 0, 0, tiled=True)]
    ppermute x39, waiting for transfers between devices: 80.9 us -> 70.5 us  [swap(): return lax.ppermute(value, ALL, [(i, i ^ j) for i in range(count)])]
    unnamed x249 -> x243, local copies, waits for them, and re-layouts: 57.4 us -> 59.1 us
  transfers between devices with their start and end apart: 51 -> 51, of which waited for: 18 -> 19; matrix products, arithmetic and copies ran while one was open for 7% -> 8% of each run, Pallas kernels for 34% -> 35%
where the time goes in v7:
time: 532 us; the launch traced here: 522 us
  Pallas kernels  206 us (39%)
  waiting for transfers between devices  126 us (24%)
  starting transfers between devices  76.5 us (14%)
  local copies, waits for them, and re-layouts  66.6 us (13%)
  other arithmetic  21.1 us (4%)
  between operations  15.4 us (3%)
  matrix products  11.7 us (2%)
    ppermute x39, waiting for transfers between devices, swap(): return lax.ppermute(value, ALL, [(i, i ^ j) for i in range(count)])  70.5 us
    pallas_call x3, Pallas kernels, attend_backward(): pl.pallas_call(functools.partial(attend_bwd_kernel, causal, start, had),...  59.9 us
    unnamed x243, local copies, waits for them, and re-layouts  59.1 us
    all_to_all x7, waiting for transfers between devices, to_all(): return lax.all_to_all(value, ALL, 0, 0, tiled=True)  54.4 us
    ppermute x39, starting transfers between devices, swap(): return lax.ppermute(value, ALL, [(i, i ^ j) for i in range(count)])  46.4 us
    pallas_call x3, Pallas kernels, attend_forward(): pl.pallas_call(functools.partial(attend_fwd_kernel, causal), grid_spec=pl...  36.9 us
    pallas_call x2, Pallas kernels, feed(): pl.pallas_call(functools.partial(feed_kernel, groups), grid=(ff // FS,),...  32.6 us
    pallas_call x11, Pallas kernels, by_tokens(): pl.pallas_call(run, grid=(steps,), in_specs=[rows(a.shape[1], first) for...  31.4 us
  transfers between devices with their start and end apart: 51, of which 19 were waited for; matrix products, arithmetic and copies ran while one was open for 8% of the time, Pallas kernels for 35%

profile of v7, /device:TPU:0, one launch (start us, length us, event | category | flops | bytes accessed | tf_op | source)
XLA Modules:
  0.0 522.4 jit_solution(6299659605853097023)
XLA Ops:
  15.0 5.1 collective-permute-start.2
  27.6 5.1 collective-permute-done.1
  42.8 8.8 %collective-permute-done.3 = bf16[4,24,2432]{2,1,0:T(8,128)(2,1)S(1)} collective-permute-done((bf16[4,24,2432]{2,1,0:T(8,128)(2,1)}, bf16[4,24,2432]{2,1,0:T(8,128)(2,1)S(1)}, u32[]{:S(2)}, u32[]{:S(2)}) %collective-permute-start.3) | collective-permute-done | bytes 466976 | tf_op jit(solution)/shard_map/ppermute | solution.py:567
  51.6 10.4 %collective-permute-done.4 = bf16[4,24,2432]{2,1,0:T(8,128)(2,1)S(1)} collective-permute-done((bf16[4,24,2432]{2,1,0:T(8,128)(2,1)}, bf16[4,24,2432]{2,1,0:T(8,128)(2,1)S(1)}, u32[]{:S(2)}, u32[]{:S(2)}) %collective-permute-start.4) | collective-permute-done | bytes 466976 | tf_op jit(solution)/shard_map/ppermute | solution.py:567
  62.0 8.0 %collective-permute-done.5 = bf16[4,24,2432]{2,1,0:T(8,128)(2,1)S(1)} collective-permute-done((bf16[4,24,2432]{2,1,0:T(8,128)(2,1)}, bf16[4,24,2432]{2,1,0:T(8,128)(2,1)S(1)}, u32[]{:S(2)}, u32[]{:S(2)}) %collective-permute-start.5) | collective-permute-done | bytes 466976 | tf_op jit(solution)/shard_map/ppermute | solution.py:567
  76.4 5.3 %enter.1 = (bf16[1024,768]{1,0:T(8,128)(2,1)S(1)}, bf16[1024,2304]{1,0:T(8,128)(2,1)S(1)}, f32[8,768]{1,0:T(8,128)S(1)}) custom-call(bf16[1024,768]{1,0:T(8,128)(2,1)S(1)} %bitcast.134, bf16[768,1152]{1,0:T(8,128)(2,1)S(1)} %bitcast.126, bf16[768,1152]{1,0:T(8,128)(2,1)S(1)} %bitcast.130, bf16[768,128]{1,0:T(8,128)(2,1)S(1)} %bitcast.163), custom_call_target="tpu_custom_call" | custom-call | flops 1000000 | bytes 10000 | tf_op jit(solution)/shard_map/enter/pallas_call | solution.py:329
  83.4 21.1 %attend_causal.1 = (bf16[1024,768]{1,0:T(8,128)(2,1)S(1)}, f32[6,2,1024]{2,1,0:T(2,128)S(1)}) custom-call(s32[2]{0:T(128)S(1)} %get-tuple-element.310.lens, bf16[1024,2304]{1,0:T(8,128)(2,1)S(1)} %get-tuple-element.167.q_ref.k_ref.v_ref.refs_0_.refs_1_.refs_2_, bf16[1024,2304]{1,0:T(8,128)(2,1)S(1)} %get-tuple-element.167.q_ref.k_ref.v_ref.refs_0_.refs_1_.refs_2_, ...), custom_call_target="tpu_custom_call" | custom-call | flops 1000000 | bytes 10000 | tf_op jit(solution)/shard_map/attend_causal/pallas_call | solution.py:165
  118.9 7.9 %attend_memory.2 = (bf16[512,768]{1,0:T(8,128)(2,1)S(1)}, f32[6,2,512]{2,1,0:T(2,128)S(1)}) custom-call(s32[2]{0:T(128)S(1)} %get-tuple-element.310.lens, bf16[512,768]{1,0:T(8,128)(2,1)S(1)} %get-tuple-element.172.q_ref.refs_0_, bf16[512,1536]{1,0:T(8,128)(2,1)S(1)} %memory.1.k_ref.v_ref.refs_1_.refs_2_, bf16[512,1536]{1,0:T(8,128)(2,1)S(1)} %memory.1.k_ref.v_ref.refs_1_.refs_2_), custom_call_target="tpu_custom_call" | custom-call | flops 1000000 | bytes 10000 | tf_op jit(solution)/shard_map/attend_memory/pallas_call | solution.py:165
  131.6 6.9 %all-to-all-start.2 = ((bf16[32,16,768]{2,1,0:T(8,128)(2,1)}), bf16[32,16,768]{2,1,0:T(8,128)(2,1)}, u32[]{:S(2)}, u32[]{:S(2)}) async-start(bf16[32,16,768]{2,1,0:T(8,128)(2,1)} %bitcast.157), calls=%async_computation.2 | async-start | bytes 1572864 | tf_op jit(solution)/shard_map/all_to_all | solution.py:562
  152.6 7.9 %attend_memory.3 = (bf16[512,768]{1,0:T(8,128)(2,1)S(1)}, f32[6,2,512]{2,1,0:T(2,128)S(1)}) custom-call(s32[2]{0:T(128)S(1)} %get-tuple-element.309.lens, bf16[512,768]{1,0:T(8,128)(2,1)S(1)} %get-tuple-element.178.q_ref.refs_0_, bf16[512,1536]{1,0:T(8,128)(2,1)S(1)} %memory.1.k_ref.v_ref.refs_1_.refs_2_, bf16[512,1536]{1,0:T(8,128)(2,1)S(1)} %memory.1.k_ref.v_ref.refs_1_.refs_2_), custom_call_target="tpu_custom_call" | custom-call | flops 1000000 | bytes 10000 | tf_op jit(solution)/shard_map/attend_memory/pallas_call | solution.py:165
  161.2 4.9 collective-permute-done.8
  182.3 35.6 %all-to-all-done.1.x_ref = bf16[32,16,768]{2,1,0:T(8,128)(2,1)} async-done(((bf16[32,16,768]{2,1,0:T(8,128)(2,1)}), bf16[32,16,768]{2,1,0:T(8,128)(2,1)}, u32[]{:S(2)}, u32[]{:S(2)}) %all-to-all-start.1) | async-done | bytes 786464 | tf_op jit(solution)/shard_map/all_to_all | solution.py:562
  231.6 16.3 %feed.2 = (bf16[2,128,768]{2,1,0:T(8,128)(2,1)}, bf16[2,128,768]{2,1,0:T(8,128)(2,1)}, bf16[2,128,768]{2,1,0:T(8,128)(2,1)}, bf16[2,128,768]{2,1,0:T(8,128)(2,1)...) custom-call(bf16[128,768]{1,0:T(8,128)(2,1)} %bitcast.162, ...), custom_call_target="tpu_custom_call" | custom-call | flops 1000000 | bytes 10000 | tf_op jit(solution)/shard_map/feed/pallas_call | solution.py:437
  251.5 4.6 collective-permute-done.16.refs_1_
  264.2 16.3 %feed.3 = (bf16[2,128,768]{2,1,0:T(8,128)(2,1)}, bf16[2,128,768]{2,1,0:T(8,128)(2,1)}, bf16[2,128,768]{2,1,0:T(8,128)(2,1)}, bf16[2,128,768]{2,1,0:T(8,128)(2,1)...) custom-call(bf16[128,768]{1,0:T(8,128)(2,1)} %bitcast.159, ...), custom_call_target="tpu_custom_call", output_to_operand_aliasing={{0}: (10, {}), {1}: (11, {}), {2}: (12, {}), {3}: (13, {}),... | custom-call | flops 1000000 | bytes 10000 | tf_op jit(solution)/shard_map/feed/pallas_call | solution.py:437
  280.5 5.7 %all-to-all-done.3 = bf16[32,16,768]{2,1,0:T(8,128)(2,1)S(1)} async-done(((bf16[32,16,768]{2,1,0:T(8,128)(2,1)}), bf16[32,16,768]{2,1,0:T(8,128)(2,1)S(1)}, u32[]{:S(2)}, u32[]{:S(2)}) %all-to-all-start.3) | async-done | bytes 786464 | tf_op jit(solution)/shard_map/all_to_all | solution.py:562
  300.8 10.6 %weight_grad.7 = bf16[768,4096]{1,0:T(8,128)(2,1)S(1)} custom-call(bf16[1024,768]{1,0:T(8,128)(2,1)S(1)} %copy-done.38, bf16[1024,4096]{1,0:T(8,128)(2,1)} %get-tuple-element.222.refs_1_), custom_call_target="tpu_custom_call" | custom-call | flops 1000000 | bytes 10000 | tf_op jit(solution)/shard_map/weight_grad/pallas_call | solution.py:363
  330.0 14.1 %attend_memory_back.2 = (bf16[512,768]{1,0:T(8,128)(2,1)S(1)}, f32[512,768]{1,0:T(8,128)S(1)}, f32[512,768]{1,0:T(8,128)}) custom-call(s32[2]{0:T(128)S(1)} %get-tuple-element.310.lens, bf16[512,768]{1,0:T(8,128)(2,1)S(1)} %copy-done.61, bf16[512,1536]{1,0:T(8,128)(2,1)} %copy-done.1, bf16[512,1536]{1,0:T(8,128)(2,1)} %copy-done.1, ...), custom_call_target="tpu_custom_call" | custom-call | flops 1000000 | bytes 10000 | tf_op jit(solution)/shard_map/attend_memory_back/pallas_call | solution.py:196
  360.2 14.0 %attend_memory_back.3 = (bf16[512,768]{1,0:T(8,128)(2,1)S(1)}, bf16[512,768]{1,0:T(8,128)(2,1)S(1)}, bf16[512,768]{1,0:T(8,128)(2,1)S(1)}) custom-call(s32[2]{0:T(128)S(1)} %get-tuple-element.309.lens, bf16[512,768]{1,0:T(8,128)(2,1)S(1)} %copy-done.57, bf16[512,1536]{1,0:T(8,128)(2,1)} %copy-done.1, bf16[512,1536]{1,0:T(8,128)(2,1)} %copy-done.1, ...), custom_call_target="tpu_custom_call" | custom-call | flops 1000000 | bytes 10000 | tf_op jit(solution)/shard_map/attend_memory_back/pallas_call | solution.py:196
  394.8 5.6 %all-to-all-start.5 = ((bf16[32,2,16,768]{3,2,1,0:T(8,128)(2,1)}), bf16[32,2,16,768]{3,2,1,0:T(8,128)(2,1)}, u32[]{:S(2)}, u32[]{:S(2)}) async-start(bf16[32,2,16,768]{3,2,1,0:T(8,128)(2,1)} %put.5), calls=%async_computation.5 | async-start | bytes 3145728 | tf_op jit(solution)/shard_map/all_to_all | solution.py:562
  409.7 31.7 %attend_causal_back.1 = (bf16[1024,768]{1,0:T(8,128)(2,1)S(1)}, bf16[1024,768]{1,0:T(8,128)(2,1)S(1)}, bf16[1024,768]{1,0:T(8,128)(2,1)S(1)}) custom-call(s32[2]{0:T(128)S(1)} %get-tuple-element.310.lens, bf16[1024,2304]{1,0:T(8,128)(2,1)} %copy-done, bf16[1024,2304]{1,0:T(8,128)(2,1)} %copy-done, bf16[1024,2304]{1,0:T(8,128)(2,1)} %copy-done, ...), custom_call_target="tpu_custom_call" | custom-call | flops 1000000 | bytes 10000 | tf_op jit(solution)/shard_map/attend_causal_back/pallas_call | solution.py:196
  443.8 11.0 %all-to-all-done.5 = bf16[32,2,16,768]{3,2,1,0:T(8,128)(2,1)} async-done(((bf16[32,2,16,768]{3,2,1,0:T(8,128)(2,1)}), bf16[32,2,16,768]{3,2,1,0:T(8,128)(2,1)}, u32[]{:S(2)}, u32[]{:S(2)}) %all-to-all-start.5) | async-done | bytes 1572896 | tf_op jit(solution)/shard_map/all_to_all | solution.py:562
  479.1 7.6 %enter_back.1 = (bf16[1024,768]{1,0:T(8,128)(2,1)}, f32[8,768]{1,0:T(8,128)S(1)}) custom-call(bf16[1024,768]{1,0:T(8,128)(2,1)S(1)} %bitcast.137, f32[1024,768]{1,0:T(8,128)S(1)} %copy-done.29, bf16[1024,768]{1,0:T(8,128)(2,1)S(1)} %get-tuple-element.293.refs_2_, bf16[1024,768]{1,0:T(8,128)(2,1)S(1)} %copy-done.70, bf16[1024,768]{1,0:T(8,128)(2,1)S(1)} %copy-done.72, ...), custom_call_target="tpu_custom_call" | custom-call | flops 1000000 | bytes 10000 | tf_op jit(solution)/shard_map/enter_back/pallas_call | solution.py:329
  490.0 8.8 %collective-permute-done.32 = bf16[4,24,2304]{2,1,0:T(8,128)(2,1)S(1)} collective-permute-done((bf16[4,24,2304]{2,1,0:T(8,128)(2,1)S(1)}, bf16[4,24,2304]{2,1,0:T(8,128)(2,1)S(1)}, u32[]{:S(2)}, u32[]{:S(2)}) %collective-permute-start.32) | collective-permute-done | bytes 442400 | tf_op jit(solution)/shard_map/ppermute | solution.py:567
  (411 shorter events, 234.0 us)
Async XLA Ops:
  7.2 101.2 %all-gather.5.cloned.1.call-start = ((), (), s32[]{:S(2)}) async-start(), calls=%async_computation.9 | async-start | bytes 6082560 | tf_op jit(solution)/shard_map/all_gather | solution.py:781
  10.5 221.2 %all-gather.9.cloned.1.call-start = ((), (), s32[]{:S(2)}) async-start(), calls=%async_computation.13 | async-start | bytes 3538944 | tf_op jit(solution)/shard_map/all_gather | solution.py:811
  11.2 220.4 %all-gather.7.cloned.1.call-start = ((), (), s32[]{:S(2)}) async-start(), calls=%async_computation.10 | async-start | bytes 7077888 | tf_op jit(solution)/shard_map/all_gather | solution.py:803
  35.0 27.0 %collective-permute-start.4 = (bf16[4,24,2432]{2,1,0:T(8,128)(2,1)}, bf16[4,24,2432]{2,1,0:T(8,128)(2,1)S(1)}, u32[]{:S(2)}, u32[]{:S(2)}) collective-permute-start(bf16[4,24,2432]{2,1,0:T(8,128)(2,1)} %get-tuple-element.332), channel_id=1, source_target_pairs={{0,16},{1,17},{2,18},{3,19},{4,20},{5,21},{6,22},{7,23},{8,24},{9,... | collective-permute-start | bytes 1400840 | tf_op jit(solution)/shard_map/ppermute | solution.py:567
  36.6 33.4 %collective-permute-start.5 = (bf16[4,24,2432]{2,1,0:T(8,128)(2,1)}, bf16[4,24,2432]{2,1,0:T(8,128)(2,1)S(1)}, u32[]{:S(2)}, u32[]{:S(2)}) collective-permute-start(bf16[4,24,2432]{2,1,0:T(8,128)(2,1)} %get-tuple-element.332), channel_id=1, source_target_pairs={{0,24},{1,25},{2,26},{3,27},{4,28},{5,29},{6,30},{7,31},{8,16},{9,... | collective-permute-start | bytes 1400840 | tf_op jit(solution)/shard_map/ppermute | solution.py:567
  38.4 93.2 %all-to-all-start = ((bf16[32,2,16,768]{3,2,1,0:T(8,128)(2,1)}), bf16[32,2,16,768]{3,2,1,0:T(8,128)(2,1)}, u32[]{:S(2)}, u32[]{:S(2)}) async-start(bf16[32,2,16,768]{3,2,1,0:T(8,128)(2,1)} %fusion.2), calls=%async_computation | async-start | bytes 3145728 | tf_op jit(solution)/shard_map/all_to_all | solution.py:562
  131.6 39.8 %all-to-all-start.2 = ((bf16[32,16,768]{2,1,0:T(8,128)(2,1)}), bf16[32,16,768]{2,1,0:T(8,128)(2,1)}, u32[]{:S(2)}, u32[]{:S(2)}) async-start(bf16[32,16,768]{2,1,0:T(8,128)(2,1)} %bitcast.157), calls=%async_computation.2 | async-start | bytes 1572864 | tf_op jit(solution)/shard_map/all_to_all | solution.py:562
  143.7 22.3 %collective-permute-start.8 = (bf16[2,8,16,768]{3,2,1,0:T(8,128)(2,1)S(1)}, bf16[2,8,16,768]{3,2,1,0:T(8,128)(2,1)S(1)}, u32[]{:S(2)}, u32[]{:S(2)}) collective-permute-start(bf16[2,8,16,768]{3,2,1,0:T(8,128)(2,1)S(1)} %get-tuple-element.182), channel_id=1, source_target_pairs={{0,16},{1,17},{2,18},{3,19},{4,20},{5,21},{6,22},{7,23},{8,24},{9,... | collective-permute-start | bytes 1179656 | tf_op jit(solution)/shard_map/ppermute | solution.py:567
  145.2 22.5 %collective-permute-start.9 = (bf16[2,8,16,768]{3,2,1,0:T(8,128)(2,1)S(1)}, bf16[2,8,16,768]{3,2,1,0:T(8,128)(2,1)S(1)}, u32[]{:S(2)}, u32[]{:S(2)}) collective-permute-start(bf16[2,8,16,768]{3,2,1,0:T(8,128)(2,1)S(1)} %get-tuple-element.183), channel_id=1, source_target_pairs={{0,24},{1,25},{2,26},{3,27},{4,28},{5,29},{6,30},{7,31},{8,16},{9,... | collective-permute-start | bytes 1179656 | tf_op jit(solution)/shard_map/ppermute | solution.py:567
  171.4 46.4 %all-to-all-start.1 = ((bf16[32,16,768]{2,1,0:T(8,128)(2,1)}), bf16[32,16,768]{2,1,0:T(8,128)(2,1)}, u32[]{:S(2)}, u32[]{:S(2)}) async-start(bf16[32,16,768]{2,1,0:T(8,128)(2,1)} %bitcast.158), calls=%async_computation.1 | async-start | bytes 1572864 | tf_op jit(solution)/shard_map/all_to_all | solution.py:562
  178.8 42.8 %collective-permute-start.13 = (bf16[8,16,768]{2,1,0:T(8,128)(2,1)}, bf16[8,16,768]{2,1,0:T(8,128)(2,1)}, u32[]{:S(2)}, u32[]{:S(2)}) collective-permute-start(bf16[8,16,768]{2,1,0:T(8,128)(2,1)} %get-tuple-element.194), channel_id=1, source_target_pairs={{0,8},{1,9},{2,10},{3,11},{4,12},{5,13},{6,14},{7,15},{8,0},{9,1},... | collective-permute-start | bytes 589832 | tf_op jit(solution)/shard_map/ppermute | solution.py:567
  180.6 43.4 %collective-permute-start.14 = (bf16[8,16,768]{2,1,0:T(8,128)(2,1)}, bf16[8,16,768]{2,1,0:T(8,128)(2,1)}, u32[]{:S(2)}, u32[]{:S(2)}) collective-permute-start(bf16[8,16,768]{2,1,0:T(8,128)(2,1)} %get-tuple-element.195), channel_id=1, source_target_pairs={{0,16},{1,17},{2,18},{3,19},{4,20},{5,21},{6,22},{7,23},{8,24},{9,... | collective-permute-start | bytes 589832 | tf_op jit(solution)/shard_map/ppermute | solution.py:567
  182.1 41.9 %collective-permute-start.15 = (bf16[8,16,768]{2,1,0:T(8,128)(2,1)}, bf16[8,16,768]{2,1,0:T(8,128)(2,1)}, u32[]{:S(2)}, u32[]{:S(2)}) collective-permute-start(bf16[8,16,768]{2,1,0:T(8,128)(2,1)} %get-tuple-element.196), channel_id=1, source_target_pairs={{0,24},{1,25},{2,26},{3,27},{4,28},{5,29},{6,30},{7,31},{8,16},{9,... | collective-permute-start | bytes 589832 | tf_op jit(solution)/shard_map/ppermute | solution.py:567
  261.5 24.6 %all-to-all-start.3 = ((bf16[32,16,768]{2,1,0:T(8,128)(2,1)}), bf16[32,16,768]{2,1,0:T(8,128)(2,1)S(1)}, u32[]{:S(2)}, u32[]{:S(2)}) async-start(bf16[32,16,768]{2,1,0:T(8,128)(2,1)} %put.3), calls=%async_computation.3 | async-start | bytes 1572864 | tf_op jit(solution)/shard_map/all_to_all | solution.py:562
  264.2 190.6 %reduce-scatter.5.cloned.1.call-start = ((), (), s32[]{:S(2)}) async-start(), calls=%async_computation.12 | async-start | bytes 3538944 | tf_op jit(solution)/shard_map/reduce_scatter | solution.py:897
  296.8 157.9 %reduce-scatter.3.cloned.1.call-start = ((), (), s32[]{:S(2)}) async-start(), calls=%async_computation.11 | async-start | bytes 7077888 | tf_op jit(solution)/shard_map/reduce_scatter | solution.py:896
  317.7 35.1 %all-to-all-start.4 = ((bf16[32,16,768]{2,1,0:T(8,128)(2,1)}), bf16[32,16,768]{2,1,0:T(8,128)(2,1)}, u32[]{:S(2)}, u32[]{:S(2)}) async-start(bf16[32,16,768]{2,1,0:T(8,128)(2,1)} %put.4), calls=%async_computation.4 | async-start | bytes 1572864 | tf_op jit(solution)/shard_map/all_to_all | solution.py:562
  321.1 31.8 %collective-permute-start.22 = (bf16[2,8,16,768]{3,2,1,0:T(8,128)(2,1)}, bf16[2,8,16,768]{3,2,1,0:T(8,128)(2,1)}, u32[]{:S(2)}, u32[]{:S(2)}) collective-permute-start(bf16[2,8,16,768]{3,2,1,0:T(8,128)(2,1)} %bitcast.54), channel_id=1, source_target_pairs={{0,8},{1,9},{2,10},{3,11},{4,12},{5,13},{6,14},{7,15},{8,0},{9,1},... | collective-permute-start | bytes 1179656 | tf_op jit(solution)/shard_map/ppermute | solution.py:567
  322.7 30.1 %collective-permute-start.23 = (bf16[2,8,16,768]{3,2,1,0:T(8,128)(2,1)}, bf16[2,8,16,768]{3,2,1,0:T(8,128)(2,1)}, u32[]{:S(2)}, u32[]{:S(2)}) collective-permute-start(bf16[2,8,16,768]{3,2,1,0:T(8,128)(2,1)} %bitcast.55), channel_id=1, source_target_pairs={{0,16},{1,17},{2,18},{3,19},{4,20},{5,21},{6,22},{7,23},{8,24},{9,... | collective-permute-start | bytes 1179656 | tf_op jit(solution)/shard_map/ppermute | solution.py:567
  324.2 28.6 %collective-permute-start.24 = (bf16[2,8,16,768]{3,2,1,0:T(8,128)(2,1)}, bf16[2,8,16,768]{3,2,1,0:T(8,128)(2,1)}, u32[]{:S(2)}, u32[]{:S(2)}) collective-permute-start(bf16[2,8,16,768]{3,2,1,0:T(8,128)(2,1)} %bitcast.56), channel_id=1, source_target_pairs={{0,24},{1,25},{2,26},{3,27},{4,28},{5,29},{6,30},{7,31},{8,16},{9,... | collective-permute-start | bytes 1179656 | tf_op jit(solution)/shard_map/ppermute | solution.py:567
  394.8 60.0 %all-to-all-start.5 = ((bf16[32,2,16,768]{3,2,1,0:T(8,128)(2,1)}), bf16[32,2,16,768]{3,2,1,0:T(8,128)(2,1)}, u32[]{:S(2)}, u32[]{:S(2)}) async-start(bf16[32,2,16,768]{3,2,1,0:T(8,128)(2,1)} %put.5), calls=%async_computation.5 | async-start | bytes 3145728 | tf_op jit(solution)/shard_map/all_to_all | solution.py:562
  406.2 56.4 %collective-permute-start.27 = (bf16[4,24,3840]{2,1,0:T(8,128)(2,1)}, bf16[4,24,3840]{2,1,0:T(8,128)(2,1)S(1)}, u32[]{:S(2)}, u32[]{:S(2)}) collective-permute-start(bf16[4,24,3840]{2,1,0:T(8,128)(2,1)} %get-tuple-element.314), channel_id=1, source_target_pairs={{0,8},{1,9},{2,10},{3,11},{4,12},{5,13},{6,14},{7,15},{8,0},{9,1},... | collective-permute-start | bytes 2211848 | tf_op jit(solution)/shard_map/ppermute | solution.py:567
  408.0 54.6 %collective-permute-start.28 = (bf16[4,24,3840]{2,1,0:T(8,128)(2,1)}, bf16[4,24,3840]{2,1,0:T(8,128)(2,1)}, u32[]{:S(2)}, u32[]{:S(2)}) collective-permute-start(bf16[4,24,3840]{2,1,0:T(8,128)(2,1)} %get-tuple-element.316), channel_id=1, source_target_pairs={{0,16},{1,17},{2,18},{3,19},{4,20},{5,21},{6,22},{7,23},{8,24},{9,... | collective-permute-start | bytes 2211848 | tf_op jit(solution)/shard_map/ppermute | solution.py:567
  409.5 53.2 %collective-permute-start.29 = (bf16[4,24,3840]{2,1,0:T(8,128)(2,1)}, bf16[4,24,3840]{2,1,0:T(8,128)(2,1)}, u32[]{:S(2)}, u32[]{:S(2)}) collective-permute-start(bf16[4,24,3840]{2,1,0:T(8,128)(2,1)} %get-tuple-element.315), channel_id=1, source_target_pairs={{0,24},{1,25},{2,26},{3,27},{4,28},{5,29},{6,30},{7,31},{8,16},{9,... | collective-permute-start | bytes 2211848 | tf_op jit(solution)/shard_map/ppermute | solution.py:567
  (145 other events, 942.1 us)
Sparse Core Ops, SparseCore 0:
  11.6 92.8 all-gather.4
  106.2 36.6 all-gather.8
  145.1 82.9 all-gather.6
  296.9 45.4 reduce-scatter.4
  344.6 89.9 reduce-scatter.2
